TPU v7x, 128 devices: a whole 4x4x4 slice. The times are simulated.
128 devices in a mesh: aa: 8 (over y_lo, z), ba: 16 (over y_hi, x, core).
Axes of the slice: x: 4, y: 4 (y_hi: 2, y_lo: 2; y = y_hi * 2 + y_lo), z: 4, core: 2. Of those that a mesh axis runs over, the one named last changes fastest.
Arguments:
- atom_cond: float32 [24576, 128], P(('aa', 'ba')), may hold values from -6 to 6
- noisy_pos: float32 [3, 24576], P(None, ('aa', 'ba')), may hold values from -8 to 8
- noise_level: float32 [1], replicated, may hold values from 0.1 to 4
- atom_token: int32 [24576], P(('aa', 'ba')), may hold values from -1 to 2047, as said below
- token_cond: float32 [2048, 768], P('aa'), may hold values from -6 to 6
- pair: bfloat16 [2048, 2048, 128], P('aa', 'ba'), may hold values from -64 to 64
- pair_bias_weight: bfloat16 [16, 128], replicated, may hold values from -0.375 to 0.375
- gains: float32 [3, 768], replicated, may hold values from 0.25 to 1.75
- w_pos: float32 [3, 128], replicated, may hold values from -3.5 to 3.5
- w_atom_token: bfloat16 [128, 768], replicated, may hold values from -0.5 to 0.5
- w_query_gate: bfloat16 [768, 1536], replicated, may hold values from -0.21875 to 0.21875
- w_key_value: bfloat16 [768, 1536], replicated, may hold values from -0.21875 to 0.21875
- w_attn_out: bfloat16 [768, 768], replicated, may hold values from -0.21875 to 0.21875
- w_up: bfloat16 [768, 3072], replicated, may hold values from -0.21875 to 0.21875
- w_down: bfloat16 [1536, 768], replicated, may hold values from -0.15625 to 0.15625
- w_token_atom: bfloat16 [768, 128], replicated, may hold values from -0.21875 to 0.21875
- w_pos_out: bfloat16 [3, 128], replicated, may hold values from -0.5 to 0.5
Outputs:
- denoised: float32 [3, 24576], P(None, ('aa', 'ba'))
- token_out: float32 [2048, 768], P('aa')
Inputs may be any that keep to these rules, and one draw needn't show every extreme that they name: `atom_token`: atom slots come in 8 groups of 3072 consecutive slots; group r holds only atoms of tokens r * 256 to (r + 1) * 256 - 1, in nondecreasing token order, live slots first and -1 after them. Every token has 1 to 12 atoms, and some token of every group has exactly 12.
All inputs are finite; a program needn't handle non-finite values.
Results may differ from a plain program's by a relative error of at most 0.01.
Values may be sent and summed in bfloat16 or wider, within the bound.
No kernel may reach another device: no remote copies, remote signals or barrier semaphores. Data moves between devices by JAX's collectives and lax.ppermute only.
A program may use at most 128 MiB of HBM per device.

v0:
```python
import jax
import jax.numpy as jnp
from jax import lax
from jax.sharding import PartitionSpec as P

D = 768
HEADS = 16


def sent_to_all(shard, axis):
    size = lax.axis_size(axis)
    return lax.all_to_all(
        jnp.broadcast_to(shard[None], (size, *shard.shape)), axis, 0, 0, tiled=True
    )


def laid_out(pieces, dim):
    pieces = jnp.moveaxis(pieces, 0, dim)
    dims = pieces.shape
    return pieces.reshape(*dims[:dim], dims[dim] * dims[dim + 1], *dims[dim + 2 :])


def gather_directly(shard, axis, dim):
    pieces = sent_to_all(shard, axis)
    return laid_out(pieces, dim)


def broadcast(shard, axis, root):
    return lax.dynamic_index_in_dim(lax.all_gather(shard, axis), root, 0, keepdims=False)


def of_everyone(shard, axis):
    everything = sent_to_all(shard, axis)
    return jnp.max(everything, axis=0)


def padded_to(lines, size):
    spare = -lines.shape[0] % size
    if not spare:
        return lines
    return jnp.concatenate([lines, jnp.zeros((spare, *lines.shape[1:]), lines.dtype)])


def split_up(shard, dim, size):
    dims = shard.shape
    pieces = shard.reshape(*dims[:dim], size, dims[dim] // size, *dims[dim + 1 :])
    return jnp.moveaxis(pieces, dim, 0)


def summed_on_arrival(shard, axis, dim):
    pieces = split_up(shard, dim, lax.axis_size(axis))
    arrived = lax.all_to_all(pieces, axis, split_axis=0, concat_axis=0, tiled=True)
    return arrived.astype(jnp.float32).sum(axis=0)


def sum_by_parts(shard, axes):
    lines = shard.reshape(-1, shard.shape[-1])
    padded = padded_to(lines, lax.axis_size(axes))
    whole = gather_directly(summed_on_arrival(padded, axes, 0).astype(jnp.bfloat16), axes, 0)
    return lax.slice_in_dim(whole, 0, len(lines)).reshape(shard.shape).astype(jnp.float32)


def layer_norm(values, gain_row):
    mean_value = jnp.mean(values, axis=-1, keepdims=True)
    centered = values - mean_value
    variance = jnp.mean(centered * centered, axis=-1, keepdims=True)
    return centered * lax.rsqrt(variance + 1e-05) * gain_row


def widen(factor, head_dim):
    return jnp.repeat(factor.T, head_dim, axis=1)


def token_sums(local_ids, rounded_state, w_atom_token, tok_rows):
    selector = (local_ids[:, None] == jnp.arange(tok_rows, dtype=jnp.int32)[None, :]).astype(
        jnp.bfloat16
    )
    hidden_atom = jax.nn.relu(
        jnp.dot(rounded_state, w_atom_token, preferred_element_type=jnp.float32)
    ).astype(jnp.bfloat16)
    sums = lax.dot_general(
        selector, hidden_atom, (((0,), (0,)), ((), ())), preferred_element_type=jnp.float32
    )
    return (sums, jnp.sum(selector.astype(jnp.float32), axis=0))


def project_start(tokens_start, gains, w_query_gate):
    normed = layer_norm(tokens_start, gains[0]).astype(jnp.bfloat16)
    query_gate = jnp.dot(normed, w_query_gate, preferred_element_type=jnp.float32)
    width = query_gate.shape[1] // 2
    query_rows = query_gate[:, :width].astype(jnp.bfloat16)
    gate_value = jax.nn.sigmoid(query_gate[:, width:]).astype(jnp.bfloat16)
    return (normed, query_rows, gate_value)


def on_device(
    atom_cond,
    noisy_pos,
    noise_level,
    atom_token,
    token_cond,
    pair,
    pair_bias_weight,
    gains,
    w_pos,
    w_atom_token,
    w_query_gate,
    w_key_value,
    w_attn_out,
    w_up,
    w_down,
    w_token_atom,
    w_pos_out,
):
    tok_rows = token_cond.shape[0]
    block_cols = pair.shape[1]
    head_dim = D // HEADS
    row_index = lax.axis_index("aa")
    col_index = lax.axis_index("ba")
    noise_sigma = noise_level[0]
    inv_scale = 1.0 / jnp.sqrt(noise_sigma * noise_sigma + 1.0)
    scaled_pos = noisy_pos * inv_scale
    atom_state = atom_cond + scaled_pos[0][:, None] * w_pos[0]
    atom_state = atom_state + scaled_pos[1][:, None] * w_pos[1]
    atom_state = atom_state + scaled_pos[2][:, None] * w_pos[2]
    rounded_state = atom_state.astype(jnp.bfloat16)
    local_token = atom_token - row_index * tok_rows
    one_hot = (local_token[:, None] == jnp.arange(tok_rows, dtype=jnp.int32)[None, :]).astype(
        jnp.bfloat16
    )
    group_state, group_ids = (
        gather_directly(rounded_state, "ba", 0),
        gather_directly(atom_token, "ba", 0),
    )
    summed, counts = token_sums(
        group_ids - row_index * tok_rows, group_state, w_atom_token, tok_rows
    )
    tokens_start = token_cond + summed / counts[:, None]
    normed, query_rows, gate_value = project_start(tokens_start, gains, w_query_gate)
    offset_row = col_index * block_cols % tok_rows
    owner_row = col_index * block_cols // tok_rows
    slice_rows = lax.dynamic_slice_in_dim(normed, offset_row, block_cols, 0)
    kv_local = jnp.dot(slice_rows, w_key_value, preferred_element_type=jnp.float32).astype(
        jnp.bfloat16
    )
    key_value = broadcast(kv_local, "aa", owner_row)
    key_heads = key_value[:, :D].reshape(block_cols, HEADS, head_dim)
    value_heads = key_value[:, D:].reshape(block_cols, HEADS, head_dim)
    query_heads = query_rows.reshape(tok_rows, HEADS, head_dim)
    scores = jnp.einsum(
        "ihd,jhd->hij", query_heads, key_heads, preferred_element_type=jnp.float32
    ) * head_dim ** (-0.5) + jnp.einsum(
        "hc,ijc->hij", pair_bias_weight, pair, preferred_element_type=jnp.float32
    )
    block_max = jnp.max(scores, axis=2)
    weights = jnp.exp(scores - block_max[:, :, None])
    block_total = jnp.sum(weights, axis=2)
    partial_out = jnp.einsum(
        "hij,jhd->ihd",
        weights.astype(jnp.bfloat16),
        value_heads,
        preferred_element_type=jnp.float32,
    ).reshape(tok_rows, D)
    overall = of_everyone(block_max, "ba")
    factor = jnp.exp(block_max - overall)
    out_all, total_all = (
        sum_by_parts((partial_out * widen(factor, head_dim)).astype(jnp.bfloat16), "ba"),
        sum_by_parts((block_total * factor).astype(jnp.bfloat16), "ba"),
    )
    attended = out_all / widen(total_all, head_dim)
    mixed_heads = (attended * gate_value.astype(jnp.float32)).astype(jnp.bfloat16)
    tokens_mid = tokens_start + jnp.dot(mixed_heads, w_attn_out, preferred_element_type=jnp.float32)
    normed_mid = layer_norm(tokens_mid, gains[1]).astype(jnp.bfloat16)
    gate_up = jnp.dot(normed_mid, w_up, preferred_element_type=jnp.float32)
    hidden_units = w_down.shape[0]
    inner_units = (jax.nn.silu(gate_up[:, :hidden_units]) * gate_up[:, hidden_units:]).astype(
        jnp.bfloat16
    )
    token_out = tokens_mid + jnp.dot(inner_units, w_down, preferred_element_type=jnp.float32)
    normed_out = layer_norm(token_out, gains[2]).astype(jnp.bfloat16)
    token_atom = jnp.dot(normed_out, w_token_atom, preferred_element_type=jnp.float32).astype(
        jnp.bfloat16
    )
    picked = jnp.dot(one_hot, token_atom, preferred_element_type=jnp.float32)
    atom_final = atom_state + picked
    atom_normed = layer_norm(atom_final, 1.0).astype(jnp.bfloat16)
    update = lax.dot_general(
        w_pos_out, atom_normed, (((1,), (1,)), ((), ())), preferred_element_type=jnp.float32
    )
    denoised = noisy_pos * (inv_scale * inv_scale) + update * (noise_sigma * inv_scale)
    return (denoised, token_out)


def solution(mesh):
    in_specs = (
        P(("aa", "ba"), None),
        P(None, ("aa", "ba")),
        P(),
        P(("aa", "ba")),
        P("aa", None),
        P("aa", "ba", None),
        P(),
        P(),
        P(),
        P(),
        P(),
        P(),
        P(),
        P(),
        P(),
        P(),
        P(),
    )
    out_specs = (P(None, ("aa", "ba")), P("aa", None))
    return jax.shard_map(
        on_device, mesh=mesh, in_specs=in_specs, out_specs=out_specs, check_vma=False
    )
```

profile of v0, /device:TPU:1, one launch (start us, length us, event | category | flops | bytes accessed | tf_op | source)
XLA Modules:
  0.0 192.1 jit_solution(10403624520729084537)
XLA Ops:
  7.2 1.4 broadcast_in_dim.14
  8.6 8.4 %all-to-all-start = ((s32[16,1,192]{2,1,0:T(1,128)}), s32[16,1,192]{2,1,0:T(1,128)S(1)}, u32[]{:S(2)}, u32[]{:S(2)}) async-start(s32[16,1,192]{2,1,0:T(1,128)} %broadcast_in_dim.14), calls=%async_computation | async-start | bytes 32768 | tf_op jit(solution)/shard_map/all_to_all | solution.py:12
  17.8 0.7 broadcast_multiply_fusion
  18.5 0.8 slice_bitcast_fusion.2
  19.3 1.0 fusion.35
  20.4 4.0 %all-to-all-done = s32[16,1,192]{2,1,0:T(1,128)S(1)} async-done(((s32[16,1,192]{2,1,0:T(1,128)}), s32[16,1,192]{2,1,0:T(1,128)S(1)}, u32[]{:S(2)}, u32[]{:S(2)}) %all-to-all-start) | async-done | bytes 12320 | tf_op jit(solution)/shard_map/all_to_all | solution.py:12
  24.4 1.0 broadcast_in_dim.15
  25.4 3.8 %all-to-all-start.1 = ((bf16[16,192,128]{2,1,0:T(8,128)(2,1)}), bf16[16,192,128]{2,1,0:T(8,128)(2,1)S(1)}, u32[]{:S(2)}, u32[]{:S(2)}) async-start(bf16[16,192,128]{2,1,0:T(8,128)(2,1)} %broadcast_in_dim.15), calls=%async_computation.1 | async-start | bytes 1572864 | tf_op jit(solution)/shard_map/all_to_all | solution.py:12
  30.1 1.4 convert_reduce_fusion
  31.4 12.4 %all-to-all-done.1 = bf16[16,192,128]{2,1,0:T(8,128)(2,1)S(1)} async-done(((bf16[16,192,128]{2,1,0:T(8,128)(2,1)}), bf16[16,192,128]{2,1,0:T(8,128)(2,1)S(1)}, u32[]{:S(2)}, u32[]{:S(2)}) %all-to-all-start.1) | async-done | bytes 786464 | tf_op jit(solution)/shard_map/all_to_all | solution.py:12
  43.9 0.9 copy-done.4
  44.8 5.7 %fusion.48 = (f32[256]{0:T(256)S(1)}, f32[256,768]{1,0:T(8,128)S(1)}) fusion(f32[256,768]{1,0:T(8,128)} %param.21, f32[256]{0:T(256)S(1)} %convert_reduce_fusion, bf16[3072,128]{1,0:T(8,128)(2,1)} %bitcast.62, bf16[128,768]{1,0:T(8,128)(2,1)S(1)} %copy-done.28, s32[3072]{0:T(1024)S(1)} %sub.80), kind=kOutput, calls=%fused_computation.89 | convolution fusion | flops 1818033920 | bytes 2570240 | tf_op jit(solution)/shard_map/dot_general | solution.py:81
  50.9 2.9 %convolution_convert_fusion = bf16[128,1536]{1,0:T(8,128)(2,1)} fusion(bf16[768,1536]{1,0:T(8,128)(2,1)} %param.28, bf16[256,768]{1,0:T(8,128)(2,1)S(1)} %multiply_convert_fusion.2, s32[]{:T(128)S(6)} %select_n.19), kind=kOutput, calls=%fused_computation.5 | convolution fusion | flops 302186496 | bytes 2949124 | tf_op jit(solution)/shard_map/dot_general | solution.py:143
  53.9 7.0 %fusion.40 = f32[16,256,128]{2,0,1:T(8,128)} fusion(bf16[256,128,128]{2,1,0:T(8,128)(2,1)} %param.22, bf16[16,128]{1,0:T(8,128)(2,1)S(1)} %copy-done.10), kind=kOutput, calls=%fused_computation.65 | convolution fusion | flops 134217728 | bytes 10489856 | tf_op jit(solution)/shard_map/hc,ijc->hij/dot_general | solution.py:152
  60.9 2.9 %copy.47 = f32[16,256,128]{1,2,0:T(8,128)} copy(f32[16,256,128]{2,0,1:T(8,128)} %fusion.40) | data formatting | bytes 4194304 | tf_op jit(solution)/shard_map/hc,ijc->hij/dot_general | solution.py:152
  63.8 0.8 fusion.53
  64.6 1.2 copy-done.3
  66.0 27.5 %all-gather.3.cloned.1.call-done = bf16[1024,1536]{1,0:T(8,128)(2,1)} async-done(((bf16[128,1536]{1,0:T(8,128)(2,1)}), bf16[1024,1536]{1,0:T(8,128)(2,1)}) %all-gather.3.cloned.1.call-update) | async-done | bytes 3145744 | tf_op jit(solution)/shard_map/all_gather | solution.py:29
  93.5 1.0 dynamic-slice_bitcast_fusion
  94.7 3.5 %fusion.49 = (f32[16,256]{1,0:T(8,128)S(1)}, f32[16,256,128]{1,2,0:T(8,128)}) fusion(f32[16,256,128]{1,2,0:T(8,128)} %copy.47, bf16[256,16,48]{0,2,1:T(8,128)(2,1)S(1)} %bitcast.60, bf16[128,16,48]{0,2,1:T(8,128)(2,1)S(1)} %bitcast.61), kind=kOutput, calls=%fused_computation.90 | convolution fusion | flops 51900416 | bytes 4800512 | tf_op jit(solution)/shard_map/ihd,jhd->hij/dot_general | solution.py:150
  98.2 0.7 broadcast_in_dim.16
  98.9 9.7 %all-to-all-start.2 = ((f32[16,16,256]{2,1,0:T(8,128)}), f32[16,16,256]{2,1,0:T(8,128)S(1)}, u32[]{:S(2)}, u32[]{:S(2)}) async-start(f32[16,16,256]{2,1,0:T(8,128)} %broadcast_in_dim.16), calls=%async_computation.2 | async-start | bytes 524288 | tf_op jit(solution)/shard_map/all_to_all | solution.py:12
  108.8 1.9 fusion.2
  110.7 6.6 %all-to-all-done.2 = f32[16,16,256]{2,1,0:T(8,128)S(1)} async-done(((f32[16,16,256]{2,1,0:T(8,128)}), f32[16,16,256]{2,1,0:T(8,128)S(1)}, u32[]{:S(2)}, u32[]{:S(2)}) %all-to-all-start.2) | async-done | bytes 262176 | tf_op jit(solution)/shard_map/all_to_all | solution.py:12
  117.9 0.7 reduce.11
  119.2 4.1 %all-to-all-start.5 = ((bf16[16,2,128]{2,1,0:T(2,128)(2,1)}), bf16[16,2,128]{2,1,0:T(2,128)(2,1)S(1)}, u32[]{:S(2)}, u32[]{:S(2)}) async-start(bf16[16,2,128]{2,1,0:T(2,128)(2,1)} %reshape.153), calls=%async_computation.5 | async-start | bytes 16384 | tf_op jit(solution)/shard_map/all_to_all | solution.py:52
  123.3 2.8 %fusion.7 = bf16[256,16,48]{0,2,1:T(8,128)(2,1)} fusion(bf16[128,16,48]{0,2,1:T(8,128)(2,1)S(1)} %bitcast.63, f32[16,256,128]{1,2,0:T(8,128)} %get-tuple-element.18, f32[16,256]{1,0:T(8,128)S(1)} %get-tuple-element.17, f32[256,16]{0,1:T(8,128)S(1)} %get-tuple-element.7), kind=kOutput, calls=%fused_computation.17 | convolution fusion | flops 51773440 | bytes 2719744 | tf_op jit(solution)/shard_map/hij,jhd->ihd/dot_general | solution.py:158
  126.1 1.9 %copy.49 = bf16[256,16,48]{2,1,0:T(8,128)(2,1)S(1)} copy(bf16[256,16,48]{0,2,1:T(8,128)(2,1)} %fusion.7) | data formatting | bytes 786432 | tf_op jit(solution)/shard_map/convert_element_type | solution.py:167
  128.1 1.9 %convert_element_type.89 = bf16[16,16,768]{2,1,0:T(8,128)(2,1)} reshape(bf16[256,16,48]{2,1,0:T(8,128)(2,1)S(1)} %copy.49) | data formatting | bytes 786432 | tf_op jit(solution)/shard_map/convert_element_type | solution.py:167
  131.0 7.0 %all-to-all-start.3 = ((bf16[16,16,768]{2,1,0:T(8,128)(2,1)}), bf16[16,16,768]{2,1,0:T(8,128)(2,1)S(1)}, u32[]{:S(2)}, u32[]{:S(2)}) async-start(bf16[16,16,768]{2,1,0:T(8,128)(2,1)} %convert_element_type.89), calls=%async_computation.3 | async-start | bytes 786432 | tf_op jit(solution)/shard_map/all_to_all | solution.py:52
  137.9 0.7 reshape.154
  139.8 1.3 reduce.12
  141.1 1.3 reshape.155
  142.4 5.3 %all-to-all-done.3 = bf16[16,16,768]{2,1,0:T(8,128)(2,1)S(1)} async-done(((bf16[16,16,768]{2,1,0:T(8,128)(2,1)}), bf16[16,16,768]{2,1,0:T(8,128)(2,1)S(1)}, u32[]{:S(2)}, u32[]{:S(2)}) %all-to-all-start.3) | async-done | bytes 393248 | tf_op jit(solution)/shard_map/all_to_all | solution.py:52
  147.7 4.3 %all-to-all-start.6 = ((bf16[16,2,128]{2,1,0:T(2,128)(2,1)}), bf16[16,2,128]{2,1,0:T(2,128)(2,1)S(1)}, u32[]{:S(2)}, u32[]{:S(2)}) async-start(bf16[16,2,128]{2,1,0:T(2,128)(2,1)} %reshape.155), calls=%async_computation.6 | async-start | bytes 16384 | tf_op jit(solution)/shard_map/all_to_all | solution.py:12
  152.7 6.4 %all-to-all-done.6 = bf16[16,2,128]{2,1,0:T(2,128)(2,1)S(1)} async-done(((bf16[16,2,128]{2,1,0:T(2,128)(2,1)}), bf16[16,2,128]{2,1,0:T(2,128)(2,1)S(1)}, u32[]{:S(2)}, u32[]{:S(2)}) %all-to-all-start.6) | async-done | bytes 8224 | tf_op jit(solution)/shard_map/all_to_all | solution.py:12
  159.1 1.5 broadcast_in_dim.18
  160.6 3.9 %all-to-all-start.4 = ((bf16[16,16,768]{2,1,0:T(8,128)(2,1)}), bf16[16,16,768]{2,1,0:T(8,128)(2,1)S(1)}, u32[]{:S(2)}, u32[]{:S(2)}) async-start(bf16[16,16,768]{2,1,0:T(8,128)(2,1)} %broadcast_in_dim.18), calls=%async_computation.4 | async-start | bytes 786432 | tf_op jit(solution)/shard_map/all_to_all | solution.py:12
  164.4 1.3 broadcast_subtract_fusion
  165.7 0.7 reshape.156
  166.4 1.0 broadcast_in_dim.20
  167.4 2.3 %copy.51 = f32[256,768]{1,0:T(8,128)} copy(f32[256,768]{0,1:T(8,128)} %bitcast.59) | data formatting | bytes 1572864 | tf_op jit(solution)/shard_map/reshape | solution.py:71
  169.7 4.6 %all-to-all-done.4 = bf16[16,16,768]{2,1,0:T(8,128)(2,1)S(1)} async-done(((bf16[16,16,768]{2,1,0:T(8,128)(2,1)}), bf16[16,16,768]{2,1,0:T(8,128)(2,1)S(1)}, u32[]{:S(2)}, u32[]{:S(2)}) %all-to-all-start.4) | async-done | bytes 393248 | tf_op jit(solution)/shard_map/all_to_all | solution.py:12
  174.3 2.5 %fusion.50 = (f32[256]{0:T(256)S(1)}, f32[256,768]{1,0:T(8,128)S(1)}) fusion(f32[256,768]{1,0:T(8,128)S(1)} %copy-done.2, bf16[768,768]{1,0:T(8,128)(2,1)} %param.29, f32[256,768]{1,0:T(8,128)} %copy.51, bf16[256,768]{1,0:T(8,128)(2,1)S(1)} %bitcast.64, f32[256,1536]{1,0:T(8,128)} %copy-done.3), kind=kOutput, calls=%fused_computation.91 | convolution fusion | flops 304152320 | bytes 4719616 | tf_op jit(solution)/shard_map/dot_general | solution.py:172
  177.1 4.0 %fusion.21 = f32[256,3072]{1,0:T(8,128)S(1)} fusion(bf16[768,3072]{1,0:T(8,128)(2,1)} %param.30, f32[256,768]{1,0:T(8,128)S(1)} %get-tuple-element.20, f32[768]{0:T(1024)S(1)} %copy-done.19, f32[256]{0:T(256)S(1)} %add_rsqrt_fusion.2, f32[256]{0:T(256)S(1)} %broadcast_multiply_fusion.3), kind=kOutput, calls=%fused_computation.41 | convolution fusion | flops 1208745984 | bytes 8655872 | tf_op jit(solution)/shard_map/dot_general | solution.py:174
  181.2 1.1 fusion.51
  182.6 1.5 fusion.52
  184.4 0.8 fusion.11
  (91 shorter events, 6.5 us)
Async XLA Ops:
  7.2 56.7 %copy-start = (bf16[768,1536]{1,0:T(8,128)(2,1)S(1)}, bf16[768,1536]{1,0:T(8,128)(2,1)}, u32[]{:S(2)}) copy-start(bf16[768,1536]{1,0:T(8,128)(2,1)} %param.27) | copy-start | bytes 7077892
  7.2 22.1 %copy-start.9 = (f32[3,768]{1,0:T(4,128)S(1)}, f32[3,768]{1,0:T(4,128)}, u32[]{:S(2)}) copy-start(f32[3,768]{1,0:T(4,128)} %param.24) | copy-start | bytes 27652
  7.2 37.6 %copy-start.28 = (bf16[128,768]{1,0:T(8,128)(2,1)S(1)}, bf16[128,768]{1,0:T(8,128)(2,1)}, u32[]{:S(2)}) copy-start(bf16[128,768]{1,0:T(8,128)(2,1)} %param.26) | copy-start | bytes 589828
  8.6 15.7 %all-to-all-start = ((s32[16,1,192]{2,1,0:T(1,128)}), s32[16,1,192]{2,1,0:T(1,128)S(1)}, u32[]{:S(2)}, u32[]{:S(2)}) async-start(s32[16,1,192]{2,1,0:T(1,128)} %broadcast_in_dim.14), calls=%async_computation | async-start | bytes 32768 | tf_op jit(solution)/shard_map/all_to_all | solution.py:12
  18.5 6.9 %copy-start.13 = (f32[1,192]{1,0:T(1,128)}, f32[1,192]{1,0:T(1,128)S(1)}, u32[]{:S(2)}) copy-start(f32[1,192]{1,0:T(1,128)S(1)} %get-tuple-element.10) | copy-start | bytes 2308
  18.5 6.9 %copy-start.15 = (f32[1,192]{1,0:T(1,128)}, f32[1,192]{1,0:T(1,128)S(1)}, u32[]{:S(2)}) copy-start(f32[1,192]{1,0:T(1,128)S(1)} %get-tuple-element.11) | copy-start | bytes 2308
  18.5 10.8 %copy-start.11 = (f32[1,192]{1,0:T(1,128)}, f32[1,192]{1,0:T(1,128)S(1)}, u32[]{:S(2)}) copy-start(f32[1,192]{1,0:T(1,128)S(1)} %get-tuple-element.9) | copy-start | bytes 2308
  19.3 6.1 %copy-start.20 = (f32[128]{0:T(128)}, f32[128]{0:T(128)S(1)}, u32[]{:S(2)}) copy-start(f32[128]{0:T(128)S(1)} %get-tuple-element.12) | copy-start | bytes 1540
  19.3 6.1 %copy-start.22 = (f32[128]{0:T(128)}, f32[128]{0:T(128)S(1)}, u32[]{:S(2)}) copy-start(f32[128]{0:T(128)S(1)} %get-tuple-element.13) | copy-start | bytes 1540
  19.3 6.1 %copy-start.24 = (f32[128]{0:T(128)}, f32[128]{0:T(128)S(1)}, u32[]{:S(2)}) copy-start(f32[128]{0:T(128)S(1)} %get-tuple-element.14) | copy-start | bytes 1540
  25.4 18.4 %all-to-all-start.1 = ((bf16[16,192,128]{2,1,0:T(8,128)(2,1)}), bf16[16,192,128]{2,1,0:T(8,128)(2,1)S(1)}, u32[]{:S(2)}, u32[]{:S(2)}) async-start(bf16[16,192,128]{2,1,0:T(8,128)(2,1)} %broadcast_in_dim.15), calls=%async_computation.1 | async-start | bytes 1572864 | tf_op jit(solution)/shard_map/all_to_all | solution.py:12
  29.2 64.3 %all-gather.3.cloned.1.call-start = ((), (), s32[]{:S(2)}) async-start(), calls=%async_computation.7 | async-start | bytes 3538944 | tf_op jit(solution)/shard_map/all_gather | solution.py:29
  43.9 0.9 copy-start.4
  50.5 3.3 %copy-start.1 = (f32[256,768]{1,0:T(8,128)}, f32[256,768]{1,0:T(8,128)S(1)}, u32[]{:S(2)}) copy-start(f32[256,768]{1,0:T(8,128)S(1)} %get-tuple-element.16) | copy-start | bytes 2359300
  50.7 3.1 %copy-start.10 = (bf16[16,128]{1,0:T(8,128)(2,1)S(1)}, bf16[16,128]{1,0:T(8,128)(2,1)}, u32[]{:S(2)}) copy-start(bf16[16,128]{1,0:T(8,128)(2,1)} %param.23) | copy-start | bytes 12292
  64.6 1.2 copy-start.3
  98.9 18.4 %all-to-all-start.2 = ((f32[16,16,256]{2,1,0:T(8,128)}), f32[16,16,256]{2,1,0:T(8,128)S(1)}, u32[]{:S(2)}, u32[]{:S(2)}) async-start(f32[16,16,256]{2,1,0:T(8,128)} %broadcast_in_dim.16), calls=%async_computation.2 | async-start | bytes 524288 | tf_op jit(solution)/shard_map/all_to_all | solution.py:12
  119.2 11.1 %all-to-all-start.5 = ((bf16[16,2,128]{2,1,0:T(2,128)(2,1)}), bf16[16,2,128]{2,1,0:T(2,128)(2,1)S(1)}, u32[]{:S(2)}, u32[]{:S(2)}) async-start(bf16[16,2,128]{2,1,0:T(2,128)(2,1)} %reshape.153), calls=%async_computation.5 | async-start | bytes 16384 | tf_op jit(solution)/shard_map/all_to_all | solution.py:52
  130.0 44.3 %copy-start.2 = (f32[256,768]{1,0:T(8,128)S(1)}, f32[256,768]{1,0:T(8,128)}, u32[]{:S(2)}) copy-start(f32[256,768]{1,0:T(8,128)} %copy-done.1) | copy-start | bytes 2359300
  130.4 0.6 copy-start.8
  131.0 16.8 %all-to-all-start.3 = ((bf16[16,16,768]{2,1,0:T(8,128)(2,1)}), bf16[16,16,768]{2,1,0:T(8,128)(2,1)S(1)}, u32[]{:S(2)}, u32[]{:S(2)}) async-start(bf16[16,16,768]{2,1,0:T(8,128)(2,1)} %convert_element_type.89), calls=%async_computation.3 | async-start | bytes 786432 | tf_op jit(solution)/shard_map/all_to_all | solution.py:52
  147.7 11.4 %all-to-all-start.6 = ((bf16[16,2,128]{2,1,0:T(2,128)(2,1)}), bf16[16,2,128]{2,1,0:T(2,128)(2,1)S(1)}, u32[]{:S(2)}, u32[]{:S(2)}) async-start(bf16[16,2,128]{2,1,0:T(2,128)(2,1)} %reshape.155), calls=%async_computation.6 | async-start | bytes 16384 | tf_op jit(solution)/shard_map/all_to_all | solution.py:12
  159.1 5.4 %copy-start.7 = (bf16[16,2,128]{2,1,0:T(2,128)(2,1)}, bf16[16,2,128]{2,1,0:T(2,128)(2,1)S(1)}, u32[]{:S(2)}) copy-start(bf16[16,2,128]{2,1,0:T(2,128)(2,1)S(1)} %all-to-all-done.6) | copy-start | bytes 24580
  160.6 13.7 %all-to-all-start.4 = ((bf16[16,16,768]{2,1,0:T(8,128)(2,1)}), bf16[16,16,768]{2,1,0:T(8,128)(2,1)S(1)}, u32[]{:S(2)}, u32[]{:S(2)}) async-start(bf16[16,16,768]{2,1,0:T(8,128)(2,1)} %broadcast_in_dim.18), calls=%async_computation.4 | async-start | bytes 786432 | tf_op jit(solution)/shard_map/all_to_all | solution.py:12
  174.3 2.8 %copy-start.19 = (f32[768]{0:T(1024)S(1)}, f32[768]{0:T(1024)}, u32[]{:S(2)}) copy-start(f32[768]{0:T(1024)} %get-tuple-element.4) | copy-start | bytes 9220
  177.1 4.0 %copy-start.27 = (bf16[1536,768]{1,0:T(8,128)(2,1)S(1)}, bf16[1536,768]{1,0:T(8,128)(2,1)}, u32[]{:S(2)}) copy-start(bf16[1536,768]{1,0:T(8,128)(2,1)} %param.31) | copy-start | bytes 7077892
  181.1 1.5 copy-start.6
  181.1 1.5 copy-start.12
  181.1 1.5 copy-start.14
  181.1 1.5 copy-start.16
  181.1 1.5 copy-start.18
  181.1 1.5 copy-start.21
  181.1 1.5 copy-start.23
  181.1 1.5 copy-start.25
  181.2 1.5 copy-start.26
  181.2 3.2 %copy-start.17 = (f32[3,192]{1,0:T(4,128)S(1)}, f32[3,192]{1,0:T(4,128)}, u32[]{:S(2)}) copy-start(f32[3,192]{1,0:T(4,128)} %param.18) | copy-start | bytes 6916
  181.2 3.2 %copy-start.29 = (bf16[3,128]{1,0:T(4,128)(2,1)S(1)}, bf16[3,128]{1,0:T(4,128)(2,1)}, u32[]{:S(2)}) copy-start(bf16[3,128]{1,0:T(4,128)(2,1)} %param.33) | copy-start | bytes 2308
  182.3 3.0 %copy-start.5 = (f32[256,768]{1,0:T(8,128)}, f32[256,768]{1,0:T(8,128)S(1)}, u32[]{:S(2)}) copy-start(f32[256,768]{1,0:T(8,128)S(1)} %get-tuple-element.22) | copy-start | bytes 2359300
Sparse Core Ops, SparseCore 0:
  54.0 39.5 all-gather.2
where the time goes:
time: 193 us; the launch traced here: 192 us
  waiting for transfers between devices  67.2 us (35%)
  starting transfers between devices  41.2 us (21%)
  matrix products  32.6 us (17%)
  local copies, waits for them, and re-layouts  25.2 us (13%)
  between operations  15.2 us (8%)
  other arithmetic  10.7 us (6%)
    all_to_all x5, waiting for transfers between devices, sent_to_all(): lax.all_to_all(jnp.broadcast_to(shard[None], (size, *shard.shape)), axis,...  34.1 us
    all_to_all x5, starting transfers between devices, sent_to_all(): lax.all_to_all(jnp.broadcast_to(shard[None], (size, *shard.shape)), axis,...  30.1 us
    all_gather x1, waiting for transfers between devices, broadcast(): lax.all_gather(shard, axis)  27.5 us
    all_to_all x2, starting transfers between devices, summed_on_arrival(): lax.all_to_all(pieces, axis, split_axis=0, concat_axis=0, tiled=True)  11 us
    dot_general x1, matrix products, on_device(): jnp.einsum('hc,ijc->hij', pair_bias_weight, pair, preferred_element_type=...  7.05 us
    unnamed x65, local copies, waits for them, and re-layouts  6.13 us
    dot_general x1, matrix products, token_sums(): lax.dot_general(selector, hidden_atom, (((0,), (0,)), ((), ())), preferre...  5.71 us
    all_to_all x2, waiting for transfers between devices, summed_on_arrival(): lax.all_to_all(pieces, axis, split_axis=0, concat_axis=0, tiled=True)  5.6 us
  transfers between devices with their start and end apart: 8, of which 8 were waited for; matrix products, arithmetic and copies ran while one was open for 18% of the time, Pallas kernels for 0%

commit v1 on v0

v1 whole, which is shorter than its diff:
```python
import functools

import jax
import jax.numpy as jnp
from jax import lax
from jax.experimental import pallas as pl
from jax.experimental.pallas import tpu as pltpu
from jax.sharding import PartitionSpec as P

D = 768
HEADS = 16
HEAD_DIM = D // HEADS
BF = jnp.bfloat16
F32 = jnp.float32
WIDE = jnp.float16
MIB = 1 << 20


def dot(a, b, dims=((1,), (0,)), **kw):
    return lax.dot_general(a, b, (dims, ((), ())), preferred_element_type=F32, **kw)


def norm_rows(values, gain_row):
    mean_value = jnp.mean(values, axis=-1, keepdims=True)
    centered = values - mean_value
    variance = jnp.mean(centered * centered, axis=-1, keepdims=True)
    return centered * lax.rsqrt(variance + 1e-05) * gain_row


def whole(n):
    return [pl.BlockSpec(memory_space=pltpu.VMEM)] * n


def state_kernel(cond_ref, pos_ref, noise_ref, ids_ref, w_pos_ref, state_ref, packed_ref):
    atoms = cond_ref.shape[0]
    sigma = noise_ref[0]
    sigma = jnp.full((1, 128), sigma, F32)
    inv = 1.0 / jnp.sqrt(sigma * sigma + 1.0)
    pos = jnp.transpose(
        jnp.concatenate([pos_ref[...] * inv[:, :1], jnp.zeros((5, atoms), F32)], axis=0)
    )
    state = cond_ref[...] + pos[:, 0:1] * w_pos_ref[0:1, :]
    state = state + pos[:, 1:2] * w_pos_ref[1:2, :]
    state = state + pos[:, 2:3] * w_pos_ref[2:3, :]
    state_ref[...] = state
    ids = ids_ref[...].astype(F32)
    first = ids[:, :128]
    second = jnp.concatenate([ids[:, 128:], jnp.zeros((1, 256 - atoms), F32)], axis=1)
    tail = jnp.concatenate([first, second, jnp.zeros((14, 128), F32)], axis=0).astype(BF)
    rounded = state.astype(BF)
    for piece in range(packed_ref.shape[0]):
        packed_ref[piece, :atoms, :] = rounded
        packed_ref[piece, atoms:, :] = tail


def bias_kernel(pair_ref, w_ref, out_ref, held):
    rows, cols, chans = pair_ref.shape
    half = rows // 2
    both = jnp.concatenate(
        [
            pair_ref[:half].reshape(half * cols, chans),
            pair_ref[half:].reshape(half * cols, chans),
        ],
        axis=1,
    )
    bias = dot(w_ref[...], both, ((1,), (1,)))
    for i in range(half):
        held[pl.ds(i, HEADS, stride=rows), :] = bias[:HEADS, i * cols : (i + 1) * cols]
        held[pl.ds(half + i, HEADS, stride=rows), :] = bias[HEADS:, i * cols : (i + 1) * cols]
    out_ref[...] = held[...].reshape(HEADS, rows, cols).astype(out_ref.dtype)


def token_kernel(
    mine_ref, other_ref, w_atom_ref, cond_ref, gains_ref, w_head_ref,
    start_ref, query_ref, gate_ref, kv_ref,
):
    tok_rows = cond_ref.shape[0]
    atoms = mine_ref.shape[1] - 16
    tokens = lax.broadcasted_iota(jnp.int32, (tok_rows, atoms), 0).astype(F32)
    sums = jnp.zeros((tok_rows, D), F32)
    counts = jnp.zeros((tok_rows, atoms), F32)
    for ref in (mine_ref, other_ref):
        for piece in range(ref.shape[0]):
            hidden = jax.nn.relu(dot(ref[piece, :atoms, :], w_atom_ref[...])).astype(BF)
            tail = ref[piece, atoms:, :].astype(F32)
            ids = jnp.concatenate([tail[0:1, :], tail[1:2, : atoms - 128]], axis=1)
            chosen = jnp.where(ids == tokens, 1.0, 0.0)
            counts += chosen
            sums += dot(chosen.astype(BF), hidden)
    start = cond_ref[...] + sums / jnp.sum(counts, axis=1, keepdims=True)
    start_ref[...] = start
    normed = norm_rows(start, gains_ref[0:1, :]).astype(BF)
    projected = dot(normed, w_head_ref[...])
    query_ref[...] = projected[:, :HEAD_DIM].astype(BF)
    gate_ref[...] = jax.nn.sigmoid(projected[:, 128 : 128 + HEAD_DIM]).astype(BF)
    kv = jnp.transpose(projected[:, 256:512])
    kv = jnp.concatenate([kv[:HEAD_DIM], kv[128 : 128 + HEAD_DIM]], axis=0).astype(BF)
    for piece in range(kv_ref.shape[0]):
        kv_ref[piece] = kv


def attend_kernel(query_ref, gate_ref, kv_ref, bias_ref, mixed_ref):
    groups, _, keys = kv_ref.shape
    tok_rows = query_ref.shape[0]
    blocks, _, cols = bias_ref.shape
    step = 64
    parts = []
    for r in range(0, tok_rows, step):
        query = query_ref[r : r + step, :]
        scores = jnp.concatenate(
            [dot(query, kv_ref[g, :HEAD_DIM, :]) for g in range(groups)], axis=1
        ) * HEAD_DIM ** (-0.5)
        bias = jnp.concatenate(
            [bias_ref[b, r : r + step, :].astype(F32) for b in range(blocks)], axis=1
        )
        scores = scores + bias
        top = jnp.max(scores, axis=1, keepdims=True)
        weights = jnp.exp(scores - top)
        total = jnp.sum(weights, axis=1, keepdims=True)
        rounded = weights.astype(BF)
        out = jnp.zeros((step, HEAD_DIM), F32)
        for g in range(groups):
            out += dot(
                rounded[:, g * keys : (g + 1) * keys], kv_ref[g, HEAD_DIM:, :], ((1,), (1,))
            )
        parts.append(out / total)
    attended = jnp.concatenate(parts, axis=0)
    mixed = attended * gate_ref[...].astype(F32)
    mixed = jnp.concatenate([mixed, jnp.zeros((tok_rows, 128 - HEAD_DIM), F32)], axis=1)
    turned = jnp.transpose(mixed)[:HEAD_DIM].astype(BF)
    for piece in range(mixed_ref.shape[0]):
        mixed_ref[piece] = turned


def close_kernel(
    mine_ref, other_ref, w_out_ref, start_ref, gains_ref, w_up_ref, w_down_ref, w_tok_ref,
    state_ref, ids_ref, w_pos_ref, pos_ref, noise_ref,
    denoised_ref, token_ref,
):
    core = lax.rem(lax.axis_index("ba"), 2)
    tok_rows = start_ref.shape[0]
    pieces = mine_ref.shape[0]
    width = pieces * HEAD_DIM
    mine = mine_ref[...].reshape(width, tok_rows)
    other = other_ref[...].reshape(width, tok_rows)
    added = dot(mine, w_out_ref[:, core].reshape(width, D), ((0,), (0,)))
    added += dot(other, w_out_ref[:, 1 - core].reshape(width, D), ((0,), (0,)))
    mid = start_ref[...] + added
    normed = norm_rows(mid, gains_ref[1:2, :]).astype(BF)
    hidden = w_down_ref.shape[0]
    first = dot(normed, w_up_ref[:, :hidden])
    second = dot(normed, w_up_ref[:, hidden:])
    inner = (jax.nn.silu(first) * second).astype(BF)
    token_out = mid + dot(inner, w_down_ref[...])
    token_ref[...] = token_out
    normed = norm_rows(token_out, gains_ref[2:3, :]).astype(BF)
    token_atom = dot(normed, w_tok_ref[...]).astype(BF)
    atoms = state_ref.shape[0]
    tokens = lax.broadcasted_iota(jnp.int32, (tok_rows, atoms), 0)
    chosen = jnp.where(ids_ref[...] == tokens, 1.0, 0.0).astype(BF)
    final = state_ref[...] + dot(chosen, token_atom, ((0,), (0,)))
    normed = norm_rows(final, 1.0).astype(BF)
    update = dot(w_pos_ref[...], normed, ((1,), (1,)))
    sigma = jnp.full((1, 128), noise_ref[0], F32)
    inv = (1.0 / jnp.sqrt(sigma * sigma + 1.0))[:, :1]
    denoised_ref[...] = pos_ref[...] * (inv * inv) + update * (sigma[:, :1] * inv)


def shape(dims, dtype):
    return jax.ShapeDtypeStruct(dims, dtype)


def on_device(
    atom_cond, noisy_pos, noise_level, atom_token, token_cond, pair, pair_bias_weight, gains,
    w_pos, w_atom_token, w_query_gate, w_key_value, w_attn_out, w_up, w_down, w_token_atom,
    w_pos_out,
):
    atoms, chans = atom_cond.shape
    tok_rows = token_cond.shape[0]
    cols = pair.shape[1]
    size = lax.axis_size("ba")
    peers = size // 2
    groups = lax.axis_size("aa")
    row_index = lax.axis_index("aa")
    head = lax.axis_index("ba")
    same_core = [list(range(core, size, 2)) for core in range(2)]
    siblings = [(i, i ^ 1) for i in range(size)]
    smem = pl.BlockSpec(memory_space=pltpu.SMEM)

    def gathered(copies):
        mine = lax.all_to_all(copies, "ba", 0, 0, tiled=True, axis_index_groups=same_core)
        return mine, lax.ppermute(mine, "ba", siblings)

    local_ids = jnp.maximum(atom_token - row_index * tok_rows, -1)[None, :]
    state, packed = pl.pallas_call(
        state_kernel,
        out_shape=(shape((atoms, chans), F32), shape((peers, atoms + 16, chans), BF)),
        in_specs=[*whole(2), smem, *whole(2)],
        out_specs=tuple(whole(2)),
        name="state",
    )(atom_cond, noisy_pos, noise_level, local_ids, w_pos)

    block = 32
    zeros = jnp.zeros_like(pair_bias_weight)
    w_both = jnp.concatenate(
        [
            jnp.concatenate([pair_bias_weight, zeros], axis=1),
            jnp.concatenate([zeros, pair_bias_weight], axis=1),
        ],
        axis=0,
    )
    bias = pl.pallas_call(
        bias_kernel,
        grid=(tok_rows // block,),
        out_shape=shape((HEADS, tok_rows, cols), F32),
        in_specs=[
            pl.BlockSpec((block, cols, chans), lambda i: (i, 0, 0)),
            pl.BlockSpec(w_both.shape, lambda i: (0, 0)),
        ],
        out_specs=pl.BlockSpec((HEADS, block, cols), lambda i: (0, i, 0)),
        scratch_shapes=[pltpu.VMEM((HEADS * block, cols), F32)],
        compiler_params=pltpu.CompilerParams(vmem_limit_bytes=24 * MIB),
        cost_estimate=pl.CostEstimate(
            flops=2 * tok_rows * cols * chans * 256, bytes_accessed=pair.size * 2 + 2 * MIB,
            transcendentals=0,
        ),
        name="bias",
    )(pair, w_both)
    bias = lax.all_to_all(bias.astype(WIDE), "ba", 0, 0, tiled=True).astype(F32)

    def column(w, at):
        part = lax.dynamic_slice_in_dim(w, at, HEAD_DIM, 1)
        return jnp.pad(part, ((0, 0), (0, 128 - HEAD_DIM)))

    w_head = jnp.concatenate(
        [
            column(w_query_gate, head * HEAD_DIM),
            column(w_query_gate, D + head * HEAD_DIM),
            column(w_key_value, head * HEAD_DIM),
            column(w_key_value, D + head * HEAD_DIM),
        ],
        axis=1,
    )

    mine, other = gathered(packed)
    start, query, gate, kv = pl.pallas_call(
        token_kernel,
        out_shape=(
            shape((tok_rows, D), F32),
            shape((tok_rows, HEAD_DIM), BF),
            shape((tok_rows, HEAD_DIM), BF),
            shape((groups, 2 * HEAD_DIM, tok_rows), BF),
        ),
        in_specs=whole(6),
        out_specs=tuple(whole(4)),
        compiler_params=pltpu.CompilerParams(vmem_limit_bytes=32 * MIB),
        name="token",
    )(mine, other, w_atom_token, token_cond, gains, w_head)
    kv = lax.all_to_all(kv, "aa", 0, 0, tiled=True)

    mixed = pl.pallas_call(
        attend_kernel,
        out_shape=shape((peers, HEAD_DIM, tok_rows), BF),
        in_specs=whole(4),
        out_specs=whole(1)[0],
        compiler_params=pltpu.CompilerParams(vmem_limit_bytes=32 * MIB),
        name="attend",
    )(query, gate, kv, bias)
    mine, other = gathered(mixed)

    return pl.pallas_call(
        close_kernel,
        out_shape=(shape((3, atoms), F32), shape((tok_rows, D), F32)),
        in_specs=[*whole(12), smem],
        out_specs=tuple(whole(2)),
        compiler_params=pltpu.CompilerParams(vmem_limit_bytes=40 * MIB),
        name="close",
    )(
        mine, other, w_attn_out.reshape(peers, 2, HEAD_DIM, D), start, gains, w_up, w_down,
        w_token_atom, state, local_ids, w_pos_out, noisy_pos, noise_level,
    )


def solution(mesh):
    both = ("aa", "ba")
    in_specs = (
        P(both, None), P(None, both), P(), P(both), P("aa", None), P("aa", "ba", None),
        *[P()] * 11,
    )
    out_specs = (P(None, both), P("aa", None))
    return jax.shard_map(
        on_device, mesh=mesh, in_specs=in_specs, out_specs=out_specs, check_vma=False
    )
```

time: 193 us -> 84.3 us (0.44)
  waiting for transfers between devices: 67.2 us -> 17.1 us
  matrix products: 32.6 us -> 0 us
  starting transfers between devices: 41.2 us -> 23.2 us
  Pallas kernels: 0 us -> 17.9 us
  local copies, waits for them, and re-layouts: 25.2 us -> 8.78 us
  between operations: 15.2 us -> 1.4 us
  blocking collectives: 0 us -> 10.5 us
  other arithmetic: 10.7 us -> 4.76 us
    dot_general x11 -> x0, matrix products: 32.6 us -> none  [the longest x1 7.05 us: on_device(): jnp.einsum('hc,ijc->hij', pair_bias_weight, pair, preferred_element_type=...]
    all_gather x1 -> x0, waiting for transfers between devices: 27.5 us -> none  [broadcast(): lax.all_gather(shard, axis)]
    all_to_all x7 -> x3, waiting for transfers between devices: 39.7 us -> 16 us  [the longest x1 9.23 us: on_device(): bias = lax.all_to_all(bias.astype(WIDE), 'ba', 0, 0, tiled=True).astype(F32)]
    all_to_all x7 -> x3, starting transfers between devices: 41.2 us -> 19.4 us  [the longest x1 7.48 us: gathered(): lax.all_to_all(copies, 'ba', 0, 0, tiled=True, axis_index_groups=same_core)]
    pallas_call x0 -> x5, Pallas kernels: none -> 17.9 us  [the longest x1 6 us: on_device(): pl.pallas_call(token_kernel, out_shape=(shape((tok_rows, D), F32), shape(...]
    all_to_all x0 -> x1, blocking collectives: none -> 10.5 us  [gathered(): lax.all_to_all(copies, 'ba', 0, 0, tiled=True, axis_index_groups=same_core)]
    broadcast_in_dim x6 -> x0, local copies, waits for them, and re-layouts: 6.28 us -> none  [the longest x5 5.31 us: sent_to_all(): jnp.broadcast_to(shard[None], (size, *shard.shape))]
    reduce_sum x8 -> x0, other arithmetic: 5.33 us -> none  [the longest x1 1.9 us: on_device(): block_total = jnp.sum(weights, axis=2)]
  transfers between devices with their start and end apart: 8 -> 5, of which waited for: 8 -> 4; matrix products, arithmetic and copies ran while one was open for 18% -> 6% of each run, Pallas kernels for 0% -> 12%
where the time goes in v1:
time: 84.3 us; the launch traced here: 83.6 us
  starting transfers between devices  23.2 us (28%)
  Pallas kernels  17.9 us (21%)
  waiting for transfers between devices  17.1 us (20%)
  blocking collectives  10.5 us (12%)
  local copies, waits for them, and re-layouts  8.78 us (10%)
  other arithmetic  4.76 us (6%)
  between operations  1.4 us (2%)
    all_to_all x1, blocking collectives, gathered(): lax.all_to_all(copies, 'ba', 0, 0, tiled=True, axis_index_groups=same_core)  10.5 us
    all_to_all x1, waiting for transfers between devices, on_device(): bias = lax.all_to_all(bias.astype(WIDE), 'ba', 0, 0, tiled=True).astype(F32)  9.23 us
    all_to_all x1, starting transfers between devices, gathered(): lax.all_to_all(copies, 'ba', 0, 0, tiled=True, axis_index_groups=same_core)  7.48 us
    unnamed x24, local copies, waits for them, and re-layouts  7.02 us
    all_to_all x1, starting transfers between devices, on_device(): bias = lax.all_to_all(bias.astype(WIDE), 'ba', 0, 0, tiled=True).astype(F32)  6.79 us
    pallas_call x1, Pallas kernels, on_device(): pl.pallas_call(token_kernel, out_shape=(shape((tok_rows, D), F32), shape(...  6 us
    all_to_all x1, waiting for transfers between devices, on_device(): kv = lax.all_to_all(kv, 'aa', 0, 0, tiled=True)  5.37 us
    all_to_all x1, starting transfers between devices, on_device(): kv = lax.all_to_all(kv, 'aa', 0, 0, tiled=True)  5.15 us
  transfers between devices with their start and end apart: 5, of which 4 were waited for; matrix products, arithmetic and copies ran while one was open for 6% of the time, Pallas kernels for 12%

profile of v1, /device:TPU:1, one launch (start us, length us, event | category | flops | bytes accessed | tf_op | source)
XLA Modules:
  0.0 83.6 jit_solution(15198343323993626858)
XLA Ops:
  1.3 1.2 %subtract_maximum_fusion = s32[192]{0:T(256)} fusion(s32[192]{0:T(256)} %param.20, s32[]{:T(128)S(6)} %mul.4), kind=kLoop, calls=%fused_computation.24 | loop fusion | flops 384 | bytes 1540 | tf_op jit(solution)/shard_map/max | solution.py:194
  2.5 2.0 %state.1 = (f32[192,128]{1,0:T(8,128)}, bf16[8,208,128]{2,1,0:T(8,128)(2,1)}) custom-call(f32[192,128]{1,0:T(8,128)} %cond_ref.2, f32[3,192]{1,0:T(4,128)} %pos_ref.3, f32[1]{0:T(128)S(6)} %copy.19.noise_ref, s32[1,192]{1,0:T(1,128)} %bitcast.3, f32[3,128]{1,0:T(4,128)} %w_pos_ref.2), custom_call_target="tpu_custom_call" | custom-call | tf_op jit(solution)/shard_map/state/pallas_call | solution.py:195
  4.5 7.5 %all-to-all-start = ((bf16[8,208,128]{2,1,0:T(8,128)(2,1)}), bf16[8,208,128]{2,1,0:T(8,128)(2,1)S(1)}, u32[]{:S(2)}, u32[]{:S(2)}) async-start(bf16[8,208,128]{2,1,0:T(8,128)(2,1)} %get-tuple-element.8), calls=%async_computation | async-start | bytes 851968 | tf_op jit(solution)/shard_map/all_to_all | solution.py:191
  12.0 0.8 fusion.11.w_ref
  12.8 0.0 copy-start
  12.8 3.4 %copy-done = bf16[256,128,128]{2,1,0:T(8,128)(2,1)S(1)} copy-done((bf16[256,128,128]{2,1,0:T(8,128)(2,1)S(1)}, bf16[256,128,128]{2,1,0:T(8,128)(2,1)}, u32[]{:S(2)}) %copy-start) | copy-done | bytes 8388632
  16.2 3.9 %bias.1 = f32[16,256,128]{2,1,0:T(8,128)S(1)} custom-call(bf16[256,128,128]{2,1,0:T(8,128)(2,1)S(1)} %copy-done, bf16[32,256]{1,0:T(8,128)(2,1)S(1)} %fusion.11.w_ref), custom_call_target="tpu_custom_call" | custom-call | flops 2147483648 | bytes 10485760 | tf_op jit(solution)/shard_map/bias/pallas_call | solution.py:212
  20.1 1.2 %convert_element_type.11 = f16[16,256,128]{2,1,0:T(8,128)(2,1)} convert(f32[16,256,128]{2,1,0:T(8,128)S(1)} %bias.1) | non-fusion elementwise | flops 524288 | bytes 3145728 | tf_op jit(solution)/shard_map/convert_element_type | solution.py:229
  21.3 1.4 %all-to-all-done.mine_ref = bf16[8,208,128]{2,1,0:T(8,128)(2,1)S(1)} async-done(((bf16[8,208,128]{2,1,0:T(8,128)(2,1)}), bf16[8,208,128]{2,1,0:T(8,128)(2,1)S(1)}, u32[]{:S(2)}, u32[]{:S(2)}) %all-to-all-start) | async-done | bytes 426016 | tf_op jit(solution)/shard_map/all_to_all | solution.py:191
  22.7 6.8 %all-to-all-start.2 = ((f16[16,256,128]{2,1,0:T(8,128)(2,1)}), f16[16,256,128]{2,1,0:T(8,128)(2,1)}, u32[]{:S(2)}, u32[]{:S(2)}) async-start(f16[16,256,128]{2,1,0:T(8,128)(2,1)} %convert_element_type.11), calls=%async_computation.2 | async-start | bytes 2097152 | tf_op jit(solution)/shard_map/all_to_all | solution.py:229
  29.5 0.2 collective-permute-start
  29.7 0.0 copy-start.4
  29.7 0.0 copy-start.5
  29.7 0.0 copy-start.8
  29.7 1.8 %constant_dynamic-slice_fusion.1 = (bf16[768,48]{1,0:T(8,128)(2,1)S(1)}, bf16[768,48]{1,0:T(8,128)(2,1)S(1)}, bf16[768,48]{1,0:T(8,128)(2,1)S(1)}, bf16[768,48]{1,0:T(8,128)(2,1)S(1)}) fusion(bf16[768,1536]{1,0:T(8,128)(2,1)} %param.28, s32[]{:T(128)S(6)} %select_n.8, s32[]{:T(128)S(6)} %select_n.9, bf16[768,1536]{1,0:T(8,128)(2,1)} %param.27), kind=kLoop, calls=%fused_computation.21 | loop fusion | bytes 589832 | tf_op jit(solution)/shard_map/dynamic_slice | solution.py:232
  31.5 0.2 fusion.7.w_head_ref
  31.7 0.0 collective-permute-done.other_ref
  31.7 0.0 copy-done.4
  31.7 0.0 copy-done.5
  31.7 0.0 copy-done.8
  31.7 6.0 %token_.1 = (f32[256,768]{1,0:T(8,128)S(1)}, bf16[256,48]{1,0:T(8,128)(2,1)S(1)}, bf16[256,48]{1,0:T(8,128)(2,1)S(1)}, bf16[8,96,256]{2,1,0:T(8,128)(2,1)}) custom-call(bf16[8,208,128]{2,1,0:T(8,128)(2,1)S(1)} %all-to-all-done.mine_ref, bf16[8,208,128]{2,1,0:T(8,128)(2,1)S(1)} %collective-permute-done.other_ref, bf16[128,768]{1,0:T(8,128)(2,1)S(1)} %copy-done.5, ...), custom_call_target="tpu_custom_call" | custom-call | tf_op jit(solution)/shard_map/token/pallas_call | solution.py:246
  37.7 9.2 %all-to-all-done.2 = f16[16,256,128]{2,1,0:T(8,128)(2,1)} async-done(((f16[16,256,128]{2,1,0:T(8,128)(2,1)}), f16[16,256,128]{2,1,0:T(8,128)(2,1)}, u32[]{:S(2)}, u32[]{:S(2)}) %all-to-all-start.2) | async-done | bytes 1048608 | tf_op jit(solution)/shard_map/all_to_all | solution.py:229
  46.9 5.2 %all-to-all-start.1 = ((bf16[8,96,256]{2,1,0:T(8,128)(2,1)}), bf16[8,96,256]{2,1,0:T(8,128)(2,1)S(1)}, u32[]{:S(2)}, u32[]{:S(2)}) async-start(bf16[8,96,256]{2,1,0:T(8,128)(2,1)} %get-tuple-element.11), calls=%async_computation.1 | async-start | bytes 786432 | tf_op jit(solution)/shard_map/all_to_all | solution.py:259
  52.1 1.4 %convert_element_type.12.bias_ref = f32[16,256,128]{2,1,0:T(8,128)S(1)} convert(f16[16,256,128]{2,1,0:T(8,128)(2,1)} %all-to-all-done.2) | non-fusion elementwise | flops 524288 | bytes 3145728 | tf_op jit(solution)/shard_map/convert_element_type | solution.py:229
  53.5 5.4 %all-to-all-done.1.kv_ref = bf16[8,96,256]{2,1,0:T(8,128)(2,1)S(1)} async-done(((bf16[8,96,256]{2,1,0:T(8,128)(2,1)}), bf16[8,96,256]{2,1,0:T(8,128)(2,1)S(1)}, u32[]{:S(2)}, u32[]{:S(2)}) %all-to-all-start.1) | async-done | bytes 393248 | tf_op jit(solution)/shard_map/all_to_all | solution.py:259
  58.8 0.0 copy-start.2
  58.8 0.0 copy-start.6
  58.8 0.0 copy-start.7
  58.8 0.0 copy-start.9
  58.8 0.0 copy-start.10
  58.9 0.0 copy-start.11
  58.9 1.3 %attend.1 = bf16[8,48,256]{2,1,0:T(8,128)(2,1)S(1)} custom-call(bf16[256,48]{1,0:T(8,128)(2,1)S(1)} %get-tuple-element.9.query_ref, bf16[256,48]{1,0:T(8,128)(2,1)S(1)} %get-tuple-element.10.gate_ref, bf16[8,96,256]{2,1,0:T(8,128)(2,1)S(1)} %all-to-all-done.1.kv_ref, f32[16,256,128]{2,1,0:T(8,128)S(1)} %convert_element_type.12.bias_ref), custom_call_target="tpu_custom_call" | custom-call | tf_op jit(solution)/shard_map/attend/pallas_call | solution.py:261
  60.2 10.5 %all_to_all.20.mine_ref = bf16[8,48,256]{2,1,0:T(8,128)(2,1)S(1)} all-to-all(bf16[8,48,256]{2,1,0:T(8,128)(2,1)S(1)} %attend.1), channel_id=1, replica_groups={{0,2,4,6,8,10,12,14},{1,3,5,7,9,11,13,15},{16,18,20,22,24,26,28,30},{17..., dimensions={0} | all-to-all | bytes 393216 | tf_op jit(solution)/shard_map/all_to_all | solution.py:191
  70.7 3.6 %collective-permute-start.1 = (bf16[8,48,256]{2,1,0:T(8,128)(2,1)S(1)}, bf16[8,48,256]{2,1,0:T(8,128)(2,1)S(1)}, u32[]{:S(2)}, u32[]{:S(2)}) collective-permute-start(bf16[8,48,256]{2,1,0:T(8,128)(2,1)S(1)} %all_to_all.20.mine_ref), channel_id=1, source_target_pairs={{0,1},{1,0},{2,3},{3,2},{4,5},{5,4},{6,7},{7,6},{8,9},{9,8},{10,11... | collective-permute-start | bytes 589832 | tf_op jit(solution)/shard_map/ppermute | solution.py:192
  74.2 1.1 %collective-permute-done.1.other_ref = bf16[8,48,256]{2,1,0:T(8,128)(2,1)S(1)} collective-permute-done((bf16[8,48,256]{2,1,0:T(8,128)(2,1)S(1)}, bf16[8,48,256]{2,1,0:T(8,128)(2,1)S(1)}, u32[]{:S(2)}, u32[]{:S(2)}) %collective-permute-start.1) | collective-permute-done | bytes 196640 | tf_op jit(solution)/shard_map/ppermute | solution.py:192
  75.3 0.0 copy-done.2
  75.3 0.0 copy-done.6
  75.3 0.0 copy-done.7
  75.3 0.0 copy-done.9
  75.3 0.0 copy-done.10
  75.3 0.0 copy-done.11
  75.3 0.0 copy-start.1
  75.4 2.3 %copy-done.1 = bf16[768,3072]{1,0:T(8,128)(2,1)S(1)} copy-done((bf16[768,3072]{1,0:T(8,128)(2,1)S(1)}, bf16[768,3072]{1,0:T(8,128)(2,1)}, u32[]{:S(2)}) %copy-start.1) | copy-done | bytes 4718616
  77.7 0.0 copy-start.3
  77.7 1.3 %copy-done.3 = bf16[768,768]{1,0:T(8,128)(2,1)S(1)} copy-done((bf16[768,768]{1,0:T(8,128)(2,1)S(1)}, bf16[768,768]{1,0:T(8,128)(2,1)}, u32[]{:S(2)}) %copy-start.3) | copy-done | bytes 1179672
  79.0 4.6 %close.1 = (f32[3,192]{1,0:T(4,128)}, f32[256,768]{1,0:T(8,128)}) custom-call(bf16[8,48,256]{2,1,0:T(8,128)(2,1)S(1)} %all_to_all.20.mine_ref, bf16[8,48,256]{2,1,0:T(8,128)(2,1)S(1)} %collective-permute-done.1.other_ref, bf16[8,2,48,768]{3,2,1,0:T(8,128)(2,1)S(1)} %bitcast.2, f32[256,768]{1,0:T(8,128)S(1)} %get-tuple-element.12.start_ref, ...), custom_call_target="tpu_custom_call" | custom-call | tf_op jit(solution)/shard_map/close/pallas_call | solution.py:271
Async XLA Ops:
  4.5 18.1 %all-to-all-start = ((bf16[8,208,128]{2,1,0:T(8,128)(2,1)}), bf16[8,208,128]{2,1,0:T(8,128)(2,1)S(1)}, u32[]{:S(2)}, u32[]{:S(2)}) async-start(bf16[8,208,128]{2,1,0:T(8,128)(2,1)} %get-tuple-element.8), calls=%async_computation | async-start | bytes 851968 | tf_op jit(solution)/shard_map/all_to_all | solution.py:191
  12.8 3.4 %copy-start = (bf16[256,128,128]{2,1,0:T(8,128)(2,1)S(1)}, bf16[256,128,128]{2,1,0:T(8,128)(2,1)}, u32[]{:S(2)}) copy-start(bf16[256,128,128]{2,1,0:T(8,128)(2,1)} %pair_ref.1) | copy-start | bytes 25165828
  22.7 24.3 %all-to-all-start.2 = ((f16[16,256,128]{2,1,0:T(8,128)(2,1)}), f16[16,256,128]{2,1,0:T(8,128)(2,1)}, u32[]{:S(2)}, u32[]{:S(2)}) async-start(f16[16,256,128]{2,1,0:T(8,128)(2,1)} %convert_element_type.11), calls=%async_computation.2 | async-start | bytes 2097152 | tf_op jit(solution)/shard_map/all_to_all | solution.py:229
  29.5 2.2 %collective-permute-start = (bf16[8,208,128]{2,1,0:T(8,128)(2,1)S(1)}, bf16[8,208,128]{2,1,0:T(8,128)(2,1)S(1)}, u32[]{:S(2)}, u32[]{:S(2)}) collective-permute-start(bf16[8,208,128]{2,1,0:T(8,128)(2,1)S(1)} %all-to-all-done.mine_ref), channel_id=1, source_target_pairs={{0,1},{1,0},{2,3},{3,2},{4,5},{5,4},{6,7},{7,6},{8,9},{9,8},{10,11... | collective-permute-start | bytes 1277960 | tf_op jit(solution)/shard_map/ppermute | solution.py:192
  29.7 2.0 %copy-start.4 = (f32[256,768]{1,0:T(8,128)S(1)}, f32[256,768]{1,0:T(8,128)}, u32[]{:S(2)}) copy-start(f32[256,768]{1,0:T(8,128)} %cond_ref.3) | copy-start | bytes 2359300
  29.7 2.0 %copy-start.5 = (bf16[128,768]{1,0:T(8,128)(2,1)S(1)}, bf16[128,768]{1,0:T(8,128)(2,1)}, u32[]{:S(2)}) copy-start(bf16[128,768]{1,0:T(8,128)(2,1)} %w_atom_ref.1) | copy-start | bytes 589828
  29.7 2.0 %copy-start.8 = (f32[3,768]{1,0:T(4,128)S(1)}, f32[3,768]{1,0:T(4,128)}, u32[]{:S(2)}) copy-start(f32[3,768]{1,0:T(4,128)} %gains_ref.3) | copy-start | bytes 27652
  46.9 11.9 %all-to-all-start.1 = ((bf16[8,96,256]{2,1,0:T(8,128)(2,1)}), bf16[8,96,256]{2,1,0:T(8,128)(2,1)S(1)}, u32[]{:S(2)}, u32[]{:S(2)}) async-start(bf16[8,96,256]{2,1,0:T(8,128)(2,1)} %get-tuple-element.11), calls=%async_computation.1 | async-start | bytes 786432 | tf_op jit(solution)/shard_map/all_to_all | solution.py:259
  58.8 16.5 %copy-start.2 = (bf16[1536,768]{1,0:T(8,128)(2,1)S(1)}, bf16[1536,768]{1,0:T(8,128)(2,1)}, u32[]{:S(2)}) copy-start(bf16[1536,768]{1,0:T(8,128)(2,1)} %w_down_ref.1) | copy-start | bytes 7077892
  58.8 16.5 %copy-start.6 = (bf16[768,128]{1,0:T(8,128)(2,1)S(1)}, bf16[768,128]{1,0:T(8,128)(2,1)}, u32[]{:S(2)}) copy-start(bf16[768,128]{1,0:T(8,128)(2,1)} %w_tok_ref.1) | copy-start | bytes 589828
  58.8 16.5 %copy-start.7 = (f32[192,128]{1,0:T(8,128)S(1)}, f32[192,128]{1,0:T(8,128)}, u32[]{:S(2)}) copy-start(f32[192,128]{1,0:T(8,128)} %get-tuple-element.13.state_ref) | copy-start | bytes 294916
  58.8 16.5 %copy-start.9 = (f32[3,192]{1,0:T(4,128)S(1)}, f32[3,192]{1,0:T(4,128)}, u32[]{:S(2)}) copy-start(f32[3,192]{1,0:T(4,128)} %pos_ref.3) | copy-start | bytes 6916
  58.8 16.5 %copy-start.10 = (s32[192]{0:T(256)S(1)}, s32[192]{0:T(256)}, u32[]{:S(2)}) copy-start(s32[192]{0:T(256)} %subtract_maximum_fusion) | copy-start | bytes 2308
  58.9 16.5 %copy-start.11 = (bf16[3,128]{1,0:T(4,128)(2,1)S(1)}, bf16[3,128]{1,0:T(4,128)(2,1)}, u32[]{:S(2)}) copy-start(bf16[3,128]{1,0:T(4,128)(2,1)} %w_pos_ref.3) | copy-start | bytes 2308
  70.7 4.7 %collective-permute-start.1 = (bf16[8,48,256]{2,1,0:T(8,128)(2,1)S(1)}, bf16[8,48,256]{2,1,0:T(8,128)(2,1)S(1)}, u32[]{:S(2)}, u32[]{:S(2)}) collective-permute-start(bf16[8,48,256]{2,1,0:T(8,128)(2,1)S(1)} %all_to_all.20.mine_ref), channel_id=1, source_target_pairs={{0,1},{1,0},{2,3},{3,2},{4,5},{5,4},{6,7},{7,6},{8,9},{9,8},{10,11... | collective-permute-start | bytes 589832 | tf_op jit(solution)/shard_map/ppermute | solution.py:192
  75.3 2.3 %copy-start.1 = (bf16[768,3072]{1,0:T(8,128)(2,1)S(1)}, bf16[768,3072]{1,0:T(8,128)(2,1)}, u32[]{:S(2)}) copy-start(bf16[768,3072]{1,0:T(8,128)(2,1)} %w_up_ref.1) | copy-start | bytes 14155780
  77.7 1.3 %copy-start.3 = (bf16[768,768]{1,0:T(8,128)(2,1)S(1)}, bf16[768,768]{1,0:T(8,128)(2,1)}, u32[]{:S(2)}) copy-start(bf16[768,768]{1,0:T(8,128)(2,1)} %param.29) | copy-start | bytes 3538948

commit v2 on v1

--- a/solution.py
+++ b/solution.py
@@ -12,7 +12,6 @@
 HEAD_DIM = D // HEADS
 BF = jnp.bfloat16
 F32 = jnp.float32
-WIDE = jnp.float16
 MIB = 1 << 20
 
 
@@ -31,7 +30,7 @@
     return [pl.BlockSpec(memory_space=pltpu.VMEM)] * n
 
 
-def state_kernel(cond_ref, pos_ref, noise_ref, ids_ref, w_pos_ref, state_ref, packed_ref):
+def state_kernel(tok_rows, cond_ref, pos_ref, noise_ref, ids_ref, w_pos_ref, state_ref, packed_ref):
     atoms = cond_ref.shape[0]
     sigma = noise_ref[0]
     sigma = jnp.full((1, 128), sigma, F32)
@@ -43,7 +42,7 @@
     state = state + pos[:, 1:2] * w_pos_ref[1:2, :]
     state = state + pos[:, 2:3] * w_pos_ref[2:3, :]
     state_ref[...] = state
-    ids = ids_ref[...].astype(F32)
+    ids = (ids_ref[...] - lax.axis_index("aa") * tok_rows).astype(F32)
     first = ids[:, :128]
     second = jnp.concatenate([ids[:, 128:], jnp.zeros((1, 256 - atoms), F32)], axis=1)
     tail = jnp.concatenate([first, second, jnp.zeros((14, 128), F32)], axis=0).astype(BF)
@@ -53,41 +52,85 @@
         packed_ref[piece, atoms:, :] = tail
 
 
-def bias_kernel(pair_ref, w_ref, out_ref, held):
-    rows, cols, chans = pair_ref.shape
+def bias_kernel(pair_ref, w_ref, out_ref, pair_vmem, held, tops, sems):
+    tok_rows, cols, chans = pair_ref.shape
+    rows = pair_vmem.shape[1]
     half = rows // 2
-    both = jnp.concatenate(
+    parts = tok_rows // rows
+
+    def arrival(part):
+        return pltpu.make_async_copy(
+            pair_ref.at[pl.ds(part * rows, rows)], pair_vmem.at[part], sems.at[part]
+        )
+
+    for part in range(parts):
+        arrival(part).start()
+    zeros = jnp.zeros((HEADS, chans), BF)
+    weight = w_ref[...]
+    weight = jnp.concatenate(
         [
-            pair_ref[:half].reshape(half * cols, chans),
-            pair_ref[half:].reshape(half * cols, chans),
+            jnp.concatenate([weight, zeros], axis=1),
+            jnp.concatenate([zeros, weight], axis=1),
         ],
-        axis=1,
-    )
-    bias = dot(w_ref[...], both, ((1,), (1,)))
-    for i in range(half):
-        held[pl.ds(i, HEADS, stride=rows), :] = bias[:HEADS, i * cols : (i + 1) * cols]
-        held[pl.ds(half + i, HEADS, stride=rows), :] = bias[HEADS:, i * cols : (i + 1) * cols]
-    out_ref[...] = held[...].reshape(HEADS, rows, cols).astype(out_ref.dtype)
+        axis=0,
+    )
+    lanes = lax.broadcasted_iota(jnp.int32, (rows, 128), 1)
+    for part in range(parts):
+        arrival(part).wait()
+        both = jnp.concatenate(
+            [
+                pair_vmem[part, :half].reshape(half * cols, chans),
+                pair_vmem[part, half:].reshape(half * cols, chans),
+            ],
+            axis=1,
+        )
+        bias = dot(weight, both, ((1,), (1,)))
+        at = (part % 2) * HEADS * rows
+        for i in range(half):
+            here = slice(i * cols, (i + 1) * cols)
+            held[pl.ds(at + i, HEADS, stride=rows), :] = bias[:HEADS, here]
+            held[pl.ds(at + half + i, HEADS, stride=rows), :] = bias[HEADS:, here]
+        top_of = jnp.zeros((rows, 128), F32)
+        for h in range(HEADS):
+            lines = held[at + h * rows : at + (h + 1) * rows, :]
+            top = jnp.max(lines, axis=1, keepdims=True)
+            out_ref[h, part * rows : (part + 1) * rows, :] = (lines - top).astype(BF)
+            top_of = jnp.where(lanes == h, top, top_of)
+        tops[part * rows : (part + 1) * rows, :] = top_of
+    top = jnp.transpose(tops[...])[:HEADS]
+    high = top.astype(BF).astype(F32)
+    rest = top - high
+    middle = rest.astype(BF).astype(F32)
+    low = rest - middle
+    pad = jnp.zeros((16 - 3 * tok_rows // 128, 128), F32)
+    for h in range(HEADS):
+        lines = [
+            term[h : h + 1, r : r + 128]
+            for term in (high, middle, low)
+            for r in range(0, tok_rows, 128)
+        ]
+        out_ref[h, tok_rows:, :] = jnp.concatenate([*lines, pad], axis=0).astype(BF)
 
 
 def token_kernel(
     mine_ref, other_ref, w_atom_ref, cond_ref, gains_ref, w_head_ref,
-    start_ref, query_ref, gate_ref, kv_ref,
+    start_ref, query_ref, gate_ref, kv_ref, hidden_ref,
 ):
     tok_rows = cond_ref.shape[0]
     atoms = mine_ref.shape[1] - 16
-    tokens = lax.broadcasted_iota(jnp.int32, (tok_rows, atoms), 0).astype(F32)
-    sums = jnp.zeros((tok_rows, D), F32)
-    counts = jnp.zeros((tok_rows, atoms), F32)
-    for ref in (mine_ref, other_ref):
+    ids = []
+    for at, ref in enumerate((mine_ref, other_ref)):
         for piece in range(ref.shape[0]):
-            hidden = jax.nn.relu(dot(ref[piece, :atoms, :], w_atom_ref[...])).astype(BF)
+            hidden = jax.nn.relu(dot(ref[piece, :atoms, :], w_atom_ref[...]))
+            row = (at * ref.shape[0] + piece) * atoms
+            hidden_ref[row : row + atoms, :] = hidden.astype(BF)
             tail = ref[piece, atoms:, :].astype(F32)
-            ids = jnp.concatenate([tail[0:1, :], tail[1:2, : atoms - 128]], axis=1)
-            chosen = jnp.where(ids == tokens, 1.0, 0.0)
-            counts += chosen
-            sums += dot(chosen.astype(BF), hidden)
-    start = cond_ref[...] + sums / jnp.sum(counts, axis=1, keepdims=True)
+            ids += [tail[0:1, :], tail[1:2, : atoms - 128]]
+    ids = jnp.concatenate(ids, axis=1)
+    tokens = lax.broadcasted_iota(jnp.int32, (tok_rows, ids.shape[1]), 0).astype(F32)
+    chosen = jnp.where(ids == tokens, 1.0, 0.0)
+    counts = jnp.sum(chosen, axis=1, keepdims=True)
+    start = cond_ref[...] + dot(chosen.astype(BF), hidden_ref[...]) / counts
     start_ref[...] = start
     normed = norm_rows(start, gains_ref[0:1, :]).astype(BF)
     projected = dot(normed, w_head_ref[...])
@@ -95,23 +138,39 @@
     gate_ref[...] = jax.nn.sigmoid(projected[:, 128 : 128 + HEAD_DIM]).astype(BF)
     kv = jnp.transpose(projected[:, 256:512])
     kv = jnp.concatenate([kv[:HEAD_DIM], kv[128 : 128 + HEAD_DIM]], axis=0).astype(BF)
-    for piece in range(kv_ref.shape[0]):
-        kv_ref[piece] = kv
-
-
-def attend_kernel(query_ref, gate_ref, kv_ref, bias_ref, mixed_ref):
-    groups, _, keys = kv_ref.shape
+    kv_ref[...] = kv
+
+
+def attend_kernel(query_ref, gate_ref, bias_ref, *refs):
+    kv_refs, mixed_ref = refs[:-1], refs[-1]
+    groups = len(kv_refs)
+    keys = kv_refs[0].shape[1]
     tok_rows = query_ref.shape[0]
-    blocks, _, cols = bias_ref.shape
+    me = lax.axis_index("aa")
+    per = keys // bias_ref.shape[2]
+    order = [
+        lax.bitwise_xor(me, g) * per + b for g in range(groups) for b in range(per)
+    ]
+    tops = []
+    for at in order:
+        tail = bias_ref[at, tok_rows:, :].astype(F32)
+        n = tok_rows // 128
+        lines = tail[:n] + tail[n : 2 * n] + tail[2 * n : 3 * n]
+        tops.append(jnp.concatenate([lines[i : i + 1] for i in range(n)], axis=1))
+    tops = jnp.transpose(jnp.concatenate(tops, axis=0))
     step = 64
     parts = []
     for r in range(0, tok_rows, step):
         query = query_ref[r : r + step, :]
         scores = jnp.concatenate(
-            [dot(query, kv_ref[g, :HEAD_DIM, :]) for g in range(groups)], axis=1
+            [dot(query, ref[:HEAD_DIM, :]) for ref in kv_refs], axis=1
         ) * HEAD_DIM ** (-0.5)
         bias = jnp.concatenate(
-            [bias_ref[b, r : r + step, :].astype(F32) for b in range(blocks)], axis=1
+            [
+                bias_ref[at, r : r + step, :].astype(F32) + tops[r : r + step, i : i + 1]
+                for i, at in enumerate(order)
+            ],
+            axis=1,
         )
         scores = scores + bias
         top = jnp.max(scores, axis=1, keepdims=True)
@@ -121,7 +180,7 @@
         out = jnp.zeros((step, HEAD_DIM), F32)
         for g in range(groups):
             out += dot(
-                rounded[:, g * keys : (g + 1) * keys], kv_ref[g, HEAD_DIM:, :], ((1,), (1,))
+                rounded[:, g * keys : (g + 1) * keys], kv_refs[g][HEAD_DIM:, :], ((1,), (1,))
             )
         parts.append(out / total)
     attended = jnp.concatenate(parts, axis=0)
@@ -157,6 +216,7 @@
     token_atom = dot(normed, w_tok_ref[...]).astype(BF)
     atoms = state_ref.shape[0]
     tokens = lax.broadcasted_iota(jnp.int32, (tok_rows, atoms), 0)
+    tokens += lax.axis_index("aa") * tok_rows
     chosen = jnp.where(ids_ref[...] == tokens, 1.0, 0.0).astype(BF)
     final = state_ref[...] + dot(chosen, token_atom, ((0,), (0,)))
     normed = norm_rows(final, 1.0).astype(BF)
@@ -181,7 +241,6 @@
     size = lax.axis_size("ba")
     peers = size // 2
     groups = lax.axis_size("aa")
-    row_index = lax.axis_index("aa")
     head = lax.axis_index("ba")
     same_core = [list(range(core, size, 2)) for core in range(2)]
     siblings = [(i, i ^ 1) for i in range(size)]
@@ -191,42 +250,35 @@
         mine = lax.all_to_all(copies, "ba", 0, 0, tiled=True, axis_index_groups=same_core)
         return mine, lax.ppermute(mine, "ba", siblings)
 
-    local_ids = jnp.maximum(atom_token - row_index * tok_rows, -1)[None, :]
+    ids = atom_token[None, :]
     state, packed = pl.pallas_call(
-        state_kernel,
+        functools.partial(state_kernel, tok_rows),
         out_shape=(shape((atoms, chans), F32), shape((peers, atoms + 16, chans), BF)),
         in_specs=[*whole(2), smem, *whole(2)],
         out_specs=tuple(whole(2)),
         name="state",
-    )(atom_cond, noisy_pos, noise_level, local_ids, w_pos)
+    )(atom_cond, noisy_pos, noise_level, ids, w_pos)
 
     block = 32
-    zeros = jnp.zeros_like(pair_bias_weight)
-    w_both = jnp.concatenate(
-        [
-            jnp.concatenate([pair_bias_weight, zeros], axis=1),
-            jnp.concatenate([zeros, pair_bias_weight], axis=1),
-        ],
-        axis=0,
-    )
     bias = pl.pallas_call(
         bias_kernel,
-        grid=(tok_rows // block,),
-        out_shape=shape((HEADS, tok_rows, cols), F32),
-        in_specs=[
-            pl.BlockSpec((block, cols, chans), lambda i: (i, 0, 0)),
-            pl.BlockSpec(w_both.shape, lambda i: (0, 0)),
+        out_shape=shape((HEADS, tok_rows + 16, cols), BF),
+        in_specs=[pl.BlockSpec(memory_space=pl.ANY), *whole(1)],
+        out_specs=whole(1)[0],
+        scratch_shapes=[
+            pltpu.VMEM((tok_rows // block, block, cols, chans), BF),
+            pltpu.VMEM((2 * HEADS * block, cols), F32),
+            pltpu.VMEM((tok_rows, 128), F32),
+            pltpu.SemaphoreType.DMA((tok_rows // block,)),
         ],
-        out_specs=pl.BlockSpec((HEADS, block, cols), lambda i: (0, i, 0)),
-        scratch_shapes=[pltpu.VMEM((HEADS * block, cols), F32)],
-        compiler_params=pltpu.CompilerParams(vmem_limit_bytes=24 * MIB),
+        compiler_params=pltpu.CompilerParams(vmem_limit_bytes=57 * MIB),
         cost_estimate=pl.CostEstimate(
             flops=2 * tok_rows * cols * chans * 256, bytes_accessed=pair.size * 2 + 2 * MIB,
             transcendentals=0,
         ),
         name="bias",
-    )(pair, w_both)
-    bias = lax.all_to_all(bias.astype(WIDE), "ba", 0, 0, tiled=True).astype(F32)
+    )(pair, pair_bias_weight)
+    bias = lax.all_to_all(bias, "ba", 0, 0, tiled=True).astype(F32)
 
     def column(w, at):
         part = lax.dynamic_slice_in_dim(w, at, HEAD_DIM, 1)
@@ -249,23 +301,29 @@
             shape((tok_rows, D), F32),
             shape((tok_rows, HEAD_DIM), BF),
             shape((tok_rows, HEAD_DIM), BF),
-            shape((groups, 2 * HEAD_DIM, tok_rows), BF),
+            shape((2 * HEAD_DIM, tok_rows), BF),
         ),
         in_specs=whole(6),
         out_specs=tuple(whole(4)),
-        compiler_params=pltpu.CompilerParams(vmem_limit_bytes=32 * MIB),
+        scratch_shapes=[pltpu.VMEM((size * atoms, D), BF)],
+        compiler_params=pltpu.CompilerParams(vmem_limit_bytes=24 * MIB),
         name="token",
     )(mine, other, w_atom_token, token_cond, gains, w_head)
-    kv = lax.all_to_all(kv, "aa", 0, 0, tiled=True)
+    spread = [kv]
+    for far in range(1, groups):
+        spread.append(lax.ppermute(kv, "aa", [(i, i ^ far) for i in range(groups)]))
 
     mixed = pl.pallas_call(
         attend_kernel,
         out_shape=shape((peers, HEAD_DIM, tok_rows), BF),
-        in_specs=whole(4),
+        in_specs=whole(3 + groups),
         out_specs=whole(1)[0],
-        compiler_params=pltpu.CompilerParams(vmem_limit_bytes=32 * MIB),
+        compiler_params=pltpu.CompilerParams(vmem_limit_bytes=16 * MIB),
+        cost_estimate=pl.CostEstimate(
+            flops=20_000_000_000, bytes_accessed=8 * MIB, transcendentals=0
+        ),
         name="attend",
-    )(query, gate, kv, bias)
+    )(query, gate, bias, *spread)
     mine, other = gathered(mixed)
 
     return pl.pallas_call(
@@ -273,11 +331,11 @@
         out_shape=(shape((3, atoms), F32), shape((tok_rows, D), F32)),
         in_specs=[*whole(12), smem],
         out_specs=tuple(whole(2)),
-        compiler_params=pltpu.CompilerParams(vmem_limit_bytes=40 * MIB),
+        compiler_params=pltpu.CompilerParams(vmem_limit_bytes=24 * MIB),
         name="close",
     )(
         mine, other, w_attn_out.reshape(peers, 2, HEAD_DIM, D), start, gains, w_up, w_down,
-        w_token_atom, state, local_ids, w_pos_out, noisy_pos, noise_level,
+        w_token_atom, state, ids, w_pos_out, noisy_pos, noise_level,
     )
 
 

time: 84.3 us -> 75.2 us (0.89)
  waiting for transfers between devices: 17.1 us -> 8.42 us
  local copies, waits for them, and re-layouts: 8.78 us -> 1.81 us
  starting transfers between devices: 23.2 us -> 28.5 us
  other arithmetic: 4.76 us -> 0.34 us
  blocking collectives: 10.5 us -> 14.1 us
  Pallas kernels: 17.9 us -> 20.2 us
    all_to_all x2 -> x1, waiting for transfers between devices: 14.6 us -> 1.11 us  [on_device(): bias = lax.all_to_all(bias, 'ba', 0, 0, tiled=True).astype(F32)]
    ppermute x0 -> x7, starting transfers between devices: none -> 11 us  [on_device(): spread.append(lax.ppermute(kv, 'aa', [(i, i ^ far) for i in range(groups)]))]
    unnamed x24, local copies, waits for them, and re-layouts: 7.02 us -> 0.06 us
    all_to_all x2 -> x1, starting transfers between devices: 11.9 us -> 5.4 us  [on_device(): bias = lax.all_to_all(bias, 'ba', 0, 0, tiled=True).astype(F32)]
    pallas_call x2, Pallas kernels: 5.94 us -> 9.87 us  [the longest x1 7.84 us: on_device(): pl.pallas_call(bias_kernel, out_shape=shape((HEADS, tok_rows + 16, cols),...]
    all_to_all x1, blocking collectives: 10.5 us -> 14.1 us  [gathered(): lax.all_to_all(copies, 'ba', 0, 0, tiled=True, axis_index_groups=same_core)]
    ppermute x0 -> x7, waiting for transfers between devices: none -> 3.44 us  [on_device(): spread.append(lax.ppermute(kv, 'aa', [(i, i ^ far) for i in range(groups)]))]
    convert_element_type x2 -> x1, other arithmetic: 2.56 us -> 0.15 us  [on_device(): bias = lax.all_to_all(bias, 'ba', 0, 0, tiled=True).astype(F32)]
  transfers between devices with their start and end apart: 5 -> 11, of which waited for: 4 -> 5; matrix products, arithmetic and copies ran while one was open for 6% -> 3% of each run, Pallas kernels for 12% -> 16%
where the time goes in v2:
time: 75.2 us; the launch traced here: 74.8 us
  starting transfers between devices  28.5 us (38%)
  Pallas kernels  20.2 us (27%)
  blocking collectives  14.1 us (19%)
  waiting for transfers between devices  8.42 us (11%)
  local copies, waits for them, and re-layouts  1.81 us (2%)
  between operations  1.47 us (2%)
    all_to_all x1, blocking collectives, gathered(): lax.all_to_all(copies, 'ba', 0, 0, tiled=True, axis_index_groups=same_core)  14.1 us
    ppermute x7, starting transfers between devices, on_device(): spread.append(lax.ppermute(kv, 'aa', [(i, i ^ far) for i in range(groups)]))  11 us
    pallas_call x1, Pallas kernels, on_device(): pl.pallas_call(bias_kernel, out_shape=shape((HEADS, tok_rows + 16, cols),...  7.84 us
    all_to_all x1, starting transfers between devices, gathered(): lax.all_to_all(copies, 'ba', 0, 0, tiled=True, axis_index_groups=same_core)  7.48 us
    all_to_all x1, starting transfers between devices, on_device(): bias = lax.all_to_all(bias, 'ba', 0, 0, tiled=True).astype(F32)  5.4 us
    ppermute x2, starting transfers between devices, gathered(): return (mine, lax.ppermute(mine, 'ba', siblings))  4.61 us
    pallas_call x1, Pallas kernels, on_device(): pl.pallas_call(close_kernel, out_shape=(shape((3, atoms), F32), shape((to...  4.58 us
    pallas_call x1, Pallas kernels, on_device(): pl.pallas_call(token_kernel, out_shape=(shape((tok_rows, D), F32), shape(...  3.78 us
  transfers between devices with their start and end apart: 11, of which 5 were waited for; matrix products, arithmetic and copies ran while one was open for 3% of the time, Pallas kernels for 16%

profile of v2, /device:TPU:1, one launch (start us, length us, event | category | flops | bytes accessed | tf_op | source)
XLA Modules:
  0.0 74.8 jit_solution(8407886281195675777)
XLA Ops:
  1.3 2.0 %state.1 = (f32[192,128]{1,0:T(8,128)}, bf16[8,208,128]{2,1,0:T(8,128)(2,1)}) custom-call(f32[192,128]{1,0:T(8,128)} %cond_ref.2, f32[3,192]{1,0:T(4,128)} %pos_ref.3, f32[1]{0:T(128)S(6)} %copy.19.noise_ref, s32[1,192]{1,0:T(1,128)} %bitcast.5, f32[3,128]{1,0:T(4,128)} %w_pos_ref.2), custom_call_target="tpu_custom_call" | custom-call | tf_op jit(solution)/shard_map/state/pallas_call | solution.py:254
  3.3 7.5 %all-to-all-start = ((bf16[8,208,128]{2,1,0:T(8,128)(2,1)}), bf16[8,208,128]{2,1,0:T(8,128)(2,1)S(1)}, u32[]{:S(2)}, u32[]{:S(2)}) async-start(bf16[8,208,128]{2,1,0:T(8,128)(2,1)} %get-tuple-element.8), calls=%async_computation | async-start | bytes 851968 | tf_op jit(solution)/shard_map/all_to_all | solution.py:250
  10.8 7.8 %bias.1 = bf16[16,272,128]{2,1,0:T(8,128)(2,1)} custom-call(bf16[256,128,128]{2,1,0:T(8,128)(2,1)} %pair_ref.1, bf16[16,128]{1,0:T(8,128)(2,1)} %w_ref.1), custom_call_target="tpu_custom_call" | custom-call | flops 2147483648 | bytes 10485760 | tf_op jit(solution)/shard_map/bias/pallas_call | solution.py:263
  18.6 2.8 %all-to-all-done.mine_ref = bf16[8,208,128]{2,1,0:T(8,128)(2,1)S(1)} async-done(((bf16[8,208,128]{2,1,0:T(8,128)(2,1)}), bf16[8,208,128]{2,1,0:T(8,128)(2,1)S(1)}, u32[]{:S(2)}, u32[]{:S(2)}) %all-to-all-start) | async-done | bytes 426016 | tf_op jit(solution)/shard_map/all_to_all | solution.py:250
  21.4 5.4 %all-to-all-start.1 = ((bf16[16,272,128]{2,1,0:T(8,128)(2,1)}), bf16[16,272,128]{2,1,0:T(8,128)(2,1)S(1)}, u32[]{:S(2)}, u32[]{:S(2)}) async-start(bf16[16,272,128]{2,1,0:T(8,128)(2,1)} %bias.1), calls=%async_computation.1 | async-start | bytes 2228224 | tf_op jit(solution)/shard_map/all_to_all | solution.py:281
  26.8 0.2 collective-permute-start
  27.0 1.8 %constant_dynamic-slice_fusion.1 = (bf16[768,48]{1,0:T(8,128)(2,1)S(1)}, bf16[768,48]{1,0:T(8,128)(2,1)S(1)}, bf16[768,48]{1,0:T(8,128)(2,1)S(1)}, bf16[768,48]{1,0:T(8,128)(2,1)S(1)}) fusion(bf16[768,1536]{1,0:T(8,128)(2,1)} %param.28, s32[]{:T(128)S(6)} %select_n.8, s32[]{:T(128)S(6)} %select_n.9, bf16[768,1536]{1,0:T(8,128)(2,1)} %param.27), kind=kLoop, calls=%fused_computation.16 | loop fusion | bytes 589832 | tf_op jit(solution)/shard_map/dynamic_slice | solution.py:284
  28.8 0.2 fusion.7.w_head_ref
  29.0 0.0 collective-permute-done.other_ref
  29.0 0.0 copy-done.2
  29.0 0.0 copy-done.3
  29.0 0.0 copy-done.6
  29.0 3.8 %token_.1 = (f32[256,768]{1,0:T(8,128)S(1)}, bf16[256,48]{1,0:T(8,128)(2,1)S(1)}, bf16[256,48]{1,0:T(8,128)(2,1)S(1)}, bf16[96,256]{1,0:T(8,128)(2,1)S(1)}) custom-call(bf16[8,208,128]{2,1,0:T(8,128)(2,1)S(1)} %all-to-all-done.mine_ref, bf16[8,208,128]{2,1,0:T(8,128)(2,1)S(1)} %collective-permute-done.other_ref, bf16[128,768]{1,0:T(8,128)(2,1)S(1)} %copy-done.3, ...), custom_call_target="tpu_custom_call" | custom-call | tf_op jit(solution)/shard_map/token/pallas_call | solution.py:298
  32.8 1.7 %collective-permute-start.1 = (bf16[96,256]{1,0:T(8,128)(2,1)S(1)}, bf16[96,256]{1,0:T(8,128)(2,1)S(1)}, u32[]{:S(2)}, u32[]{:S(2)}) collective-permute-start(bf16[96,256]{1,0:T(8,128)(2,1)S(1)} %get-tuple-element.11.refs_0_), channel_id=1, source_target_pairs={{0,16},{16,0},{32,48},{48,32},{64,80},{80,64},{96,112},{112,96},{1... | collective-permute-start | bytes 147464 | tf_op jit(solution)/shard_map/ppermute | solution.py:314
  34.5 3.3 %collective-permute-start.2 = (bf16[96,256]{1,0:T(8,128)(2,1)S(1)}, bf16[96,256]{1,0:T(8,128)(2,1)S(1)}, u32[]{:S(2)}, u32[]{:S(2)}) collective-permute-start(bf16[96,256]{1,0:T(8,128)(2,1)S(1)} %get-tuple-element.11.refs_0_), channel_id=1, source_target_pairs={{0,32},{16,48},{32,0},{48,16},{64,96},{80,112},{96,64},{112,80},{1... | collective-permute-start | bytes 147464 | tf_op jit(solution)/shard_map/ppermute | solution.py:314
  37.8 0.0 collective-permute-start.3
  37.8 0.4 collective-permute-start.4
  38.2 0.5 collective-permute-start.5
  38.7 0.0 collective-permute-done.1.refs_1_
  38.7 4.3 %collective-permute-start.6 = (bf16[96,256]{1,0:T(8,128)(2,1)S(1)}, bf16[96,256]{1,0:T(8,128)(2,1)S(1)}, u32[]{:S(2)}, u32[]{:S(2)}) collective-permute-start(bf16[96,256]{1,0:T(8,128)(2,1)S(1)} %get-tuple-element.11.refs_0_), channel_id=1, source_target_pairs={{0,96},{16,112},{32,64},{48,80},{64,32},{80,48},{96,0},{112,16},{1... | collective-permute-start | bytes 147464 | tf_op jit(solution)/shard_map/ppermute | solution.py:314
  43.0 0.0 collective-permute-done.2.refs_2_
  43.0 0.8 %collective-permute-start.7 = (bf16[96,256]{1,0:T(8,128)(2,1)S(1)}, bf16[96,256]{1,0:T(8,128)(2,1)S(1)}, u32[]{:S(2)}, u32[]{:S(2)}) collective-permute-start(bf16[96,256]{1,0:T(8,128)(2,1)S(1)} %get-tuple-element.11.refs_0_), channel_id=1, source_target_pairs={{0,112},{16,96},{32,80},{48,64},{64,48},{80,32},{96,16},{112,0},{1... | collective-permute-start | bytes 147464 | tf_op jit(solution)/shard_map/ppermute | solution.py:314
  43.8 1.1 %all-to-all-done.1 = bf16[16,272,128]{2,1,0:T(8,128)(2,1)S(1)} async-done(((bf16[16,272,128]{2,1,0:T(8,128)(2,1)}), bf16[16,272,128]{2,1,0:T(8,128)(2,1)S(1)}, u32[]{:S(2)}, u32[]{:S(2)}) %all-to-all-start.1) | async-done | bytes 1114144 | tf_op jit(solution)/shard_map/all_to_all | solution.py:281
  44.9 0.1 convert_element_type.8.bias_ref
  45.0 0.0 collective-permute-done.3.refs_3_
  45.0 0.0 collective-permute-done.4.refs_4_
  45.1 0.0 collective-permute-done.5.refs_5_
  45.1 2.4 %collective-permute-done.6.refs_6_ = bf16[96,256]{1,0:T(8,128)(2,1)S(1)} collective-permute-done((bf16[96,256]{1,0:T(8,128)(2,1)S(1)}, bf16[96,256]{1,0:T(8,128)(2,1)S(1)}, u32[]{:S(2)}, u32[]{:S(2)}) %collective-permute-start.6) | collective-permute-done | bytes 49184 | tf_op jit(solution)/shard_map/ppermute | solution.py:314
  47.5 1.0 %collective-permute-done.7.refs_7_ = bf16[96,256]{1,0:T(8,128)(2,1)S(1)} collective-permute-done((bf16[96,256]{1,0:T(8,128)(2,1)S(1)}, bf16[96,256]{1,0:T(8,128)(2,1)S(1)}, u32[]{:S(2)}, u32[]{:S(2)}) %collective-permute-start.7) | collective-permute-done | bytes 49184 | tf_op jit(solution)/shard_map/ppermute | solution.py:314
  48.5 0.0 copy-start.4
  48.5 0.0 copy-start.5
  48.5 0.0 copy-start.7
  48.5 0.0 copy-start.8
  48.6 0.0 copy-start.9
  48.6 2.0 %attend.1 = bf16[8,48,256]{2,1,0:T(8,128)(2,1)S(1)} custom-call(bf16[256,48]{1,0:T(8,128)(2,1)S(1)} %get-tuple-element.9.query_ref, bf16[256,48]{1,0:T(8,128)(2,1)S(1)} %get-tuple-element.10.gate_ref, f32[16,272,128]{2,1,0:T(8,128)S(1)} %convert_element_type.8.bias_ref, bf16[96,256]{1,0:T(8,128)(2,1)S(1)} %get-tuple-element.11.refs_0_, ...), custom_call_target="tpu_custom_call" | custom-call | flops 20000000000 | bytes 8388608 | tf_op jit(solution)/shard_map/attend/pallas_call | solution.py:316
  50.5 14.1 %all_to_all.15.mine_ref = bf16[8,48,256]{2,1,0:T(8,128)(2,1)S(1)} all-to-all(bf16[8,48,256]{2,1,0:T(8,128)(2,1)S(1)} %attend.1), channel_id=1, replica_groups={{0,2,4,6,8,10,12,14},{1,3,5,7,9,11,13,15},{16,18,20,22,24,26,28,30},{17..., dimensions={0} | all-to-all | bytes 393216 | tf_op jit(solution)/shard_map/all_to_all | solution.py:250
  64.6 4.4 %collective-permute-start.8 = (bf16[8,48,256]{2,1,0:T(8,128)(2,1)S(1)}, bf16[8,48,256]{2,1,0:T(8,128)(2,1)S(1)}, u32[]{:S(2)}, u32[]{:S(2)}) collective-permute-start(bf16[8,48,256]{2,1,0:T(8,128)(2,1)S(1)} %all_to_all.15.mine_ref), channel_id=1, source_target_pairs={{0,1},{1,0},{2,3},{3,2},{4,5},{5,4},{6,7},{7,6},{8,9},{9,8},{10,11... | collective-permute-start | bytes 589832 | tf_op jit(solution)/shard_map/ppermute | solution.py:251
  69.1 1.1 %collective-permute-done.8.other_ref = bf16[8,48,256]{2,1,0:T(8,128)(2,1)S(1)} collective-permute-done((bf16[8,48,256]{2,1,0:T(8,128)(2,1)S(1)}, bf16[8,48,256]{2,1,0:T(8,128)(2,1)S(1)}, u32[]{:S(2)}, u32[]{:S(2)}) %collective-permute-start.8) | collective-permute-done | bytes 196640 | tf_op jit(solution)/shard_map/ppermute | solution.py:251
  70.1 0.0 slice-done
  70.1 0.0 slice-done.1
  70.1 0.0 copy-done
  70.1 0.0 copy-done.1
  70.2 0.0 copy-done.4
  70.2 0.0 copy-done.5
  70.2 0.0 copy-done.7
  70.2 0.0 copy-done.8
  70.2 0.0 copy-done.9
  70.2 4.6 %close.1 = (f32[3,192]{1,0:T(4,128)}, f32[256,768]{1,0:T(8,128)}) custom-call(bf16[8,48,256]{2,1,0:T(8,128)(2,1)S(1)} %all_to_all.15.mine_ref, bf16[8,48,256]{2,1,0:T(8,128)(2,1)S(1)} %collective-permute-done.8.other_ref, bf16[8,2,48,768]{3,2,1,0:T(8,128)(2,1)S(1)} %bitcast.4, f32[256,768]{1,0:T(8,128)S(1)} %get-tuple-element.12.start_ref, ...), custom_call_target="tpu_custom_call" | custom-call | tf_op jit(solution)/shard_map/close/pallas_call | solution.py:329
  (8 shorter events, 0.0 us)
Async XLA Ops:
  3.3 18.1 %all-to-all-start = ((bf16[8,208,128]{2,1,0:T(8,128)(2,1)}), bf16[8,208,128]{2,1,0:T(8,128)(2,1)S(1)}, u32[]{:S(2)}, u32[]{:S(2)}) async-start(bf16[8,208,128]{2,1,0:T(8,128)(2,1)} %get-tuple-element.8), calls=%async_computation | async-start | bytes 851968 | tf_op jit(solution)/shard_map/all_to_all | solution.py:250
  21.4 23.5 %all-to-all-start.1 = ((bf16[16,272,128]{2,1,0:T(8,128)(2,1)}), bf16[16,272,128]{2,1,0:T(8,128)(2,1)S(1)}, u32[]{:S(2)}, u32[]{:S(2)}) async-start(bf16[16,272,128]{2,1,0:T(8,128)(2,1)} %bias.1), calls=%async_computation.1 | async-start | bytes 2228224 | tf_op jit(solution)/shard_map/all_to_all | solution.py:281
  26.8 2.1 %collective-permute-start = (bf16[8,208,128]{2,1,0:T(8,128)(2,1)S(1)}, bf16[8,208,128]{2,1,0:T(8,128)(2,1)S(1)}, u32[]{:S(2)}, u32[]{:S(2)}) collective-permute-start(bf16[8,208,128]{2,1,0:T(8,128)(2,1)S(1)} %all-to-all-done.mine_ref), channel_id=1, source_target_pairs={{0,1},{1,0},{2,3},{3,2},{4,5},{5,4},{6,7},{7,6},{8,9},{9,8},{10,11... | collective-permute-start | bytes 1277960 | tf_op jit(solution)/shard_map/ppermute | solution.py:251
  27.0 2.0 %copy-start.2 = (f32[256,768]{1,0:T(8,128)S(1)}, f32[256,768]{1,0:T(8,128)}, u32[]{:S(2)}) copy-start(f32[256,768]{1,0:T(8,128)} %cond_ref.3) | copy-start | bytes 2359300
  27.0 2.0 %copy-start.3 = (bf16[128,768]{1,0:T(8,128)(2,1)S(1)}, bf16[128,768]{1,0:T(8,128)(2,1)}, u32[]{:S(2)}) copy-start(bf16[128,768]{1,0:T(8,128)(2,1)} %w_atom_ref.1) | copy-start | bytes 589828
  27.0 2.0 %copy-start.6 = (f32[3,768]{1,0:T(4,128)S(1)}, f32[3,768]{1,0:T(4,128)}, u32[]{:S(2)}) copy-start(f32[3,768]{1,0:T(4,128)} %gains_ref.3) | copy-start | bytes 27652
  32.8 5.9 %collective-permute-start.1 = (bf16[96,256]{1,0:T(8,128)(2,1)S(1)}, bf16[96,256]{1,0:T(8,128)(2,1)S(1)}, u32[]{:S(2)}, u32[]{:S(2)}) collective-permute-start(bf16[96,256]{1,0:T(8,128)(2,1)S(1)} %get-tuple-element.11.refs_0_), channel_id=1, source_target_pairs={{0,16},{16,0},{32,48},{48,32},{64,80},{80,64},{96,112},{112,96},{1... | collective-permute-start | bytes 147464 | tf_op jit(solution)/shard_map/ppermute | solution.py:314
  34.5 8.5 %collective-permute-start.2 = (bf16[96,256]{1,0:T(8,128)(2,1)S(1)}, bf16[96,256]{1,0:T(8,128)(2,1)S(1)}, u32[]{:S(2)}, u32[]{:S(2)}) collective-permute-start(bf16[96,256]{1,0:T(8,128)(2,1)S(1)} %get-tuple-element.11.refs_0_), channel_id=1, source_target_pairs={{0,32},{16,48},{32,0},{48,16},{64,96},{80,112},{96,64},{112,80},{1... | collective-permute-start | bytes 147464 | tf_op jit(solution)/shard_map/ppermute | solution.py:314
  37.8 7.2 %collective-permute-start.3 = (bf16[96,256]{1,0:T(8,128)(2,1)S(1)}, bf16[96,256]{1,0:T(8,128)(2,1)S(1)}, u32[]{:S(2)}, u32[]{:S(2)}) collective-permute-start(bf16[96,256]{1,0:T(8,128)(2,1)S(1)} %get-tuple-element.11.refs_0_), channel_id=1, source_target_pairs={{0,48},{16,32},{32,16},{48,0},{64,112},{80,96},{96,80},{112,64},{1... | collective-permute-start | bytes 147464 | tf_op jit(solution)/shard_map/ppermute | solution.py:314
  37.8 7.2 %collective-permute-start.4 = (bf16[96,256]{1,0:T(8,128)(2,1)S(1)}, bf16[96,256]{1,0:T(8,128)(2,1)S(1)}, u32[]{:S(2)}, u32[]{:S(2)}) collective-permute-start(bf16[96,256]{1,0:T(8,128)(2,1)S(1)} %get-tuple-element.11.refs_0_), channel_id=1, source_target_pairs={{0,64},{16,80},{32,96},{48,112},{64,0},{80,16},{96,32},{112,48},{1... | collective-permute-start | bytes 147464 | tf_op jit(solution)/shard_map/ppermute | solution.py:314
  38.2 6.8 %collective-permute-start.5 = (bf16[96,256]{1,0:T(8,128)(2,1)S(1)}, bf16[96,256]{1,0:T(8,128)(2,1)S(1)}, u32[]{:S(2)}, u32[]{:S(2)}) collective-permute-start(bf16[96,256]{1,0:T(8,128)(2,1)S(1)} %get-tuple-element.11.refs_0_), channel_id=1, source_target_pairs={{0,80},{16,64},{32,112},{48,96},{64,16},{80,0},{96,48},{112,32},{1... | collective-permute-start | bytes 147464 | tf_op jit(solution)/shard_map/ppermute | solution.py:314
  38.7 8.8 %collective-permute-start.6 = (bf16[96,256]{1,0:T(8,128)(2,1)S(1)}, bf16[96,256]{1,0:T(8,128)(2,1)S(1)}, u32[]{:S(2)}, u32[]{:S(2)}) collective-permute-start(bf16[96,256]{1,0:T(8,128)(2,1)S(1)} %get-tuple-element.11.refs_0_), channel_id=1, source_target_pairs={{0,96},{16,112},{32,64},{48,80},{64,32},{80,48},{96,0},{112,16},{1... | collective-permute-start | bytes 147464 | tf_op jit(solution)/shard_map/ppermute | solution.py:314
  43.0 5.5 %collective-permute-start.7 = (bf16[96,256]{1,0:T(8,128)(2,1)S(1)}, bf16[96,256]{1,0:T(8,128)(2,1)S(1)}, u32[]{:S(2)}, u32[]{:S(2)}) collective-permute-start(bf16[96,256]{1,0:T(8,128)(2,1)S(1)} %get-tuple-element.11.refs_0_), channel_id=1, source_target_pairs={{0,112},{16,96},{32,80},{48,64},{64,48},{80,32},{96,16},{112,0},{1... | collective-permute-start | bytes 147464 | tf_op jit(solution)/shard_map/ppermute | solution.py:314
  48.5 21.6 %slice-start = ((s8[4718592]{0:T(1024)(128)(4,1)}), s8[4194304]{0:T(1024)(128)(4,1)S(1)}, s32[]{:S(2)}) async-start(s8[4718592]{0:T(1024)(128)(4,1)} %bitcast.2), calls=%async_computation.3 | async-start | bytes 8388608
  48.5 21.6 %slice-start.1 = ((s8[4718592]{0:T(1024)(128)(4,1)}), s8[524288]{0:T(1024)(128)(4,1)S(1)}, s32[]{:S(2)}) async-start(s8[4718592]{0:T(1024)(128)(4,1)} %bitcast.2), calls=%async_computation.4 | async-start | bytes 1048576
  48.5 21.6 %copy-start = (bf16[1536,768]{1,0:T(8,128)(2,1)S(1)}, bf16[1536,768]{1,0:T(8,128)(2,1)}, u32[]{:S(2)}) copy-start(bf16[1536,768]{1,0:T(8,128)(2,1)} %w_down_ref.1) | copy-start | bytes 7077892
  48.5 21.6 %copy-start.1 = (bf16[768,768]{1,0:T(8,128)(2,1)S(1)}, bf16[768,768]{1,0:T(8,128)(2,1)}, u32[]{:S(2)}) copy-start(bf16[768,768]{1,0:T(8,128)(2,1)} %param.29) | copy-start | bytes 3538948
  48.5 21.6 %copy-start.4 = (bf16[768,128]{1,0:T(8,128)(2,1)S(1)}, bf16[768,128]{1,0:T(8,128)(2,1)}, u32[]{:S(2)}) copy-start(bf16[768,128]{1,0:T(8,128)(2,1)} %w_tok_ref.1) | copy-start | bytes 589828
  48.5 21.6 %copy-start.5 = (f32[192,128]{1,0:T(8,128)S(1)}, f32[192,128]{1,0:T(8,128)}, u32[]{:S(2)}) copy-start(f32[192,128]{1,0:T(8,128)} %get-tuple-element.13.state_ref) | copy-start | bytes 294916
  48.5 21.6 %copy-start.7 = (f32[3,192]{1,0:T(4,128)S(1)}, f32[3,192]{1,0:T(4,128)}, u32[]{:S(2)}) copy-start(f32[3,192]{1,0:T(4,128)} %pos_ref.3) | copy-start | bytes 6916
  48.5 21.6 %copy-start.8 = (s32[192]{0:T(256)S(1)}, s32[192]{0:T(256)}, u32[]{:S(2)}) copy-start(s32[192]{0:T(256)} %param.20) | copy-start | bytes 2308
  48.6 21.6 %copy-start.9 = (bf16[3,128]{1,0:T(4,128)(2,1)S(1)}, bf16[3,128]{1,0:T(4,128)(2,1)}, u32[]{:S(2)}) copy-start(bf16[3,128]{1,0:T(4,128)(2,1)} %w_pos_ref.3) | copy-start | bytes 2308
  64.6 5.5 %collective-permute-start.8 = (bf16[8,48,256]{2,1,0:T(8,128)(2,1)S(1)}, bf16[8,48,256]{2,1,0:T(8,128)(2,1)S(1)}, u32[]{:S(2)}, u32[]{:S(2)}) collective-permute-start(bf16[8,48,256]{2,1,0:T(8,128)(2,1)S(1)} %all_to_all.15.mine_ref), channel_id=1, source_target_pairs={{0,1},{1,0},{2,3},{3,2},{4,5},{5,4},{6,7},{7,6},{8,9},{9,8},{10,11... | collective-permute-start | bytes 589832 | tf_op jit(solution)/shard_map/ppermute | solution.py:251

commit v3 on v2

--- a/solution.py
+++ b/solution.py
@@ -10,6 +10,7 @@
 D = 768
 HEADS = 16
 HEAD_DIM = D // HEADS
+DUO = 2 * HEAD_DIM
 BF = jnp.bfloat16
 F32 = jnp.float32
 MIB = 1 << 20
@@ -26,17 +27,23 @@
     return centered * lax.rsqrt(variance + 1e-05) * gain_row
 
 
+def three(values):
+    high = values.astype(BF).astype(F32)
+    rest = values - high
+    middle = rest.astype(BF).astype(F32)
+    return high, middle, rest - middle
+
+
 def whole(n):
     return [pl.BlockSpec(memory_space=pltpu.VMEM)] * n
 
 
 def state_kernel(tok_rows, cond_ref, pos_ref, noise_ref, ids_ref, w_pos_ref, state_ref, packed_ref):
     atoms = cond_ref.shape[0]
-    sigma = noise_ref[0]
-    sigma = jnp.full((1, 128), sigma, F32)
+    sigma = noise_ref[...]
     inv = 1.0 / jnp.sqrt(sigma * sigma + 1.0)
     pos = jnp.transpose(
-        jnp.concatenate([pos_ref[...] * inv[:, :1], jnp.zeros((5, atoms), F32)], axis=0)
+        jnp.concatenate([pos_ref[...] * inv, jnp.zeros((5, atoms), F32)], axis=0)
     )
     state = cond_ref[...] + pos[:, 0:1] * w_pos_ref[0:1, :]
     state = state + pos[:, 1:2] * w_pos_ref[1:2, :]
@@ -57,6 +64,7 @@
     rows = pair_vmem.shape[1]
     half = rows // 2
     parts = tok_rows // rows
+    span = tok_rows + 16
 
     def arrival(part):
         return pltpu.make_async_copy(
@@ -94,14 +102,12 @@
         for h in range(HEADS):
             lines = held[at + h * rows : at + (h + 1) * rows, :]
             top = jnp.max(lines, axis=1, keepdims=True)
-            out_ref[h, part * rows : (part + 1) * rows, :] = (lines - top).astype(BF)
+            first = h % 2 * span + part * rows
+            out_ref[h // 2, first : first + rows, :] = (lines - top).astype(BF)
             top_of = jnp.where(lanes == h, top, top_of)
         tops[part * rows : (part + 1) * rows, :] = top_of
     top = jnp.transpose(tops[...])[:HEADS]
-    high = top.astype(BF).astype(F32)
-    rest = top - high
-    middle = rest.astype(BF).astype(F32)
-    low = rest - middle
+    high, middle, low = three(top)
     pad = jnp.zeros((16 - 3 * tok_rows // 128, 128), F32)
     for h in range(HEADS):
         lines = [
@@ -109,7 +115,8 @@
             for term in (high, middle, low)
             for r in range(0, tok_rows, 128)
         ]
-        out_ref[h, tok_rows:, :] = jnp.concatenate([*lines, pad], axis=0).astype(BF)
+        first = h % 2 * span + tok_rows
+        out_ref[h // 2, first : first + 16, :] = jnp.concatenate([*lines, pad], axis=0).astype(BF)
 
 
 def token_kernel(
@@ -134,61 +141,93 @@
     start_ref[...] = start
     normed = norm_rows(start, gains_ref[0:1, :]).astype(BF)
     projected = dot(normed, w_head_ref[...])
-    query_ref[...] = projected[:, :HEAD_DIM].astype(BF)
-    gate_ref[...] = jax.nn.sigmoid(projected[:, 128 : 128 + HEAD_DIM]).astype(BF)
+    query_ref[...] = projected[:, :DUO].astype(BF)
+    gate_ref[...] = jax.nn.sigmoid(projected[:, 128 : 128 + DUO]).astype(BF)
     kv = jnp.transpose(projected[:, 256:512])
-    kv = jnp.concatenate([kv[:HEAD_DIM], kv[128 : 128 + HEAD_DIM]], axis=0).astype(BF)
+    kv = jnp.concatenate([kv[:DUO], kv[128 : 128 + DUO]], axis=0).astype(BF)
     kv_ref[...] = kv
 
 
 def attend_kernel(query_ref, gate_ref, bias_ref, *refs):
     kv_refs, mixed_ref = refs[:-1], refs[-1]
-    groups = len(kv_refs)
+    ring = len(kv_refs)
     keys = kv_refs[0].shape[1]
     tok_rows = query_ref.shape[0]
-    me = lax.axis_index("aa")
+    span = tok_rows + 16
+    place = lax.rem(lax.axis_index("aa"), ring)
     per = keys // bias_ref.shape[2]
     order = [
-        lax.bitwise_xor(me, g) * per + b for g in range(groups) for b in range(per)
+        lax.rem(place - by + ring, ring) * per + b for by in range(ring) for b in range(per)
     ]
-    tops = []
-    for at in order:
-        tail = bias_ref[at, tok_rows:, :].astype(F32)
-        n = tok_rows // 128
-        lines = tail[:n] + tail[n : 2 * n] + tail[2 * n : 3 * n]
-        tops.append(jnp.concatenate([lines[i : i + 1] for i in range(n)], axis=1))
-    tops = jnp.transpose(jnp.concatenate(tops, axis=0))
-    step = 64
-    parts = []
-    for r in range(0, tok_rows, step):
-        query = query_ref[r : r + step, :]
-        scores = jnp.concatenate(
-            [dot(query, ref[:HEAD_DIM, :]) for ref in kv_refs], axis=1
-        ) * HEAD_DIM ** (-0.5)
-        bias = jnp.concatenate(
-            [
-                bias_ref[at, r : r + step, :].astype(F32) + tops[r : r + step, i : i + 1]
-                for i, at in enumerate(order)
-            ],
-            axis=1,
-        )
-        scores = scores + bias
-        top = jnp.max(scores, axis=1, keepdims=True)
-        weights = jnp.exp(scores - top)
-        total = jnp.sum(weights, axis=1, keepdims=True)
-        rounded = weights.astype(BF)
-        out = jnp.zeros((step, HEAD_DIM), F32)
-        for g in range(groups):
-            out += dot(
-                rounded[:, g * keys : (g + 1) * keys], kv_refs[g][HEAD_DIM:, :], ((1,), (1,))
+    n = tok_rows // 128
+    step = 128
+    outs, stats = [], []
+    for j in range(2):
+        mine = slice(j * HEAD_DIM, (j + 1) * HEAD_DIM)
+        tops = []
+        for at in order:
+            tail = bias_ref[at, j * span + tok_rows : (j + 1) * span, :]
+            lines = tail[:n] + tail[n : 2 * n] + tail[2 * n : 3 * n]
+            tops.append(jnp.concatenate([lines[i : i + 1] for i in range(n)], axis=1))
+        tops = jnp.transpose(jnp.concatenate(tops, axis=0))
+        parts, largest, totals = [], [], []
+        for r in range(0, tok_rows, step):
+            query = query_ref[r : r + step, mine]
+            scores = jnp.concatenate(
+                [dot(query, ref[mine, :]) for ref in kv_refs], axis=1
+            ) * HEAD_DIM ** (-0.5)
+            first = j * span + r
+            bias = jnp.concatenate(
+                [
+                    bias_ref[at, first : first + step, :] + tops[r : r + step, i : i + 1]
+                    for i, at in enumerate(order)
+                ],
+                axis=1,
             )
-        parts.append(out / total)
-    attended = jnp.concatenate(parts, axis=0)
-    mixed = attended * gate_ref[...].astype(F32)
-    mixed = jnp.concatenate([mixed, jnp.zeros((tok_rows, 128 - HEAD_DIM), F32)], axis=1)
-    turned = jnp.transpose(mixed)[:HEAD_DIM].astype(BF)
+            scores = scores + bias
+            top = jnp.max(scores, axis=1, keepdims=True)
+            weights = jnp.exp(scores - top)
+            totals.append(jnp.sum(weights, axis=1, keepdims=True))
+            largest.append(top)
+            rounded = weights.astype(BF)
+            out = jnp.zeros((step, HEAD_DIM), F32)
+            for g, ref in enumerate(kv_refs):
+                values = ref[DUO + j * HEAD_DIM : DUO + (j + 1) * HEAD_DIM, :]
+                out += dot(rounded[:, g * keys : (g + 1) * keys], values, ((1,), (1,)))
+            parts.append(out)
+        outs.append(jnp.concatenate(parts, axis=0))
+        stats += [jnp.concatenate(largest, axis=0), jnp.concatenate(totals, axis=0)]
+    gated = jnp.concatenate(outs, axis=1) * gate_ref[...].astype(F32)
+    spare = jnp.zeros((tok_rows, 128 - DUO - len(stats)), F32)
+    turned = jnp.transpose(jnp.concatenate([gated, *stats, spare], axis=1))
+    terms = three(turned[DUO : DUO + 4])
+    sent = jnp.concatenate([turned[:DUO], *terms, jnp.zeros((4, tok_rows), F32)], axis=0)
+    sent = sent.astype(BF)
     for piece in range(mixed_ref.shape[0]):
-        mixed_ref[piece] = turned
+        mixed_ref[piece] = sent
+
+
+def joined(ref):
+    half = ref.shape[0] // 2
+    mixed = []
+    for x in range(half):
+        pair = (ref[x], ref[half + x])
+        stats = []
+        for part in pair:
+            tail = part[DUO:].astype(F32)
+            stats.append(tail[0:4] + tail[4:8] + tail[8:12])
+        for j in range(2):
+            tops = [st[2 * j : 2 * j + 1] for st in stats]
+            overall = jnp.maximum(*tops)
+            factors = [jnp.exp(top - overall) for top in tops]
+            total = sum(f * st[2 * j + 1 : 2 * j + 2] for f, st in zip(factors, stats))
+            mixed.append(
+                sum(
+                    part[j * HEAD_DIM : (j + 1) * HEAD_DIM].astype(F32) * (f / total)
+                    for part, f in zip(pair, factors)
+                ).astype(BF)
+            )
+    return jnp.concatenate(mixed, axis=0)
 
 
 def close_kernel(
@@ -199,11 +238,9 @@
     core = lax.rem(lax.axis_index("ba"), 2)
     tok_rows = start_ref.shape[0]
     pieces = mine_ref.shape[0]
-    width = pieces * HEAD_DIM
-    mine = mine_ref[...].reshape(width, tok_rows)
-    other = other_ref[...].reshape(width, tok_rows)
-    added = dot(mine, w_out_ref[:, core].reshape(width, D), ((0,), (0,)))
-    added += dot(other, w_out_ref[:, 1 - core].reshape(width, D), ((0,), (0,)))
+    depth = pieces * HEAD_DIM
+    added = dot(joined(mine_ref), w_out_ref[:, core].reshape(depth, D), ((0,), (0,)))
+    added += dot(joined(other_ref), w_out_ref[:, 1 - core].reshape(depth, D), ((0,), (0,)))
     mid = start_ref[...] + added
     normed = norm_rows(mid, gains_ref[1:2, :]).astype(BF)
     hidden = w_down_ref.shape[0]
@@ -221,9 +258,9 @@
     final = state_ref[...] + dot(chosen, token_atom, ((0,), (0,)))
     normed = norm_rows(final, 1.0).astype(BF)
     update = dot(w_pos_ref[...], normed, ((1,), (1,)))
-    sigma = jnp.full((1, 128), noise_ref[0], F32)
-    inv = (1.0 / jnp.sqrt(sigma * sigma + 1.0))[:, :1]
-    denoised_ref[...] = pos_ref[...] * (inv * inv) + update * (sigma[:, :1] * inv)
+    sigma = noise_ref[...]
+    inv = 1.0 / jnp.sqrt(sigma * sigma + 1.0)
+    denoised_ref[...] = pos_ref[...] * (inv * inv) + update * (sigma * inv)
 
 
 def shape(dims, dtype):
@@ -241,28 +278,29 @@
     size = lax.axis_size("ba")
     peers = size // 2
     groups = lax.axis_size("aa")
-    head = lax.axis_index("ba")
+    duo = lax.rem(lax.axis_index("ba"), peers)
     same_core = [list(range(core, size, 2)) for core in range(2)]
+    halves = [list(range(peers)), list(range(peers, size))]
     siblings = [(i, i ^ 1) for i in range(size)]
-    smem = pl.BlockSpec(memory_space=pltpu.SMEM)
 
     def gathered(copies):
         mine = lax.all_to_all(copies, "ba", 0, 0, tiled=True, axis_index_groups=same_core)
         return mine, lax.ppermute(mine, "ba", siblings)
 
     ids = atom_token[None, :]
+    noise = noise_level[:, None]
     state, packed = pl.pallas_call(
         functools.partial(state_kernel, tok_rows),
         out_shape=(shape((atoms, chans), F32), shape((peers, atoms + 16, chans), BF)),
-        in_specs=[*whole(2), smem, *whole(2)],
+        in_specs=whole(5),
         out_specs=tuple(whole(2)),
         name="state",
-    )(atom_cond, noisy_pos, noise_level, ids, w_pos)
+    )(atom_cond, noisy_pos, noise, ids, w_pos)
 
     block = 32
     bias = pl.pallas_call(
         bias_kernel,
-        out_shape=shape((HEADS, tok_rows + 16, cols), BF),
+        out_shape=shape((peers, 2 * (tok_rows + 16), cols), BF),
         in_specs=[pl.BlockSpec(memory_space=pl.ANY), *whole(1)],
         out_specs=whole(1)[0],
         scratch_shapes=[
@@ -278,18 +316,20 @@
         ),
         name="bias",
     )(pair, pair_bias_weight)
-    bias = lax.all_to_all(bias, "ba", 0, 0, tiled=True).astype(F32)
+    bias = lax.all_to_all(
+        bias, "ba", 0, 0, tiled=True, axis_index_groups=halves
+    ).astype(F32)
 
     def column(w, at):
-        part = lax.dynamic_slice_in_dim(w, at, HEAD_DIM, 1)
-        return jnp.pad(part, ((0, 0), (0, 128 - HEAD_DIM)))
+        part = lax.dynamic_slice_in_dim(w, at, DUO, 1)
+        return jnp.pad(part, ((0, 0), (0, 128 - DUO)))
 
     w_head = jnp.concatenate(
         [
-            column(w_query_gate, head * HEAD_DIM),
-            column(w_query_gate, D + head * HEAD_DIM),
-            column(w_key_value, head * HEAD_DIM),
-            column(w_key_value, D + head * HEAD_DIM),
+            column(w_query_gate, duo * DUO),
+            column(w_query_gate, D + duo * DUO),
+            column(w_key_value, duo * DUO),
+            column(w_key_value, D + duo * DUO),
         ],
         axis=1,
     )
@@ -299,9 +339,9 @@
         token_kernel,
         out_shape=(
             shape((tok_rows, D), F32),
-            shape((tok_rows, HEAD_DIM), BF),
-            shape((tok_rows, HEAD_DIM), BF),
-            shape((2 * HEAD_DIM, tok_rows), BF),
+            shape((tok_rows, DUO), BF),
+            shape((tok_rows, DUO), BF),
+            shape((2 * DUO, tok_rows), BF),
         ),
         in_specs=whole(6),
         out_specs=tuple(whole(4)),
@@ -309,14 +349,23 @@
         compiler_params=pltpu.CompilerParams(vmem_limit_bytes=24 * MIB),
         name="token",
     )(mine, other, w_atom_token, token_cond, gains, w_head)
-    spread = [kv]
-    for far in range(1, groups):
-        spread.append(lax.ppermute(kv, "aa", [(i, i ^ far) for i in range(groups)]))
+    ring = groups // 2
+    spread = []
+    for by in range(ring):
+        moves = []
+        for low in range(2):
+            for high in range(2):
+                for z in range(ring):
+                    for w in range(peers):
+                        source = (high * ring + z) * size + low * peers + w
+                        target = (low * ring + (z + by) % ring) * size + high * peers + w
+                        moves.append((source, target))
+        spread.append(lax.ppermute(kv, ("aa", "ba"), moves))
 
     mixed = pl.pallas_call(
         attend_kernel,
-        out_shape=shape((peers, HEAD_DIM, tok_rows), BF),
-        in_specs=whole(3 + groups),
+        out_shape=shape((peers, DUO + 16, tok_rows), BF),
+        in_specs=whole(3 + ring),
         out_specs=whole(1)[0],
         compiler_params=pltpu.CompilerParams(vmem_limit_bytes=16 * MIB),
         cost_estimate=pl.CostEstimate(
@@ -329,13 +378,13 @@
     return pl.pallas_call(
         close_kernel,
         out_shape=(shape((3, atoms), F32), shape((tok_rows, D), F32)),
-        in_specs=[*whole(12), smem],
+        in_specs=whole(13),
         out_specs=tuple(whole(2)),
         compiler_params=pltpu.CompilerParams(vmem_limit_bytes=24 * MIB),
         name="close",
     )(
-        mine, other, w_attn_out.reshape(peers, 2, HEAD_DIM, D), start, gains, w_up, w_down,
-        w_token_atom, state, ids, w_pos_out, noisy_pos, noise_level,
+        mine, other, w_attn_out.reshape(peers // 2, 2, DUO, D), start, gains, w_up, w_down,
+        w_token_atom, state, ids, w_pos_out, noisy_pos, noise,
     )
 
 

time: 75.2 us -> 72.1 us (0.959)
  starting transfers between devices: 28.5 us -> 21.5 us
  blocking collectives: 14.1 us -> 17.2 us
  Pallas kernels: 20.2 us -> 21.3 us
    ppermute x7 -> x4, starting transfers between devices: 11 us -> 6.41 us  [on_device(): spread.append(lax.ppermute(kv, ('aa', 'ba'), moves))]
    all_to_all x1, blocking collectives: 14.1 us -> 17.2 us  [gathered(): lax.all_to_all(copies, 'ba', 0, 0, tiled=True, axis_index_groups=same_core)]
    ppermute x7 -> x4, waiting for transfers between devices: 3.44 us -> 0.39 us  [on_device(): spread.append(lax.ppermute(kv, ('aa', 'ba'), moves))]
    all_to_all x1, waiting for transfers between devices: 1.11 us -> 3.42 us  [on_device(): lax.all_to_all(bias, 'ba', 0, 0, tiled=True, axis_index_groups=halves)]
    ppermute x2, starting transfers between devices: 4.61 us -> 3.35 us  [gathered(): return (mine, lax.ppermute(mine, 'ba', siblings))]
    all_to_all x1, starting transfers between devices: 5.4 us -> 4.31 us  [on_device(): lax.all_to_all(bias, 'ba', 0, 0, tiled=True, axis_index_groups=halves)]
    pallas_call x2, Pallas kernels: 9.8 us -> 10.8 us  [the longest x1 7.85 us: on_device(): pl.pallas_call(bias_kernel, out_shape=shape((peers, 2 * (tok_rows + 16),...]
  transfers between devices with their start and end apart: 11 -> 8, of which waited for: 5 -> 4; matrix products, arithmetic and copies ran while one was open for 3% -> 3% of each run, Pallas kernels for 16% -> 16%
where the time goes in v3:
time: 72.1 us; the launch traced here: 71.7 us
  starting transfers between devices  21.5 us (30%)
  Pallas kernels  21.3 us (30%)
  blocking collectives  17.2 us (24%)
  waiting for transfers between devices  8.04 us (11%)
  local copies, waits for them, and re-layouts  1.81 us (3%)
  between operations  1.48 us (2%)
    all_to_all x1, blocking collectives, gathered(): lax.all_to_all(copies, 'ba', 0, 0, tiled=True, axis_index_groups=same_core)  17.2 us
    pallas_call x1, Pallas kernels, on_device(): pl.pallas_call(bias_kernel, out_shape=shape((peers, 2 * (tok_rows + 16),...  7.85 us
    all_to_all x1, starting transfers between devices, gathered(): lax.all_to_all(copies, 'ba', 0, 0, tiled=True, axis_index_groups=same_core)  7.48 us
    ppermute x4, starting transfers between devices, on_device(): spread.append(lax.ppermute(kv, ('aa', 'ba'), moves))  6.41 us
    pallas_call x1, Pallas kernels, on_device(): pl.pallas_call(close_kernel, out_shape=(shape((3, atoms), F32), shape((to...  4.63 us
    all_to_all x1, starting transfers between devices, on_device(): lax.all_to_all(bias, 'ba', 0, 0, tiled=True, axis_index_groups=halves)  4.31 us
    pallas_call x1, Pallas kernels, on_device(): pl.pallas_call(token_kernel, out_shape=(shape((tok_rows, D), F32), shape(...  3.79 us
    all_to_all x1, waiting for transfers between devices, on_device(): lax.all_to_all(bias, 'ba', 0, 0, tiled=True, axis_index_groups=halves)  3.42 us
  transfers between devices with their start and end apart: 8, of which 4 were waited for; matrix products, arithmetic and copies ran while one was open for 3% of the time, Pallas kernels for 16%

profile of v3, /device:TPU:1, one launch (start us, length us, event | category | flops | bytes accessed | tf_op | source)
XLA Modules:
  0.0 71.7 jit_solution(11296709936349715197)
XLA Ops:
  1.3 2.0 %state.1 = (f32[192,128]{1,0:T(8,128)}, bf16[8,208,128]{2,1,0:T(8,128)(2,1)}) custom-call(f32[192,128]{1,0:T(8,128)} %cond_ref.2, f32[3,192]{1,0:T(4,128)} %pos_ref.3, f32[1,1]{1,0:T(1,128)} %bitcast.3.noise_ref, s32[1,192]{1,0:T(1,128)} %bitcast.8, f32[3,128]{1,0:T(4,128)} %w_pos_ref.2), custom_call_target="tpu_custom_call" | custom-call | tf_op jit(solution)/shard_map/state/pallas_call | solution.py:292
  3.3 7.5 %all-to-all-start = ((bf16[8,208,128]{2,1,0:T(8,128)(2,1)}), bf16[8,208,128]{2,1,0:T(8,128)(2,1)S(1)}, u32[]{:S(2)}, u32[]{:S(2)}) async-start(bf16[8,208,128]{2,1,0:T(8,128)(2,1)} %get-tuple-element.8), calls=%async_computation | async-start | bytes 851968 | tf_op jit(solution)/shard_map/all_to_all | solution.py:287
  10.8 7.9 %bias.1 = bf16[8,544,128]{2,1,0:T(8,128)(2,1)} custom-call(bf16[256,128,128]{2,1,0:T(8,128)(2,1)} %pair_ref.1, bf16[16,128]{1,0:T(8,128)(2,1)} %w_ref.1), custom_call_target="tpu_custom_call" | custom-call | flops 2147483648 | bytes 10485760 | tf_op jit(solution)/shard_map/bias/pallas_call | solution.py:301
  18.7 2.8 %all-to-all-done.mine_ref = bf16[8,208,128]{2,1,0:T(8,128)(2,1)S(1)} async-done(((bf16[8,208,128]{2,1,0:T(8,128)(2,1)}), bf16[8,208,128]{2,1,0:T(8,128)(2,1)S(1)}, u32[]{:S(2)}, u32[]{:S(2)}) %all-to-all-start) | async-done | bytes 426016 | tf_op jit(solution)/shard_map/all_to_all | solution.py:287
  21.4 4.3 %all-to-all-start.1 = ((bf16[8,544,128]{2,1,0:T(8,128)(2,1)}), bf16[8,544,128]{2,1,0:T(8,128)(2,1)S(1)}, u32[]{:S(2)}, u32[]{:S(2)}) async-start(bf16[8,544,128]{2,1,0:T(8,128)(2,1)} %bias.1), calls=%async_computation.1 | async-start | bytes 2228224 | tf_op jit(solution)/shard_map/all_to_all | solution.py:319
  25.8 0.2 collective-permute-start
  25.9 0.0 copy-start.2
  25.9 0.0 copy-start.3
  25.9 1.8 %constant_dynamic-slice_fusion.1 = (bf16[768,96]{1,0:T(8,128)(2,1)S(1)}, bf16[768,96]{1,0:T(8,128)(2,1)S(1)}, bf16[768,96]{1,0:T(8,128)(2,1)S(1)}, bf16[768,96]{1,0:T(8,128)(2,1)S(1)}) fusion(bf16[768,1536]{1,0:T(8,128)(2,1)} %param.28, s32[]{:T(128)S(6)} %select_n.8, s32[]{:T(128)S(6)} %select_n.9, bf16[768,1536]{1,0:T(8,128)(2,1)} %param.27), kind=kLoop, calls=%fused_computation.16 | loop fusion | bytes 1179656 | tf_op jit(solution)/shard_map/dynamic_slice | solution.py:324
  27.7 0.2 fusion.7.w_head_ref
  27.9 0.0 collective-permute-done.other_ref
  27.9 0.0 copy-done.2
  27.9 0.0 copy-done.3
  27.9 0.0 copy-done.6
  27.9 3.8 %token_.1 = (f32[256,768]{1,0:T(8,128)S(1)}, bf16[256,96]{1,0:T(8,128)(2,1)S(1)}, bf16[256,96]{1,0:T(8,128)(2,1)S(1)}, bf16[192,256]{1,0:T(8,128)(2,1)S(1)}) custom-call(bf16[8,208,128]{2,1,0:T(8,128)(2,1)S(1)} %all-to-all-done.mine_ref, bf16[8,208,128]{2,1,0:T(8,128)(2,1)S(1)} %collective-permute-done.other_ref, bf16[128,768]{1,0:T(8,128)(2,1)S(1)} %copy-done.3, ...), custom_call_target="tpu_custom_call" | custom-call | tf_op jit(solution)/shard_map/token/pallas_call | solution.py:338
  31.7 0.7 collective-permute-start.1
  32.4 1.7 %collective-permute-start.2 = (bf16[192,256]{1,0:T(8,128)(2,1)S(1)}, bf16[192,256]{1,0:T(8,128)(2,1)S(1)}, u32[]{:S(2)}, u32[]{:S(2)}) collective-permute-start(bf16[192,256]{1,0:T(8,128)(2,1)S(1)} %get-tuple-element.11), channel_id=1, source_target_pairs={{0,16},{1,17},{2,18},{3,19},{4,20},{5,21},{6,22},{7,23},{16,32},{1... | collective-permute-start | bytes 294920 | tf_op jit(solution)/shard_map/ppermute | solution.py:363
  34.1 3.3 %collective-permute-start.3 = (bf16[192,256]{1,0:T(8,128)(2,1)S(1)}, bf16[192,256]{1,0:T(8,128)(2,1)S(1)}, u32[]{:S(2)}, u32[]{:S(2)}) collective-permute-start(bf16[192,256]{1,0:T(8,128)(2,1)S(1)} %get-tuple-element.11), channel_id=1, source_target_pairs={{0,32},{1,33},{2,34},{3,35},{4,36},{5,37},{6,38},{7,39},{16,48},{1... | collective-permute-start | bytes 294920 | tf_op jit(solution)/shard_map/ppermute | solution.py:363
  37.4 0.7 %collective-permute-start.4 = (bf16[192,256]{1,0:T(8,128)(2,1)S(1)}, bf16[192,256]{1,0:T(8,128)(2,1)S(1)}, u32[]{:S(2)}, u32[]{:S(2)}) collective-permute-start(bf16[192,256]{1,0:T(8,128)(2,1)S(1)} %get-tuple-element.11), channel_id=1, source_target_pairs={{0,48},{1,49},{2,50},{3,51},{4,52},{5,53},{6,54},{7,55},{16,0},{17... | collective-permute-start | bytes 294920 | tf_op jit(solution)/shard_map/ppermute | solution.py:363
  38.2 3.4 %all-to-all-done.1 = bf16[8,544,128]{2,1,0:T(8,128)(2,1)S(1)} async-done(((bf16[8,544,128]{2,1,0:T(8,128)(2,1)}), bf16[8,544,128]{2,1,0:T(8,128)(2,1)S(1)}, u32[]{:S(2)}, u32[]{:S(2)}) %all-to-all-start.1) | async-done | bytes 1114144 | tf_op jit(solution)/shard_map/all_to_all | solution.py:319
  41.6 0.1 convert_element_type.8.bias_ref
  41.7 0.0 collective-permute-done.1.refs_0_
  41.7 0.0 collective-permute-done.2.refs_1_
  41.7 0.4 collective-permute-done.3.refs_2_
  42.1 0.0 collective-permute-done.4.refs_3_
  42.1 0.0 slice-start
  42.1 0.0 slice-start.1
  42.1 0.0 copy-start
  42.1 0.0 copy-start.1
  42.2 0.0 copy-start.4
  42.2 0.0 copy-start.5
  42.2 0.0 copy-start.7
  42.2 0.0 copy-start.8
  42.2 0.0 copy-start.9
  42.2 3.0 %attend.1 = bf16[8,112,256]{2,1,0:T(8,128)(2,1)S(1)} custom-call(bf16[256,96]{1,0:T(8,128)(2,1)S(1)} %get-tuple-element.9.query_ref, bf16[256,96]{1,0:T(8,128)(2,1)S(1)} %get-tuple-element.10.gate_ref, f32[8,544,128]{2,1,0:T(8,128)S(1)} %convert_element_type.8.bias_ref, bf16[192,256]{1,0:T(8,128)(2,1)S(1)} %collective-permute-done.1.refs_0_, ...), custom_call_target="tpu_custom_call" | custom-call | flops 20000000000 | bytes 8388608 | tf_op jit(solution)/shard_map/attend/pallas_call | solution.py:365
  45.2 17.2 %all_to_all.15.mine_ref = bf16[8,112,256]{2,1,0:T(8,128)(2,1)S(1)} all-to-all(bf16[8,112,256]{2,1,0:T(8,128)(2,1)S(1)} %attend.1), channel_id=1, replica_groups={{0,2,4,6,8,10,12,14},{1,3,5,7,9,11,13,15},{16,18,20,22,24,26,28,30},{17..., dimensions={0} | all-to-all | bytes 917504 | tf_op jit(solution)/shard_map/all_to_all | solution.py:287
  62.4 3.2 %collective-permute-start.5 = (bf16[8,112,256]{2,1,0:T(8,128)(2,1)S(1)}, bf16[8,112,256]{2,1,0:T(8,128)(2,1)S(1)}, u32[]{:S(2)}, u32[]{:S(2)}) collective-permute-start(bf16[8,112,256]{2,1,0:T(8,128)(2,1)S(1)} %all_to_all.15.mine_ref), channel_id=1, source_target_pairs={{0,1},{1,0},{2,3},{3,2},{4,5},{5,4},{6,7},{7,6},{8,9},{9,8},{10,11... | collective-permute-start | bytes 1376264 | tf_op jit(solution)/shard_map/ppermute | solution.py:288
  65.6 1.4 %collective-permute-done.5.other_ref = bf16[8,112,256]{2,1,0:T(8,128)(2,1)S(1)} collective-permute-done((bf16[8,112,256]{2,1,0:T(8,128)(2,1)S(1)}, bf16[8,112,256]{2,1,0:T(8,128)(2,1)S(1)}, u32[]{:S(2)}, u32[]{:S(2)}) %collective-permute-start.5) | collective-permute-done | bytes 458784 | tf_op jit(solution)/shard_map/ppermute | solution.py:288
  67.0 0.0 slice-done
  67.0 0.0 slice-done.1
  67.0 0.0 copy-done
  67.0 0.0 copy-done.1
  67.0 0.0 copy-done.4
  67.0 0.0 copy-done.5
  67.0 0.0 copy-done.7
  67.0 0.0 copy-done.8
  67.0 0.0 copy-done.9
  67.1 4.6 %close.1 = (f32[3,192]{1,0:T(4,128)}, f32[256,768]{1,0:T(8,128)}) custom-call(bf16[8,112,256]{2,1,0:T(8,128)(2,1)S(1)} %all_to_all.15.mine_ref, bf16[8,112,256]{2,1,0:T(8,128)(2,1)S(1)} %collective-permute-done.5.other_ref, bf16[4,2,96,768]{3,2,1,0:T(8,128)(2,1)S(1)} %bitcast.7, f32[256,768]{1,0:T(8,128)S(1)} %get-tuple-element.12.start_ref, ...), custom_call_target="tpu_custom_call" | custom-call | tf_op jit(solution)/shard_map/close/pallas_call | solution.py:378
  (2 shorter events, 0.0 us)
Async XLA Ops:
  3.3 18.1 %all-to-all-start = ((bf16[8,208,128]{2,1,0:T(8,128)(2,1)}), bf16[8,208,128]{2,1,0:T(8,128)(2,1)S(1)}, u32[]{:S(2)}, u32[]{:S(2)}) async-start(bf16[8,208,128]{2,1,0:T(8,128)(2,1)} %get-tuple-element.8), calls=%async_computation | async-start | bytes 851968 | tf_op jit(solution)/shard_map/all_to_all | solution.py:287
  21.4 20.1 %all-to-all-start.1 = ((bf16[8,544,128]{2,1,0:T(8,128)(2,1)}), bf16[8,544,128]{2,1,0:T(8,128)(2,1)S(1)}, u32[]{:S(2)}, u32[]{:S(2)}) async-start(bf16[8,544,128]{2,1,0:T(8,128)(2,1)} %bias.1), calls=%async_computation.1 | async-start | bytes 2228224 | tf_op jit(solution)/shard_map/all_to_all | solution.py:319
  25.8 2.1 %collective-permute-start = (bf16[8,208,128]{2,1,0:T(8,128)(2,1)S(1)}, bf16[8,208,128]{2,1,0:T(8,128)(2,1)S(1)}, u32[]{:S(2)}, u32[]{:S(2)}) collective-permute-start(bf16[8,208,128]{2,1,0:T(8,128)(2,1)S(1)} %all-to-all-done.mine_ref), channel_id=1, source_target_pairs={{0,1},{1,0},{2,3},{3,2},{4,5},{5,4},{6,7},{7,6},{8,9},{9,8},{10,11... | collective-permute-start | bytes 1277960 | tf_op jit(solution)/shard_map/ppermute | solution.py:288
  25.9 2.0 %copy-start.2 = (f32[256,768]{1,0:T(8,128)S(1)}, f32[256,768]{1,0:T(8,128)}, u32[]{:S(2)}) copy-start(f32[256,768]{1,0:T(8,128)} %cond_ref.3) | copy-start | bytes 2359300
  25.9 2.0 %copy-start.3 = (bf16[128,768]{1,0:T(8,128)(2,1)S(1)}, bf16[128,768]{1,0:T(8,128)(2,1)}, u32[]{:S(2)}) copy-start(bf16[128,768]{1,0:T(8,128)(2,1)} %w_atom_ref.1) | copy-start | bytes 589828
  25.9 2.0 %copy-start.6 = (f32[3,768]{1,0:T(4,128)S(1)}, f32[3,768]{1,0:T(4,128)}, u32[]{:S(2)}) copy-start(f32[3,768]{1,0:T(4,128)} %gains_ref.3) | copy-start | bytes 27652
  31.7 10.0 %collective-permute-start.1 = (bf16[192,256]{1,0:T(8,128)(2,1)S(1)}, bf16[192,256]{1,0:T(8,128)(2,1)S(1)}, u32[]{:S(2)}, u32[]{:S(2)}) collective-permute-start(bf16[192,256]{1,0:T(8,128)(2,1)S(1)} %get-tuple-element.11), channel_id=1, source_target_pairs={{0,0},{1,1},{2,2},{3,3},{4,4},{5,5},{6,6},{7,7},{16,16},{17,17},{1... | collective-permute-start | bytes 294920 | tf_op jit(solution)/shard_map/ppermute | solution.py:363
  32.4 9.3 %collective-permute-start.2 = (bf16[192,256]{1,0:T(8,128)(2,1)S(1)}, bf16[192,256]{1,0:T(8,128)(2,1)S(1)}, u32[]{:S(2)}, u32[]{:S(2)}) collective-permute-start(bf16[192,256]{1,0:T(8,128)(2,1)S(1)} %get-tuple-element.11), channel_id=1, source_target_pairs={{0,16},{1,17},{2,18},{3,19},{4,20},{5,21},{6,22},{7,23},{16,32},{1... | collective-permute-start | bytes 294920 | tf_op jit(solution)/shard_map/ppermute | solution.py:363
  34.1 8.0 %collective-permute-start.3 = (bf16[192,256]{1,0:T(8,128)(2,1)S(1)}, bf16[192,256]{1,0:T(8,128)(2,1)S(1)}, u32[]{:S(2)}, u32[]{:S(2)}) collective-permute-start(bf16[192,256]{1,0:T(8,128)(2,1)S(1)} %get-tuple-element.11), channel_id=1, source_target_pairs={{0,32},{1,33},{2,34},{3,35},{4,36},{5,37},{6,38},{7,39},{16,48},{1... | collective-permute-start | bytes 294920 | tf_op jit(solution)/shard_map/ppermute | solution.py:363
  37.4 4.7 %collective-permute-start.4 = (bf16[192,256]{1,0:T(8,128)(2,1)S(1)}, bf16[192,256]{1,0:T(8,128)(2,1)S(1)}, u32[]{:S(2)}, u32[]{:S(2)}) collective-permute-start(bf16[192,256]{1,0:T(8,128)(2,1)S(1)} %get-tuple-element.11), channel_id=1, source_target_pairs={{0,48},{1,49},{2,50},{3,51},{4,52},{5,53},{6,54},{7,55},{16,0},{17... | collective-permute-start | bytes 294920 | tf_op jit(solution)/shard_map/ppermute | solution.py:363
  42.1 24.9 %slice-start = ((s8[4718592]{0:T(1024)(128)(4,1)}), s8[4194304]{0:T(1024)(128)(4,1)S(1)}, s32[]{:S(2)}) async-start(s8[4718592]{0:T(1024)(128)(4,1)} %bitcast.5), calls=%async_computation.3 | async-start | bytes 8388608
  42.1 24.9 %slice-start.1 = ((s8[4718592]{0:T(1024)(128)(4,1)}), s8[524288]{0:T(1024)(128)(4,1)S(1)}, s32[]{:S(2)}) async-start(s8[4718592]{0:T(1024)(128)(4,1)} %bitcast.5), calls=%async_computation.4 | async-start | bytes 1048576
  42.1 24.9 %copy-start = (bf16[1536,768]{1,0:T(8,128)(2,1)S(1)}, bf16[1536,768]{1,0:T(8,128)(2,1)}, u32[]{:S(2)}) copy-start(bf16[1536,768]{1,0:T(8,128)(2,1)} %w_down_ref.1) | copy-start | bytes 7077892
  42.1 24.9 %copy-start.1 = (bf16[768,768]{1,0:T(8,128)(2,1)S(1)}, bf16[768,768]{1,0:T(8,128)(2,1)}, u32[]{:S(2)}) copy-start(bf16[768,768]{1,0:T(8,128)(2,1)} %param.29) | copy-start | bytes 3538948
  42.2 24.9 %copy-start.4 = (bf16[768,128]{1,0:T(8,128)(2,1)S(1)}, bf16[768,128]{1,0:T(8,128)(2,1)}, u32[]{:S(2)}) copy-start(bf16[768,128]{1,0:T(8,128)(2,1)} %w_tok_ref.1) | copy-start | bytes 589828
  42.2 24.8 %copy-start.5 = (f32[192,128]{1,0:T(8,128)S(1)}, f32[192,128]{1,0:T(8,128)}, u32[]{:S(2)}) copy-start(f32[192,128]{1,0:T(8,128)} %get-tuple-element.13.state_ref) | copy-start | bytes 294916
  42.2 24.8 %copy-start.7 = (f32[3,192]{1,0:T(4,128)S(1)}, f32[3,192]{1,0:T(4,128)}, u32[]{:S(2)}) copy-start(f32[3,192]{1,0:T(4,128)} %pos_ref.3) | copy-start | bytes 6916
  42.2 24.8 %copy-start.8 = (s32[192]{0:T(256)S(1)}, s32[192]{0:T(256)}, u32[]{:S(2)}) copy-start(s32[192]{0:T(256)} %param.20) | copy-start | bytes 2308
  42.2 24.8 %copy-start.9 = (bf16[3,128]{1,0:T(4,128)(2,1)S(1)}, bf16[3,128]{1,0:T(4,128)(2,1)}, u32[]{:S(2)}) copy-start(bf16[3,128]{1,0:T(4,128)(2,1)} %w_pos_ref.3) | copy-start | bytes 2308
  62.4 4.6 %collective-permute-start.5 = (bf16[8,112,256]{2,1,0:T(8,128)(2,1)S(1)}, bf16[8,112,256]{2,1,0:T(8,128)(2,1)S(1)}, u32[]{:S(2)}, u32[]{:S(2)}) collective-permute-start(bf16[8,112,256]{2,1,0:T(8,128)(2,1)S(1)} %all_to_all.15.mine_ref), channel_id=1, source_target_pairs={{0,1},{1,0},{2,3},{3,2},{4,5},{5,4},{6,7},{7,6},{8,9},{9,8},{10,11... | collective-permute-start | bytes 1376264 | tf_op jit(solution)/shard_map/ppermute | solution.py:288

commit v4 on v3

--- a/solution.py
+++ b/solution.py
@@ -11,6 +11,7 @@
 HEADS = 16
 HEAD_DIM = D // HEADS
 DUO = 2 * HEAD_DIM
+STEPS = (2, 1, 3, 0)
 BF = jnp.bfloat16
 F32 = jnp.float32
 MIB = 1 << 20
@@ -93,14 +94,15 @@
             axis=1,
         )
         bias = dot(weight, both, ((1,), (1,)))
-        at = (part % 2) * HEADS * rows
+        step = rows + 8
+        at = (part % 2) * HEADS * step
         for i in range(half):
             here = slice(i * cols, (i + 1) * cols)
-            held[pl.ds(at + i, HEADS, stride=rows), :] = bias[:HEADS, here]
-            held[pl.ds(at + half + i, HEADS, stride=rows), :] = bias[HEADS:, here]
+            held[pl.ds(at + i, HEADS, stride=step), :] = bias[:HEADS, here]
+            held[pl.ds(at + half + i, HEADS, stride=step), :] = bias[HEADS:, here]
         top_of = jnp.zeros((rows, 128), F32)
         for h in range(HEADS):
-            lines = held[at + h * rows : at + (h + 1) * rows, :]
+            lines = held[at + h * step : at + h * step + rows, :]
             top = jnp.max(lines, axis=1, keepdims=True)
             first = h % 2 * span + part * rows
             out_ref[h // 2, first : first + rows, :] = (lines - top).astype(BF)
@@ -156,9 +158,7 @@
     span = tok_rows + 16
     place = lax.rem(lax.axis_index("aa"), ring)
     per = keys // bias_ref.shape[2]
-    order = [
-        lax.rem(place - by + ring, ring) * per + b for by in range(ring) for b in range(per)
-    ]
+    order = [lax.rem(place - by + ring, ring) * per + b for by in STEPS for b in range(per)]
     n = tok_rows // 128
     step = 128
     outs, stats = [], []
@@ -211,7 +211,7 @@
     half = ref.shape[0] // 2
     mixed = []
     for x in range(half):
-        pair = (ref[x], ref[half + x])
+        pair = (ref[2 * x], ref[2 * x + 1])
         stats = []
         for part in pair:
             tail = part[DUO:].astype(F32)
@@ -279,12 +279,14 @@
     peers = size // 2
     groups = lax.axis_size("aa")
     duo = lax.rem(lax.axis_index("ba"), peers)
-    same_core = [list(range(core, size, 2)) for core in range(2)]
+    woven = [i + j for i in range(0, peers, 2) for j in (0, peers)]
+    same_core = [woven, [(i + peers + 1) % size for i in woven]]
+    turned_core = [woven, [(i + 5) % size for i in woven]]
     halves = [list(range(peers)), list(range(peers, size))]
     siblings = [(i, i ^ 1) for i in range(size)]
 
-    def gathered(copies):
-        mine = lax.all_to_all(copies, "ba", 0, 0, tiled=True, axis_index_groups=same_core)
+    def gathered(copies, sets):
+        mine = lax.all_to_all(copies, "ba", 0, 0, tiled=True, axis_index_groups=sets)
         return mine, lax.ppermute(mine, "ba", siblings)
 
     ids = atom_token[None, :]
@@ -297,7 +299,7 @@
         name="state",
     )(atom_cond, noisy_pos, noise, ids, w_pos)
 
-    block = 32
+    block = 64
     bias = pl.pallas_call(
         bias_kernel,
         out_shape=shape((peers, 2 * (tok_rows + 16), cols), BF),
@@ -305,7 +307,7 @@
         out_specs=whole(1)[0],
         scratch_shapes=[
             pltpu.VMEM((tok_rows // block, block, cols, chans), BF),
-            pltpu.VMEM((2 * HEADS * block, cols), F32),
+            pltpu.VMEM((2 * HEADS * (block + 8), cols), F32),
             pltpu.VMEM((tok_rows, 128), F32),
             pltpu.SemaphoreType.DMA((tok_rows // block,)),
         ],
@@ -334,7 +336,7 @@
         axis=1,
     )
 
-    mine, other = gathered(packed)
+    mine, other = gathered(packed, turned_core)
     start, query, gate, kv = pl.pallas_call(
         token_kernel,
         out_shape=(
@@ -351,7 +353,7 @@
     )(mine, other, w_atom_token, token_cond, gains, w_head)
     ring = groups // 2
     spread = []
-    for by in range(ring):
+    for by in STEPS:
         moves = []
         for low in range(2):
             for high in range(2):
@@ -373,7 +375,7 @@
         ),
         name="attend",
     )(query, gate, bias, *spread)
-    mine, other = gathered(mixed)
+    mine, other = gathered(mixed, same_core)
 
     return pl.pallas_call(
         close_kernel,

time: 72.1 us -> 70.7 us (0.981)
  starting transfers between devices: 21.5 us -> 26.2 us
  waiting for transfers between devices: 8.04 us -> 4.4 us
  blocking collectives: 17.2 us -> 15.6 us
  Pallas kernels: 21.3 us -> 20.4 us
    all_to_all x1, waiting for transfers between devices: 2.78 us -> 0.01 us  [gathered(): lax.all_to_all(copies, 'ba', 0, 0, tiled=True, axis_index_groups=sets)]
    all_to_all x1, starting transfers between devices: 4.31 us -> 6.07 us  [on_device(): lax.all_to_all(bias, 'ba', 0, 0, tiled=True, axis_index_groups=halves)]
    all_to_all x1, blocking collectives: 17.2 us -> 15.6 us  [gathered(): lax.all_to_all(copies, 'ba', 0, 0, tiled=True, axis_index_groups=sets)]
    ppermute x2, starting transfers between devices: 3.35 us -> 4.7 us  [gathered(): return (mine, lax.ppermute(mine, 'ba', siblings))]
    all_to_all x1, starting transfers between devices: 7.48 us -> 8.39 us  [gathered(): lax.all_to_all(copies, 'ba', 0, 0, tiled=True, axis_index_groups=sets)]
    pallas_call x1, Pallas kernels: 7.85 us -> 6.95 us  [on_device(): pl.pallas_call(bias_kernel, out_shape=shape((peers, 2 * (tok_rows + 16),...]
  transfers between devices with their start and end apart: 8 -> 8, of which waited for: 4 -> 2; matrix products, arithmetic and copies ran while one was open for 3% -> 3% of each run, Pallas kernels for 16% -> 15%
where the time goes in v4:
time: 70.7 us; the launch traced here: 70.3 us
  starting transfers between devices  26.2 us (37%)
  Pallas kernels  20.4 us (29%)
  blocking collectives  15.6 us (22%)
  waiting for transfers between devices  4.4 us (6%)
  local copies, waits for them, and re-layouts  1.83 us (3%)
  between operations  1.53 us (2%)
    all_to_all x1, blocking collectives, gathered(): lax.all_to_all(copies, 'ba', 0, 0, tiled=True, axis_index_groups=sets)  15.6 us
    all_to_all x1, starting transfers between devices, gathered(): lax.all_to_all(copies, 'ba', 0, 0, tiled=True, axis_index_groups=sets)  8.39 us
    ppermute x4, starting transfers between devices, on_device(): spread.append(lax.ppermute(kv, ('aa', 'ba'), moves))  7.01 us
    pallas_call x1, Pallas kernels, on_device(): pl.pallas_call(bias_kernel, out_shape=shape((peers, 2 * (tok_rows + 16),...  6.95 us
    all_to_all x1, starting transfers between devices, on_device(): lax.all_to_all(bias, 'ba', 0, 0, tiled=True, axis_index_groups=halves)  6.07 us
    ppermute x2, starting transfers between devices, gathered(): return (mine, lax.ppermute(mine, 'ba', siblings))  4.7 us
    pallas_call x1, Pallas kernels, on_device(): pl.pallas_call(close_kernel, out_shape=(shape((3, atoms), F32), shape((to...  4.63 us
    pallas_call x1, Pallas kernels, on_device(): pl.pallas_call(token_kernel, out_shape=(shape((tok_rows, D), F32), shape(...  3.8 us
  transfers between devices with their start and end apart: 8, of which 2 were waited for; matrix products, arithmetic and copies ran while one was open for 3% of the time, Pallas kernels for 15%

profile of v4, /device:TPU:1, one launch (start us, length us, event | category | flops | bytes accessed | tf_op | source)
XLA Modules:
  0.0 70.3 jit_solution(9873244614230479674)
XLA Ops:
  1.3 2.0 %state.1 = (f32[192,128]{1,0:T(8,128)}, bf16[8,208,128]{2,1,0:T(8,128)(2,1)}) custom-call(f32[192,128]{1,0:T(8,128)} %cond_ref.2, f32[3,192]{1,0:T(4,128)} %pos_ref.3, f32[1,1]{1,0:T(1,128)} %bitcast.3.noise_ref, s32[1,192]{1,0:T(1,128)} %bitcast.8, f32[3,128]{1,0:T(4,128)} %w_pos_ref.2), custom_call_target="tpu_custom_call" | custom-call | tf_op jit(solution)/shard_map/state/pallas_call | solution.py:294
  3.3 8.4 %all-to-all-start = ((bf16[8,208,128]{2,1,0:T(8,128)(2,1)}), bf16[8,208,128]{2,1,0:T(8,128)(2,1)S(1)}, u32[]{:S(2)}, u32[]{:S(2)}) async-start(bf16[8,208,128]{2,1,0:T(8,128)(2,1)} %get-tuple-element.8), calls=%async_computation | async-start | bytes 851968 | tf_op jit(solution)/shard_map/all_to_all | solution.py:289
  11.7 7.0 %bias.1 = bf16[8,544,128]{2,1,0:T(8,128)(2,1)} custom-call(bf16[256,128,128]{2,1,0:T(8,128)(2,1)} %pair_ref.1, bf16[16,128]{1,0:T(8,128)(2,1)} %w_ref.1), custom_call_target="tpu_custom_call" | custom-call | flops 2147483648 | bytes 10485760 | tf_op jit(solution)/shard_map/bias/pallas_call | solution.py:303
  18.7 0.0 all-to-all-done.mine_ref
  18.7 6.1 %all-to-all-start.1 = ((bf16[8,544,128]{2,1,0:T(8,128)(2,1)}), bf16[8,544,128]{2,1,0:T(8,128)(2,1)S(1)}, u32[]{:S(2)}, u32[]{:S(2)}) async-start(bf16[8,544,128]{2,1,0:T(8,128)(2,1)} %bias.1), calls=%async_computation.1 | async-start | bytes 2228224 | tf_op jit(solution)/shard_map/all_to_all | solution.py:321
  24.8 0.0 collective-permute-start
  24.8 0.0 copy-start.3
  24.8 0.0 copy-start.6
  24.8 1.8 %constant_dynamic-slice_fusion.1 = (bf16[768,96]{1,0:T(8,128)(2,1)S(1)}, bf16[768,96]{1,0:T(8,128)(2,1)S(1)}, bf16[768,96]{1,0:T(8,128)(2,1)S(1)}, bf16[768,96]{1,0:T(8,128)(2,1)S(1)}) fusion(bf16[768,1536]{1,0:T(8,128)(2,1)} %param.28, s32[]{:T(128)S(6)} %select_n.8, s32[]{:T(128)S(6)} %select_n.9, bf16[768,1536]{1,0:T(8,128)(2,1)} %param.27), kind=kLoop, calls=%fused_computation.16 | loop fusion | bytes 1179656 | tf_op jit(solution)/shard_map/dynamic_slice | solution.py:326
  26.6 0.2 fusion.7.w_head_ref
  26.8 0.0 collective-permute-done.other_ref
  26.8 0.0 copy-done.2
  26.8 0.0 copy-done.3
  26.8 0.0 copy-done.6
  26.8 3.8 %token_.1 = (f32[256,768]{1,0:T(8,128)S(1)}, bf16[256,96]{1,0:T(8,128)(2,1)S(1)}, bf16[256,96]{1,0:T(8,128)(2,1)S(1)}, bf16[192,256]{1,0:T(8,128)(2,1)S(1)}) custom-call(bf16[8,208,128]{2,1,0:T(8,128)(2,1)S(1)} %all-to-all-done.mine_ref, bf16[8,208,128]{2,1,0:T(8,128)(2,1)S(1)} %collective-permute-done.other_ref, bf16[128,768]{1,0:T(8,128)(2,1)S(1)} %copy-done.3, ...), custom_call_target="tpu_custom_call" | custom-call | tf_op jit(solution)/shard_map/token/pallas_call | solution.py:340
  30.6 3.7 %collective-permute-start.1 = (bf16[192,256]{1,0:T(8,128)(2,1)S(1)}, bf16[192,256]{1,0:T(8,128)(2,1)S(1)}, u32[]{:S(2)}, u32[]{:S(2)}) collective-permute-start(bf16[192,256]{1,0:T(8,128)(2,1)S(1)} %get-tuple-element.11), channel_id=1, source_target_pairs={{0,32},{1,33},{2,34},{3,35},{4,36},{5,37},{6,38},{7,39},{16,48},{1... | collective-permute-start | bytes 294920 | tf_op jit(solution)/shard_map/ppermute | solution.py:365
  34.3 0.7 %collective-permute-start.2 = (bf16[192,256]{1,0:T(8,128)(2,1)S(1)}, bf16[192,256]{1,0:T(8,128)(2,1)S(1)}, u32[]{:S(2)}, u32[]{:S(2)}) collective-permute-start(bf16[192,256]{1,0:T(8,128)(2,1)S(1)} %get-tuple-element.11), channel_id=1, source_target_pairs={{0,16},{1,17},{2,18},{3,19},{4,20},{5,21},{6,22},{7,23},{16,32},{1... | collective-permute-start | bytes 294920 | tf_op jit(solution)/shard_map/ppermute | solution.py:365
  35.0 1.9 %collective-permute-start.3 = (bf16[192,256]{1,0:T(8,128)(2,1)S(1)}, bf16[192,256]{1,0:T(8,128)(2,1)S(1)}, u32[]{:S(2)}, u32[]{:S(2)}) collective-permute-start(bf16[192,256]{1,0:T(8,128)(2,1)S(1)} %get-tuple-element.11), channel_id=1, source_target_pairs={{0,48},{1,49},{2,50},{3,51},{4,52},{5,53},{6,54},{7,55},{16,0},{17... | collective-permute-start | bytes 294920 | tf_op jit(solution)/shard_map/ppermute | solution.py:365
  37.0 0.7 collective-permute-start.4
  37.6 2.9 %all-to-all-done.1 = bf16[8,544,128]{2,1,0:T(8,128)(2,1)S(1)} async-done(((bf16[8,544,128]{2,1,0:T(8,128)(2,1)}), bf16[8,544,128]{2,1,0:T(8,128)(2,1)S(1)}, u32[]{:S(2)}, u32[]{:S(2)}) %all-to-all-start.1) | async-done | bytes 1114144 | tf_op jit(solution)/shard_map/all_to_all | solution.py:321
  40.6 0.1 convert_element_type.8.bias_ref
  40.7 0.0 collective-permute-done.1.refs_0_
  40.7 0.0 collective-permute-done.2.refs_1_
  40.7 0.0 collective-permute-done.3.refs_2_
  40.7 0.0 collective-permute-done.4.refs_3_
  40.8 0.0 slice-start
  40.8 0.0 slice-start.1
  40.8 0.0 copy-start
  40.8 0.0 copy-start.1
  40.8 0.0 copy-start.4
  40.8 0.0 copy-start.5
  40.8 0.0 copy-start.7
  40.8 0.0 copy-start.8
  40.8 0.0 copy-start.9
  40.9 3.0 %attend.1 = bf16[8,112,256]{2,1,0:T(8,128)(2,1)S(1)} custom-call(bf16[256,96]{1,0:T(8,128)(2,1)S(1)} %get-tuple-element.9.query_ref, bf16[256,96]{1,0:T(8,128)(2,1)S(1)} %get-tuple-element.10.gate_ref, f32[8,544,128]{2,1,0:T(8,128)S(1)} %convert_element_type.8.bias_ref, bf16[192,256]{1,0:T(8,128)(2,1)S(1)} %collective-permute-done.1.refs_0_, ...), custom_call_target="tpu_custom_call" | custom-call | flops 20000000000 | bytes 8388608 | tf_op jit(solution)/shard_map/attend/pallas_call | solution.py:367
  43.8 15.6 %all_to_all.15.mine_ref = bf16[8,112,256]{2,1,0:T(8,128)(2,1)S(1)} all-to-all(bf16[8,112,256]{2,1,0:T(8,128)(2,1)S(1)} %attend.1), channel_id=1, replica_groups={{0,8,2,10,4,12,6,14},{9,1,11,3,13,5,15,7},{16,24,18,26,20,28,22,30},{25..., dimensions={0} | all-to-all | bytes 917504 | tf_op jit(solution)/shard_map/all_to_all | solution.py:289
  59.5 4.7 %collective-permute-start.5 = (bf16[8,112,256]{2,1,0:T(8,128)(2,1)S(1)}, bf16[8,112,256]{2,1,0:T(8,128)(2,1)S(1)}, u32[]{:S(2)}, u32[]{:S(2)}) collective-permute-start(bf16[8,112,256]{2,1,0:T(8,128)(2,1)S(1)} %all_to_all.15.mine_ref), channel_id=1, source_target_pairs={{0,1},{1,0},{2,3},{3,2},{4,5},{5,4},{6,7},{7,6},{8,9},{9,8},{10,11... | collective-permute-start | bytes 1376264 | tf_op jit(solution)/shard_map/ppermute | solution.py:290
  64.2 1.4 %collective-permute-done.5.other_ref = bf16[8,112,256]{2,1,0:T(8,128)(2,1)S(1)} collective-permute-done((bf16[8,112,256]{2,1,0:T(8,128)(2,1)S(1)}, bf16[8,112,256]{2,1,0:T(8,128)(2,1)S(1)}, u32[]{:S(2)}, u32[]{:S(2)}) %collective-permute-start.5) | collective-permute-done | bytes 458784 | tf_op jit(solution)/shard_map/ppermute | solution.py:290
  65.6 0.0 slice-done
  65.6 0.0 slice-done.1
  65.6 0.0 copy-done
  65.6 0.0 copy-done.1
  65.6 0.0 copy-done.4
  65.6 0.0 copy-done.5
  65.6 0.0 copy-done.7
  65.7 0.0 copy-done.8
  65.7 0.0 copy-done.9
  65.7 4.6 %close.1 = (f32[3,192]{1,0:T(4,128)}, f32[256,768]{1,0:T(8,128)}) custom-call(bf16[8,112,256]{2,1,0:T(8,128)(2,1)S(1)} %all_to_all.15.mine_ref, bf16[8,112,256]{2,1,0:T(8,128)(2,1)S(1)} %collective-permute-done.5.other_ref, bf16[4,2,96,768]{3,2,1,0:T(8,128)(2,1)S(1)} %bitcast.7, f32[256,768]{1,0:T(8,128)S(1)} %get-tuple-element.12.start_ref, ...), custom_call_target="tpu_custom_call" | custom-call | tf_op jit(solution)/shard_map/close/pallas_call | solution.py:380
  (2 shorter events, 0.0 us)
Async XLA Ops:
  3.3 15.4 %all-to-all-start = ((bf16[8,208,128]{2,1,0:T(8,128)(2,1)}), bf16[8,208,128]{2,1,0:T(8,128)(2,1)S(1)}, u32[]{:S(2)}, u32[]{:S(2)}) async-start(bf16[8,208,128]{2,1,0:T(8,128)(2,1)} %get-tuple-element.8), calls=%async_computation | async-start | bytes 851968 | tf_op jit(solution)/shard_map/all_to_all | solution.py:289
  18.7 21.9 %all-to-all-start.1 = ((bf16[8,544,128]{2,1,0:T(8,128)(2,1)}), bf16[8,544,128]{2,1,0:T(8,128)(2,1)S(1)}, u32[]{:S(2)}, u32[]{:S(2)}) async-start(bf16[8,544,128]{2,1,0:T(8,128)(2,1)} %bias.1), calls=%async_computation.1 | async-start | bytes 2228224 | tf_op jit(solution)/shard_map/all_to_all | solution.py:321
  24.8 2.0 %collective-permute-start = (bf16[8,208,128]{2,1,0:T(8,128)(2,1)S(1)}, bf16[8,208,128]{2,1,0:T(8,128)(2,1)S(1)}, u32[]{:S(2)}, u32[]{:S(2)}) collective-permute-start(bf16[8,208,128]{2,1,0:T(8,128)(2,1)S(1)} %all-to-all-done.mine_ref), channel_id=1, source_target_pairs={{0,1},{1,0},{2,3},{3,2},{4,5},{5,4},{6,7},{7,6},{8,9},{9,8},{10,11... | collective-permute-start | bytes 1277960 | tf_op jit(solution)/shard_map/ppermute | solution.py:290
  24.8 2.0 %copy-start.2 = (f32[256,768]{1,0:T(8,128)S(1)}, f32[256,768]{1,0:T(8,128)}, u32[]{:S(2)}) copy-start(f32[256,768]{1,0:T(8,128)} %cond_ref.3) | copy-start | bytes 2359300
  24.8 2.0 %copy-start.3 = (bf16[128,768]{1,0:T(8,128)(2,1)S(1)}, bf16[128,768]{1,0:T(8,128)(2,1)}, u32[]{:S(2)}) copy-start(bf16[128,768]{1,0:T(8,128)(2,1)} %w_atom_ref.1) | copy-start | bytes 589828
  24.8 2.0 %copy-start.6 = (f32[3,768]{1,0:T(4,128)S(1)}, f32[3,768]{1,0:T(4,128)}, u32[]{:S(2)}) copy-start(f32[3,768]{1,0:T(4,128)} %gains_ref.3) | copy-start | bytes 27652
  30.6 10.1 %collective-permute-start.1 = (bf16[192,256]{1,0:T(8,128)(2,1)S(1)}, bf16[192,256]{1,0:T(8,128)(2,1)S(1)}, u32[]{:S(2)}, u32[]{:S(2)}) collective-permute-start(bf16[192,256]{1,0:T(8,128)(2,1)S(1)} %get-tuple-element.11), channel_id=1, source_target_pairs={{0,32},{1,33},{2,34},{3,35},{4,36},{5,37},{6,38},{7,39},{16,48},{1... | collective-permute-start | bytes 294920 | tf_op jit(solution)/shard_map/ppermute | solution.py:365
  34.3 6.4 %collective-permute-start.2 = (bf16[192,256]{1,0:T(8,128)(2,1)S(1)}, bf16[192,256]{1,0:T(8,128)(2,1)S(1)}, u32[]{:S(2)}, u32[]{:S(2)}) collective-permute-start(bf16[192,256]{1,0:T(8,128)(2,1)S(1)} %get-tuple-element.11), channel_id=1, source_target_pairs={{0,16},{1,17},{2,18},{3,19},{4,20},{5,21},{6,22},{7,23},{16,32},{1... | collective-permute-start | bytes 294920 | tf_op jit(solution)/shard_map/ppermute | solution.py:365
  35.0 5.7 %collective-permute-start.3 = (bf16[192,256]{1,0:T(8,128)(2,1)S(1)}, bf16[192,256]{1,0:T(8,128)(2,1)S(1)}, u32[]{:S(2)}, u32[]{:S(2)}) collective-permute-start(bf16[192,256]{1,0:T(8,128)(2,1)S(1)} %get-tuple-element.11), channel_id=1, source_target_pairs={{0,48},{1,49},{2,50},{3,51},{4,52},{5,53},{6,54},{7,55},{16,0},{17... | collective-permute-start | bytes 294920 | tf_op jit(solution)/shard_map/ppermute | solution.py:365
  37.0 3.8 %collective-permute-start.4 = (bf16[192,256]{1,0:T(8,128)(2,1)S(1)}, bf16[192,256]{1,0:T(8,128)(2,1)S(1)}, u32[]{:S(2)}, u32[]{:S(2)}) collective-permute-start(bf16[192,256]{1,0:T(8,128)(2,1)S(1)} %get-tuple-element.11), channel_id=1, source_target_pairs={{0,0},{1,1},{2,2},{3,3},{4,4},{5,5},{6,6},{7,7},{16,16},{17,17},{1... | collective-permute-start | bytes 294920 | tf_op jit(solution)/shard_map/ppermute | solution.py:365
  40.8 24.9 %slice-start = ((s8[4718592]{0:T(1024)(128)(4,1)}), s8[4194304]{0:T(1024)(128)(4,1)S(1)}, s32[]{:S(2)}) async-start(s8[4718592]{0:T(1024)(128)(4,1)} %bitcast.5), calls=%async_computation.3 | async-start | bytes 8388608
  40.8 24.9 %slice-start.1 = ((s8[4718592]{0:T(1024)(128)(4,1)}), s8[524288]{0:T(1024)(128)(4,1)S(1)}, s32[]{:S(2)}) async-start(s8[4718592]{0:T(1024)(128)(4,1)} %bitcast.5), calls=%async_computation.4 | async-start | bytes 1048576
  40.8 24.8 %copy-start = (bf16[1536,768]{1,0:T(8,128)(2,1)S(1)}, bf16[1536,768]{1,0:T(8,128)(2,1)}, u32[]{:S(2)}) copy-start(bf16[1536,768]{1,0:T(8,128)(2,1)} %w_down_ref.1) | copy-start | bytes 7077892
  40.8 24.8 %copy-start.1 = (bf16[768,768]{1,0:T(8,128)(2,1)S(1)}, bf16[768,768]{1,0:T(8,128)(2,1)}, u32[]{:S(2)}) copy-start(bf16[768,768]{1,0:T(8,128)(2,1)} %param.29) | copy-start | bytes 3538948
  40.8 24.8 %copy-start.4 = (bf16[768,128]{1,0:T(8,128)(2,1)S(1)}, bf16[768,128]{1,0:T(8,128)(2,1)}, u32[]{:S(2)}) copy-start(bf16[768,128]{1,0:T(8,128)(2,1)} %w_tok_ref.1) | copy-start | bytes 589828
  40.8 24.8 %copy-start.5 = (f32[192,128]{1,0:T(8,128)S(1)}, f32[192,128]{1,0:T(8,128)}, u32[]{:S(2)}) copy-start(f32[192,128]{1,0:T(8,128)} %get-tuple-element.13.state_ref) | copy-start | bytes 294916
  40.8 24.8 %copy-start.7 = (f32[3,192]{1,0:T(4,128)S(1)}, f32[3,192]{1,0:T(4,128)}, u32[]{:S(2)}) copy-start(f32[3,192]{1,0:T(4,128)} %pos_ref.3) | copy-start | bytes 6916
  40.8 24.8 %copy-start.8 = (s32[192]{0:T(256)S(1)}, s32[192]{0:T(256)}, u32[]{:S(2)}) copy-start(s32[192]{0:T(256)} %param.20) | copy-start | bytes 2308
  40.8 24.8 %copy-start.9 = (bf16[3,128]{1,0:T(4,128)(2,1)S(1)}, bf16[3,128]{1,0:T(4,128)(2,1)}, u32[]{:S(2)}) copy-start(bf16[3,128]{1,0:T(4,128)(2,1)} %w_pos_ref.3) | copy-start | bytes 2308
  59.5 6.1 %collective-permute-start.5 = (bf16[8,112,256]{2,1,0:T(8,128)(2,1)S(1)}, bf16[8,112,256]{2,1,0:T(8,128)(2,1)S(1)}, u32[]{:S(2)}, u32[]{:S(2)}) collective-permute-start(bf16[8,112,256]{2,1,0:T(8,128)(2,1)S(1)} %all_to_all.15.mine_ref), channel_id=1, source_target_pairs={{0,1},{1,0},{2,3},{3,2},{4,5},{5,4},{6,7},{7,6},{8,9},{9,8},{10,11... | collective-permute-start | bytes 1376264 | tf_op jit(solution)/shard_map/ppermute | solution.py:290

commit v5 on v4

--- a/solution.py
+++ b/solution.py
@@ -11,7 +11,7 @@
 HEADS = 16
 HEAD_DIM = D // HEADS
 DUO = 2 * HEAD_DIM
-STEPS = (2, 1, 3, 0)
+STEPS = (2, 3, 1, 0)
 BF = jnp.bfloat16
 F32 = jnp.float32
 MIB = 1 << 20

time: 70.7 us -> 70.6 us (level)
  starting transfers between devices: 26.2 us -> 23.5 us
  blocking collectives: 15.6 us -> 17 us
  waiting for transfers between devices: 4.4 us -> 5.61 us
    ppermute x2, starting transfers between devices: 4.7 us -> 3.28 us  [gathered(): return (mine, lax.ppermute(mine, 'ba', siblings))]
    all_to_all x1, blocking collectives: 15.6 us -> 17 us  [gathered(): lax.all_to_all(copies, 'ba', 0, 0, tiled=True, axis_index_groups=sets)]
    all_to_all x1, waiting for transfers between devices: 2.94 us -> 4.15 us  [on_device(): lax.all_to_all(bias, 'ba', 0, 0, tiled=True, axis_index_groups=halves)]
    ppermute x4, starting transfers between devices: 7.01 us -> 5.8 us  [on_device(): spread.append(lax.ppermute(kv, ('aa', 'ba'), moves))]
where the time goes in v5:
time: 70.6 us; the launch traced here: 70.2 us
  starting transfers between devices  23.5 us (33%)
  Pallas kernels  20.4 us (29%)
  blocking collectives  17 us (24%)
  waiting for transfers between devices  5.61 us (8%)
  local copies, waits for them, and re-layouts  1.83 us (3%)
  between operations  1.53 us (2%)
    all_to_all x1, blocking collectives, gathered(): lax.all_to_all(copies, 'ba', 0, 0, tiled=True, axis_index_groups=sets)  17 us
    all_to_all x1, starting transfers between devices, gathered(): lax.all_to_all(copies, 'ba', 0, 0, tiled=True, axis_index_groups=sets)  8.39 us
    pallas_call x1, Pallas kernels, on_device(): pl.pallas_call(bias_kernel, out_shape=shape((peers, 2 * (tok_rows + 16),...  6.95 us
    all_to_all x1, starting transfers between devices, on_device(): lax.all_to_all(bias, 'ba', 0, 0, tiled=True, axis_index_groups=halves)  6.07 us
    ppermute x4, starting transfers between devices, on_device(): spread.append(lax.ppermute(kv, ('aa', 'ba'), moves))  5.8 us
    pallas_call x1, Pallas kernels, on_device(): pl.pallas_call(close_kernel, out_shape=(shape((3, atoms), F32), shape((to...  4.64 us
    all_to_all x1, waiting for transfers between devices, on_device(): lax.all_to_all(bias, 'ba', 0, 0, tiled=True, axis_index_groups=halves)  4.15 us
    pallas_call x1, Pallas kernels, on_device(): pl.pallas_call(token_kernel, out_shape=(shape((tok_rows, D), F32), shape(...  3.8 us
  transfers between devices with their start and end apart: 8, of which 2 were waited for; matrix products, arithmetic and copies ran while one was open for 3% of the time, Pallas kernels for 15%

profile of v5, /device:TPU:1, one launch (start us, length us, event | category | flops | bytes accessed | tf_op | source)
XLA Modules:
  0.0 70.2 jit_solution(10175430749676073953)
XLA Ops:
  1.3 2.0 %state.1 = (f32[192,128]{1,0:T(8,128)}, bf16[8,208,128]{2,1,0:T(8,128)(2,1)}) custom-call(f32[192,128]{1,0:T(8,128)} %cond_ref.2, f32[3,192]{1,0:T(4,128)} %pos_ref.3, f32[1,1]{1,0:T(1,128)} %bitcast.3.noise_ref, s32[1,192]{1,0:T(1,128)} %bitcast.8, f32[3,128]{1,0:T(4,128)} %w_pos_ref.2), custom_call_target="tpu_custom_call" | custom-call | tf_op jit(solution)/shard_map/state/pallas_call | solution.py:294
  3.3 8.4 %all-to-all-start = ((bf16[8,208,128]{2,1,0:T(8,128)(2,1)}), bf16[8,208,128]{2,1,0:T(8,128)(2,1)S(1)}, u32[]{:S(2)}, u32[]{:S(2)}) async-start(bf16[8,208,128]{2,1,0:T(8,128)(2,1)} %get-tuple-element.8), calls=%async_computation | async-start | bytes 851968 | tf_op jit(solution)/shard_map/all_to_all | solution.py:289
  11.7 7.0 %bias.1 = bf16[8,544,128]{2,1,0:T(8,128)(2,1)} custom-call(bf16[256,128,128]{2,1,0:T(8,128)(2,1)} %pair_ref.1, bf16[16,128]{1,0:T(8,128)(2,1)} %w_ref.1), custom_call_target="tpu_custom_call" | custom-call | flops 2147483648 | bytes 10485760 | tf_op jit(solution)/shard_map/bias/pallas_call | solution.py:303
  18.7 0.0 all-to-all-done.mine_ref
  18.7 6.1 %all-to-all-start.1 = ((bf16[8,544,128]{2,1,0:T(8,128)(2,1)}), bf16[8,544,128]{2,1,0:T(8,128)(2,1)S(1)}, u32[]{:S(2)}, u32[]{:S(2)}) async-start(bf16[8,544,128]{2,1,0:T(8,128)(2,1)} %bias.1), calls=%async_computation.1 | async-start | bytes 2228224 | tf_op jit(solution)/shard_map/all_to_all | solution.py:321
  24.8 0.0 collective-permute-start
  24.8 0.0 copy-start.3
  24.8 0.0 copy-start.6
  24.8 1.8 %constant_dynamic-slice_fusion.1 = (bf16[768,96]{1,0:T(8,128)(2,1)S(1)}, bf16[768,96]{1,0:T(8,128)(2,1)S(1)}, bf16[768,96]{1,0:T(8,128)(2,1)S(1)}, bf16[768,96]{1,0:T(8,128)(2,1)S(1)}) fusion(bf16[768,1536]{1,0:T(8,128)(2,1)} %param.28, s32[]{:T(128)S(6)} %select_n.8, s32[]{:T(128)S(6)} %select_n.9, bf16[768,1536]{1,0:T(8,128)(2,1)} %param.27), kind=kLoop, calls=%fused_computation.16 | loop fusion | bytes 1179656 | tf_op jit(solution)/shard_map/dynamic_slice | solution.py:326
  26.6 0.2 fusion.7.w_head_ref
  26.8 0.0 collective-permute-done.other_ref
  26.8 0.0 copy-done.2
  26.8 0.0 copy-done.3
  26.8 0.0 copy-done.6
  26.8 3.8 %token_.1 = (f32[256,768]{1,0:T(8,128)S(1)}, bf16[256,96]{1,0:T(8,128)(2,1)S(1)}, bf16[256,96]{1,0:T(8,128)(2,1)S(1)}, bf16[192,256]{1,0:T(8,128)(2,1)S(1)}) custom-call(bf16[8,208,128]{2,1,0:T(8,128)(2,1)S(1)} %all-to-all-done.mine_ref, bf16[8,208,128]{2,1,0:T(8,128)(2,1)S(1)} %collective-permute-done.other_ref, bf16[128,768]{1,0:T(8,128)(2,1)S(1)} %copy-done.3, ...), custom_call_target="tpu_custom_call" | custom-call | tf_op jit(solution)/shard_map/token/pallas_call | solution.py:340
  30.6 3.7 %collective-permute-start.1 = (bf16[192,256]{1,0:T(8,128)(2,1)S(1)}, bf16[192,256]{1,0:T(8,128)(2,1)S(1)}, u32[]{:S(2)}, u32[]{:S(2)}) collective-permute-start(bf16[192,256]{1,0:T(8,128)(2,1)S(1)} %get-tuple-element.11), channel_id=1, source_target_pairs={{0,32},{1,33},{2,34},{3,35},{4,36},{5,37},{6,38},{7,39},{16,48},{1... | collective-permute-start | bytes 294920 | tf_op jit(solution)/shard_map/ppermute | solution.py:365
  34.3 0.4 collective-permute-start.2
  34.7 1.0 %collective-permute-start.3 = (bf16[192,256]{1,0:T(8,128)(2,1)S(1)}, bf16[192,256]{1,0:T(8,128)(2,1)S(1)}, u32[]{:S(2)}, u32[]{:S(2)}) collective-permute-start(bf16[192,256]{1,0:T(8,128)(2,1)S(1)} %get-tuple-element.11), channel_id=1, source_target_pairs={{0,16},{1,17},{2,18},{3,19},{4,20},{5,21},{6,22},{7,23},{16,32},{1... | collective-permute-start | bytes 294920 | tf_op jit(solution)/shard_map/ppermute | solution.py:365
  35.7 0.7 collective-permute-start.4
  36.4 4.2 %all-to-all-done.1 = bf16[8,544,128]{2,1,0:T(8,128)(2,1)S(1)} async-done(((bf16[8,544,128]{2,1,0:T(8,128)(2,1)}), bf16[8,544,128]{2,1,0:T(8,128)(2,1)S(1)}, u32[]{:S(2)}, u32[]{:S(2)}) %all-to-all-start.1) | async-done | bytes 1114144 | tf_op jit(solution)/shard_map/all_to_all | solution.py:321
  40.6 0.1 convert_element_type.8.bias_ref
  40.7 0.0 collective-permute-done.1.refs_0_
  40.7 0.0 collective-permute-done.2.refs_1_
  40.7 0.0 collective-permute-done.3.refs_2_
  40.7 0.0 collective-permute-done.4.refs_3_
  40.8 0.0 slice-start
  40.8 0.0 slice-start.1
  40.8 0.0 copy-start
  40.8 0.0 copy-start.1
  40.8 0.0 copy-start.4
  40.8 0.0 copy-start.5
  40.8 0.0 copy-start.7
  40.8 0.0 copy-start.8
  40.8 0.0 copy-start.9
  40.9 3.0 %attend.1 = bf16[8,112,256]{2,1,0:T(8,128)(2,1)S(1)} custom-call(bf16[256,96]{1,0:T(8,128)(2,1)S(1)} %get-tuple-element.9.query_ref, bf16[256,96]{1,0:T(8,128)(2,1)S(1)} %get-tuple-element.10.gate_ref, f32[8,544,128]{2,1,0:T(8,128)S(1)} %convert_element_type.8.bias_ref, bf16[192,256]{1,0:T(8,128)(2,1)S(1)} %collective-permute-done.1.refs_0_, ...), custom_call_target="tpu_custom_call" | custom-call | flops 20000000000 | bytes 8388608 | tf_op jit(solution)/shard_map/attend/pallas_call | solution.py:367
  43.8 17.0 %all_to_all.15.mine_ref = bf16[8,112,256]{2,1,0:T(8,128)(2,1)S(1)} all-to-all(bf16[8,112,256]{2,1,0:T(8,128)(2,1)S(1)} %attend.1), channel_id=1, replica_groups={{0,8,2,10,4,12,6,14},{9,1,11,3,13,5,15,7},{16,24,18,26,20,28,22,30},{25..., dimensions={0} | all-to-all | bytes 917504 | tf_op jit(solution)/shard_map/all_to_all | solution.py:289
  60.8 3.3 %collective-permute-start.5 = (bf16[8,112,256]{2,1,0:T(8,128)(2,1)S(1)}, bf16[8,112,256]{2,1,0:T(8,128)(2,1)S(1)}, u32[]{:S(2)}, u32[]{:S(2)}) collective-permute-start(bf16[8,112,256]{2,1,0:T(8,128)(2,1)S(1)} %all_to_all.15.mine_ref), channel_id=1, source_target_pairs={{0,1},{1,0},{2,3},{3,2},{4,5},{5,4},{6,7},{7,6},{8,9},{9,8},{10,11... | collective-permute-start | bytes 1376264 | tf_op jit(solution)/shard_map/ppermute | solution.py:290
  64.1 1.4 %collective-permute-done.5.other_ref = bf16[8,112,256]{2,1,0:T(8,128)(2,1)S(1)} collective-permute-done((bf16[8,112,256]{2,1,0:T(8,128)(2,1)S(1)}, bf16[8,112,256]{2,1,0:T(8,128)(2,1)S(1)}, u32[]{:S(2)}, u32[]{:S(2)}) %collective-permute-start.5) | collective-permute-done | bytes 458784 | tf_op jit(solution)/shard_map/ppermute | solution.py:290
  65.5 0.0 slice-done
  65.5 0.0 slice-done.1
  65.5 0.0 copy-done
  65.5 0.0 copy-done.1
  65.5 0.0 copy-done.4
  65.6 0.0 copy-done.5
  65.6 0.0 copy-done.7
  65.6 0.0 copy-done.8
  65.6 0.0 copy-done.9
  65.6 4.6 %close.1 = (f32[3,192]{1,0:T(4,128)}, f32[256,768]{1,0:T(8,128)}) custom-call(bf16[8,112,256]{2,1,0:T(8,128)(2,1)S(1)} %all_to_all.15.mine_ref, bf16[8,112,256]{2,1,0:T(8,128)(2,1)S(1)} %collective-permute-done.5.other_ref, bf16[4,2,96,768]{3,2,1,0:T(8,128)(2,1)S(1)} %bitcast.7, f32[256,768]{1,0:T(8,128)S(1)} %get-tuple-element.12.start_ref, ...), custom_call_target="tpu_custom_call" | custom-call | tf_op jit(solution)/shard_map/close/pallas_call | solution.py:380
  (2 shorter events, 0.0 us)
Async XLA Ops:
  3.3 15.4 %all-to-all-start = ((bf16[8,208,128]{2,1,0:T(8,128)(2,1)}), bf16[8,208,128]{2,1,0:T(8,128)(2,1)S(1)}, u32[]{:S(2)}, u32[]{:S(2)}) async-start(bf16[8,208,128]{2,1,0:T(8,128)(2,1)} %get-tuple-element.8), calls=%async_computation | async-start | bytes 851968 | tf_op jit(solution)/shard_map/all_to_all | solution.py:289
  18.7 21.9 %all-to-all-start.1 = ((bf16[8,544,128]{2,1,0:T(8,128)(2,1)}), bf16[8,544,128]{2,1,0:T(8,128)(2,1)S(1)}, u32[]{:S(2)}, u32[]{:S(2)}) async-start(bf16[8,544,128]{2,1,0:T(8,128)(2,1)} %bias.1), calls=%async_computation.1 | async-start | bytes 2228224 | tf_op jit(solution)/shard_map/all_to_all | solution.py:321
  24.8 2.0 %collective-permute-start = (bf16[8,208,128]{2,1,0:T(8,128)(2,1)S(1)}, bf16[8,208,128]{2,1,0:T(8,128)(2,1)S(1)}, u32[]{:S(2)}, u32[]{:S(2)}) collective-permute-start(bf16[8,208,128]{2,1,0:T(8,128)(2,1)S(1)} %all-to-all-done.mine_ref), channel_id=1, source_target_pairs={{0,1},{1,0},{2,3},{3,2},{4,5},{5,4},{6,7},{7,6},{8,9},{9,8},{10,11... | collective-permute-start | bytes 1277960 | tf_op jit(solution)/shard_map/ppermute | solution.py:290
  24.8 2.0 %copy-start.2 = (f32[256,768]{1,0:T(8,128)S(1)}, f32[256,768]{1,0:T(8,128)}, u32[]{:S(2)}) copy-start(f32[256,768]{1,0:T(8,128)} %cond_ref.3) | copy-start | bytes 2359300
  24.8 2.0 %copy-start.3 = (bf16[128,768]{1,0:T(8,128)(2,1)S(1)}, bf16[128,768]{1,0:T(8,128)(2,1)}, u32[]{:S(2)}) copy-start(bf16[128,768]{1,0:T(8,128)(2,1)} %w_atom_ref.1) | copy-start | bytes 589828
  24.8 2.0 %copy-start.6 = (f32[3,768]{1,0:T(4,128)S(1)}, f32[3,768]{1,0:T(4,128)}, u32[]{:S(2)}) copy-start(f32[3,768]{1,0:T(4,128)} %gains_ref.3) | copy-start | bytes 27652
  30.6 10.1 %collective-permute-start.1 = (bf16[192,256]{1,0:T(8,128)(2,1)S(1)}, bf16[192,256]{1,0:T(8,128)(2,1)S(1)}, u32[]{:S(2)}, u32[]{:S(2)}) collective-permute-start(bf16[192,256]{1,0:T(8,128)(2,1)S(1)} %get-tuple-element.11), channel_id=1, source_target_pairs={{0,32},{1,33},{2,34},{3,35},{4,36},{5,37},{6,38},{7,39},{16,48},{1... | collective-permute-start | bytes 294920 | tf_op jit(solution)/shard_map/ppermute | solution.py:365
  34.3 6.4 %collective-permute-start.2 = (bf16[192,256]{1,0:T(8,128)(2,1)S(1)}, bf16[192,256]{1,0:T(8,128)(2,1)S(1)}, u32[]{:S(2)}, u32[]{:S(2)}) collective-permute-start(bf16[192,256]{1,0:T(8,128)(2,1)S(1)} %get-tuple-element.11), channel_id=1, source_target_pairs={{0,48},{1,49},{2,50},{3,51},{4,52},{5,53},{6,54},{7,55},{16,0},{17... | collective-permute-start | bytes 294920 | tf_op jit(solution)/shard_map/ppermute | solution.py:365
  34.7 6.0 %collective-permute-start.3 = (bf16[192,256]{1,0:T(8,128)(2,1)S(1)}, bf16[192,256]{1,0:T(8,128)(2,1)S(1)}, u32[]{:S(2)}, u32[]{:S(2)}) collective-permute-start(bf16[192,256]{1,0:T(8,128)(2,1)S(1)} %get-tuple-element.11), channel_id=1, source_target_pairs={{0,16},{1,17},{2,18},{3,19},{4,20},{5,21},{6,22},{7,23},{16,32},{1... | collective-permute-start | bytes 294920 | tf_op jit(solution)/shard_map/ppermute | solution.py:365
  35.7 5.0 %collective-permute-start.4 = (bf16[192,256]{1,0:T(8,128)(2,1)S(1)}, bf16[192,256]{1,0:T(8,128)(2,1)S(1)}, u32[]{:S(2)}, u32[]{:S(2)}) collective-permute-start(bf16[192,256]{1,0:T(8,128)(2,1)S(1)} %get-tuple-element.11), channel_id=1, source_target_pairs={{0,0},{1,1},{2,2},{3,3},{4,4},{5,5},{6,6},{7,7},{16,16},{17,17},{1... | collective-permute-start | bytes 294920 | tf_op jit(solution)/shard_map/ppermute | solution.py:365
  40.8 24.8 %slice-start = ((s8[4718592]{0:T(1024)(128)(4,1)}), s8[4194304]{0:T(1024)(128)(4,1)S(1)}, s32[]{:S(2)}) async-start(s8[4718592]{0:T(1024)(128)(4,1)} %bitcast.5), calls=%async_computation.3 | async-start | bytes 8388608
  40.8 24.8 %slice-start.1 = ((s8[4718592]{0:T(1024)(128)(4,1)}), s8[524288]{0:T(1024)(128)(4,1)S(1)}, s32[]{:S(2)}) async-start(s8[4718592]{0:T(1024)(128)(4,1)} %bitcast.5), calls=%async_computation.4 | async-start | bytes 1048576
  40.8 24.8 %copy-start = (bf16[1536,768]{1,0:T(8,128)(2,1)S(1)}, bf16[1536,768]{1,0:T(8,128)(2,1)}, u32[]{:S(2)}) copy-start(bf16[1536,768]{1,0:T(8,128)(2,1)} %w_down_ref.1) | copy-start | bytes 7077892
  40.8 24.8 %copy-start.1 = (bf16[768,768]{1,0:T(8,128)(2,1)S(1)}, bf16[768,768]{1,0:T(8,128)(2,1)}, u32[]{:S(2)}) copy-start(bf16[768,768]{1,0:T(8,128)(2,1)} %param.29) | copy-start | bytes 3538948
  40.8 24.7 %copy-start.4 = (bf16[768,128]{1,0:T(8,128)(2,1)S(1)}, bf16[768,128]{1,0:T(8,128)(2,1)}, u32[]{:S(2)}) copy-start(bf16[768,128]{1,0:T(8,128)(2,1)} %w_tok_ref.1) | copy-start | bytes 589828
  40.8 24.7 %copy-start.5 = (f32[192,128]{1,0:T(8,128)S(1)}, f32[192,128]{1,0:T(8,128)}, u32[]{:S(2)}) copy-start(f32[192,128]{1,0:T(8,128)} %get-tuple-element.13.state_ref) | copy-start | bytes 294916
  40.8 24.7 %copy-start.7 = (f32[3,192]{1,0:T(4,128)S(1)}, f32[3,192]{1,0:T(4,128)}, u32[]{:S(2)}) copy-start(f32[3,192]{1,0:T(4,128)} %pos_ref.3) | copy-start | bytes 6916
  40.8 24.7 %copy-start.8 = (s32[192]{0:T(256)S(1)}, s32[192]{0:T(256)}, u32[]{:S(2)}) copy-start(s32[192]{0:T(256)} %param.20) | copy-start | bytes 2308
  40.8 24.7 %copy-start.9 = (bf16[3,128]{1,0:T(4,128)(2,1)S(1)}, bf16[3,128]{1,0:T(4,128)(2,1)}, u32[]{:S(2)}) copy-start(bf16[3,128]{1,0:T(4,128)(2,1)} %w_pos_ref.3) | copy-start | bytes 2308
  60.8 4.7 %collective-permute-start.5 = (bf16[8,112,256]{2,1,0:T(8,128)(2,1)S(1)}, bf16[8,112,256]{2,1,0:T(8,128)(2,1)S(1)}, u32[]{:S(2)}, u32[]{:S(2)}) collective-permute-start(bf16[8,112,256]{2,1,0:T(8,128)(2,1)S(1)} %all_to_all.15.mine_ref), channel_id=1, source_target_pairs={{0,1},{1,0},{2,3},{3,2},{4,5},{5,4},{6,7},{7,6},{8,9},{9,8},{10,11... | collective-permute-start | bytes 1376264 | tf_op jit(solution)/shard_map/ppermute | solution.py:290
